TPU v7x, 256 devices: a whole 4x4x8 slice. The times are simulated.
256 devices in a mesh: row: 8 (over y, x_hi), col: 32 (over z, x_lo, core).
Axes of the slice: x: 4 (x_hi: 2, x_lo: 2; x = x_hi * 2 + x_lo), y: 4, z: 8, core: 2. Of those that a mesh axis runs over, the one named last changes fastest.
Arguments:
- covariance: float32 [12288, 12288], P('row', 'col'), may hold values from -6 to 6
- process_noise: float32 [12288, 12288], P('row', 'col'), may hold values from -3 to 3
- depth_field: float32 [64, 64], replicated, may hold values from 0.4 to 2
- coriolis: float32 [64, 64], replicated, may hold values from -0.6 to 0.6
- drag_rate: float32 [64, 64], replicated, may hold values from 0.05 to 0.5
Outputs:
- forecast: float32 [12288, 12288], P('row', 'col')
All inputs are finite; a program needn't handle non-finite values.
Results may differ from a plain program's by a relative error of at most 0.00002.
Values sent between devices are 32-bit elements; how exact they have to be, the bound alone decides.
No kernel may reach another device: no remote copies, remote signals or barrier semaphores. Data moves between devices by JAX's collectives and lax.ppermute only.
A program may use at most 128 MiB of HBM per device.

v0:
```python
import jax
import jax.numpy as jnp
from jax import lax
from jax.sharding import PartitionSpec as P

GX = 64


STEP_SIZE = 0.9


def extended(x, sides, width):
    for axis, dim in sides:
        size, length = (lax.axis_size(axis), x.shape[dim])
        up = [(i, (i + 1) % size) for i in range(size - 1)]
        down = [(j, i) for i, j in up]
        last = lax.slice_in_dim(x, length - width, length, axis=dim)
        leading = lax.slice_in_dim(x, 0, width, axis=dim)
        before = lax.ppermute(last, axis, up)
        after = lax.ppermute(leading, axis, down)
        x = jnp.concatenate([before, x, after], axis=dim)
    return x


def x_diff(field):
    padded = jnp.pad(field, ((0, 0), (1, 1), (0, 0)))
    return padded[:, 2:] - padded[:, :-2]


def tendency(padded, depth_rows, coriolis_rows, drag_rows):
    inner = padded[1:-1]
    height = inner[:, 0]
    east_flow = inner[:, 1]
    north_flow = inner[:, 2]
    depth_b = depth_rows[:, :, None]
    turn_b = coriolis_rows[:, :, None]
    drag_b = drag_rows[:, :, None]
    d_height = -0.5 * depth_b * (x_diff(east_flow) + (padded[2:, 2] - padded[:-2, 2]))
    d_east = -0.5 * x_diff(height) + turn_b * north_flow - drag_b * east_flow
    d_north = -0.5 * (padded[2:, 0] - padded[:-2, 0]) - turn_b * east_flow - drag_b * north_flow
    return jnp.stack([d_height, d_east, d_north], axis=1)


def advance(field, extend, coefficients):
    depth_rows, coriolis_rows, drag_rows = coefficients
    slope_one = tendency(extend(field), depth_rows, coriolis_rows, drag_rows)
    slope_two = tendency(
        extend(field + 0.5 * STEP_SIZE * slope_one), depth_rows, coriolis_rows, drag_rows
    )
    slope_three = tendency(
        extend(field + 0.5 * STEP_SIZE * slope_two), depth_rows, coriolis_rows, drag_rows
    )
    slope_four = tendency(
        extend(field + STEP_SIZE * slope_three), depth_rows, coriolis_rows, drag_rows
    )
    return field + STEP_SIZE / 6.0 * (slope_one + 2.0 * slope_two + 2.0 * slope_three + slope_four)


def local_rows(depth_field, coriolis, drag_rate, first_row, row_count):
    return (
        lax.dynamic_slice_in_dim(depth_field, first_row, row_count, 0),
        lax.dynamic_slice_in_dim(coriolis, first_row, row_count, 0),
        lax.dynamic_slice_in_dim(drag_rate, first_row, row_count, 0),
    )


def row_extend(field):
    return extended(field, (("row", 0),), 1)


def col_extend(field):
    return extended(field, (("col", 0),), 1)


def shards(covariance, process_noise, depth_field, coriolis, drag_rate):
    state_rows = covariance.shape[0]
    columns = covariance.shape[1]
    grid_rows = state_rows // (3 * GX)
    first_row = lax.axis_index("row") * grid_rows
    row_coeffs = local_rows(depth_field, coriolis, drag_rate, first_row, grid_rows)
    forward = advance(covariance.reshape(grid_rows, 3, GX, columns), row_extend, row_coeffs)
    forward = forward.reshape(state_rows, columns)
    col_grid_rows = columns // (3 * GX)
    col_first = lax.axis_index("col") * col_grid_rows
    col_coeffs = local_rows(depth_field, coriolis, drag_rate, col_first, col_grid_rows)
    twice = advance(forward.T.reshape(col_grid_rows, 3, GX, state_rows), col_extend, col_coeffs)
    result = twice.reshape(columns, state_rows).T
    return result + process_noise


def solution(mesh):
    return jax.shard_map(
        shards,
        mesh=mesh,
        in_specs=(P("row", "col"), P("row", "col"), P(), P(), P()),
        out_specs=P("row", "col"),
        check_vma=False,
    )
```

profile of v0, /device:TPU:193, one launch (start us, length us, event | category | flops | bytes accessed | tf_op | source)
XLA Modules:
  0.0 237.7 jit_solution(6302694212734155594)
XLA Ops:
  1.1 4.7 %collective-permute-start.1 = (f32[1,3,64,384]{3,2,0,1:T(8,128)S(1)}, f32[1,3,64,384]{3,2,0,1:T(8,128)S(1)}, u32[]{:S(2)}, u32[]{:S(2)}) collective-permute-start(f32[1,3,64,384]{3,2,0,1:T(8,128)S(1)} %bitcast.269), channel_id=1, source_target_pairs={{0,32},{32,64},{64,96},{96,128},{128,160},{160,192},{192,224},{1,3... | collective-permute-start | bytes 884744 | tf_op jit(solution)/shard_map/ppermute | solution.py:19
  9.1 2.3 collective-permute-done.1
  11.4 2.5 %fusion.123 = (f32[8,3,64,384]{3,2,0,1:T(8,128)S(1)}, f32[9,3,64,384]{3,2,0,1:T(8,128)S(1)}, f32[9,3,64,384]{3,2,0,1:T(8,128)S(1)}) fusion(f32[8,3,64,384]{3,2,1,0:T(8,128)} %bitcast.237, f32[9,3,64,384]{3,2,0,1:T(8,128)S(1)} %constant_dynamic-update-slice_fusion.3), kind=kLoop, calls=%fused_computation.255 | loop fusion | bytes 9437184 | tf_op jit(solution)/shard_map/reshape | solution.py:81
  14.0 5.7 %collective-permute-done = f32[1,3,64,384]{3,2,0,1:T(8,128)S(1)} collective-permute-done((f32[1,3,64,384]{3,2,0,1:T(8,128)S(1)}, f32[1,3,64,384]{3,2,0,1:T(8,128)S(1)}, u32[]{:S(2)}, u32[]{:S(2)}) %collective-permute-start) | collective-permute-done | bytes 294944 | tf_op jit(solution)/shard_map/ppermute | solution.py:20
  22.2 4.7 %collective-permute-start.3 = (f32[1,3,64,384]{3,2,0,1:T(8,128)S(1)}, f32[1,3,64,384]{3,2,0,1:T(8,128)S(1)}, u32[]{:S(2)}, u32[]{:S(2)}) collective-permute-start(f32[1,3,64,384]{3,2,0,1:T(8,128)S(1)} %get-tuple-element.46), channel_id=1, source_target_pairs={{0,32},{32,64},{64,96},{96,128},{128,160},{160,192},{192,224},{1,3... | collective-permute-start | bytes 884744 | tf_op jit(solution)/shard_map/ppermute | solution.py:19
  28.7 2.9 %collective-permute-done.3 = f32[1,3,64,384]{3,2,0,1:T(8,128)S(1)} collective-permute-done((f32[1,3,64,384]{3,2,0,1:T(8,128)S(1)}, f32[1,3,64,384]{3,2,0,1:T(8,128)S(1)}, u32[]{:S(2)}, u32[]{:S(2)}) %collective-permute-start.3) | collective-permute-done | bytes 294944 | tf_op jit(solution)/shard_map/ppermute | solution.py:19
  32.4 7.6 %collective-permute-done.2 = f32[1,3,64,384]{3,2,0,1:T(8,128)S(1)} collective-permute-done((f32[1,3,64,384]{3,2,0,1:T(8,128)S(1)}, f32[1,3,64,384]{3,2,0,1:T(8,128)S(1)}, u32[]{:S(2)}, u32[]{:S(2)}) %collective-permute-start.2) | collective-permute-done | bytes 294944 | tf_op jit(solution)/shard_map/ppermute | solution.py:20
  41.0 4.7 %collective-permute-start.5 = (f32[1,3,64,384]{3,2,0,1:T(8,128)S(1)}, f32[1,3,64,384]{3,2,0,1:T(8,128)S(1)}, u32[]{:S(2)}, u32[]{:S(2)}) collective-permute-start(f32[1,3,64,384]{3,2,0,1:T(8,128)S(1)} %get-tuple-element.40), channel_id=1, source_target_pairs={{0,32},{32,64},{64,96},{96,128},{128,160},{160,192},{192,224},{1,3... | collective-permute-start | bytes 884744 | tf_op jit(solution)/shard_map/ppermute | solution.py:19
  50.0 8.3 %collective-permute-done.4 = f32[1,3,64,384]{3,2,0,1:T(8,128)S(1)} collective-permute-done((f32[1,3,64,384]{3,2,0,1:T(8,128)S(1)}, f32[1,3,64,384]{3,2,0,1:T(8,128)S(1)}, u32[]{:S(2)}, u32[]{:S(2)}) %collective-permute-start.4) | collective-permute-done | bytes 294944 | tf_op jit(solution)/shard_map/ppermute | solution.py:20
  59.4 3.8 %collective-permute-start.7 = (f32[1,3,64,384]{3,2,0,1:T(8,128)S(1)}, f32[1,3,64,384]{3,2,0,1:T(8,128)S(1)}, u32[]{:S(2)}, u32[]{:S(2)}) collective-permute-start(f32[1,3,64,384]{3,2,0,1:T(8,128)S(1)} %get-tuple-element.34), channel_id=1, source_target_pairs={{0,32},{32,64},{64,96},{96,128},{128,160},{160,192},{192,224},{1,3... | collective-permute-start | bytes 884744 | tf_op jit(solution)/shard_map/ppermute | solution.py:19
  67.6 8.3 %collective-permute-done.6 = f32[1,3,64,384]{3,2,0,1:T(8,128)S(1)} collective-permute-done((f32[1,3,64,384]{3,2,0,1:T(8,128)S(1)}, f32[1,3,64,384]{3,2,0,1:T(8,128)S(1)}, u32[]{:S(2)}, u32[]{:S(2)}) %collective-permute-start.6) | collective-permute-done | bytes 294944 | tf_op jit(solution)/shard_map/ppermute | solution.py:20
  80.4 5.5 %collective-permute-start.9 = (f32[1,3,64,1536]{3,2,0,1:T(8,128)}, f32[1,3,64,1536]{3,2,0,1:T(8,128)S(1)}, u32[]{:S(2)}, u32[]{:S(2)}) collective-permute-start(f32[1,3,64,1536]{3,2,0,1:T(8,128)} %bitcast.266), channel_id=1, source_target_pairs={{0,1},{1,2},{2,3},{3,4},{4,5},{5,6},{6,7},{7,8},{8,9},{9,10},{10,1... | collective-permute-start | bytes 3538952 | tf_op jit(solution)/shard_map/ppermute | solution.py:19
  92.9 19.1 %collective-permute-done.9 = f32[1,3,64,1536]{3,2,0,1:T(8,128)S(1)} collective-permute-done((f32[1,3,64,1536]{3,2,0,1:T(8,128)}, f32[1,3,64,1536]{3,2,0,1:T(8,128)S(1)}, u32[]{:S(2)}, u32[]{:S(2)}) %collective-permute-start.9) | collective-permute-done | bytes 1179680 | tf_op jit(solution)/shard_map/ppermute | solution.py:19
  112.9 14.2 %collective-permute-done.8 = f32[1,3,64,1536]{3,2,0,1:T(8,128)} collective-permute-done((f32[1,3,64,1536]{3,2,0,1:T(8,128)}, f32[1,3,64,1536]{3,2,0,1:T(8,128)}, u32[]{:S(2)}, u32[]{:S(2)}) %collective-permute-start.8) | collective-permute-done | bytes 1179680 | tf_op jit(solution)/shard_map/ppermute | solution.py:20
  132.1 2.4 %collective-permute-start.10 = (f32[1,3,64,1536]{3,2,0,1:T(8,128)S(1)}, f32[1,3,64,1536]{3,2,0,1:T(8,128)S(1)}, u32[]{:S(2)}, u32[]{:S(2)}) collective-permute-start(f32[1,3,64,1536]{3,2,0,1:T(8,128)S(1)} %get-tuple-element.19), channel_id=1, source_target_pairs={{1,0},{2,1},{3,2},{4,3},{5,4},{6,5},{7,6},{8,7},{9,8},{10,9},{11,1... | collective-permute-start | bytes 3538952 | tf_op jit(solution)/shard_map/ppermute | solution.py:20
  135.3 22.2 %collective-permute-done.11 = f32[1,3,64,1536]{3,2,0,1:T(8,128)S(1)} collective-permute-done((f32[1,3,64,1536]{3,2,0,1:T(8,128)S(1)}, f32[1,3,64,1536]{3,2,0,1:T(8,128)S(1)}, u32[]{:S(2)}, u32[]{:S(2)}) %collective-permute-start.11) | collective-permute-done | bytes 1179680 | tf_op jit(solution)/shard_map/ppermute | solution.py:19
  159.5 17.0 %collective-permute-start.13 = (f32[1,3,64,1536]{3,2,0,1:T(8,128)S(1)}, f32[1,3,64,1536]{3,2,0,1:T(8,128)S(1)}, u32[]{:S(2)}, u32[]{:S(2)}) collective-permute-start(f32[1,3,64,1536]{3,2,0,1:T(8,128)S(1)} %get-tuple-element.14), channel_id=1, source_target_pairs={{0,1},{1,2},{2,3},{3,4},{4,5},{5,6},{6,7},{7,8},{8,9},{9,10},{10,1... | collective-permute-start | bytes 3538952 | tf_op jit(solution)/shard_map/ppermute | solution.py:19
  179.6 22.7 %collective-permute-done.13 = f32[1,3,64,1536]{3,2,0,1:T(8,128)S(1)} collective-permute-done((f32[1,3,64,1536]{3,2,0,1:T(8,128)S(1)}, f32[1,3,64,1536]{3,2,0,1:T(8,128)S(1)}, u32[]{:S(2)}, u32[]{:S(2)}) %collective-permute-start.13) | collective-permute-done | bytes 1179680 | tf_op jit(solution)/shard_map/ppermute | solution.py:19
  203.1 3.8 %collective-permute-done.12 = f32[1,3,64,1536]{3,2,0,1:T(8,128)S(1)} collective-permute-done((f32[1,3,64,1536]{3,2,0,1:T(8,128)S(1)}, f32[1,3,64,1536]{3,2,0,1:T(8,128)S(1)}, u32[]{:S(2)}, u32[]{:S(2)}) %collective-permute-start.12) | collective-permute-done | bytes 1179680 | tf_op jit(solution)/shard_map/ppermute | solution.py:20
  210.2 2.6 %collective-permute-start.14 = (f32[1,3,64,1536]{3,2,0,1:T(8,128)S(1)}, f32[1,3,64,1536]{3,2,0,1:T(8,128)S(1)}, u32[]{:S(2)}, u32[]{:S(2)}) collective-permute-start(f32[1,3,64,1536]{3,2,0,1:T(8,128)S(1)} %get-tuple-element.7), channel_id=1, source_target_pairs={{1,0},{2,1},{3,2},{4,3},{5,4},{6,5},{7,6},{8,7},{9,8},{10,9},{11,1... | collective-permute-start | bytes 3538952 | tf_op jit(solution)/shard_map/ppermute | solution.py:20
  213.7 9.4 %collective-permute-done.15 = f32[1,3,64,1536]{3,2,0,1:T(8,128)S(1)} collective-permute-done((f32[1,3,64,1536]{3,2,0,1:T(8,128)S(1)}, f32[1,3,64,1536]{3,2,0,1:T(8,128)S(1)}, u32[]{:S(2)}, u32[]{:S(2)}) %collective-permute-start.15) | collective-permute-done | bytes 1179680 | tf_op jit(solution)/shard_map/ppermute | solution.py:19
  223.9 3.8 %collective-permute-done.14 = f32[1,3,64,1536]{3,2,0,1:T(8,128)S(1)} collective-permute-done((f32[1,3,64,1536]{3,2,0,1:T(8,128)S(1)}, f32[1,3,64,1536]{3,2,0,1:T(8,128)S(1)}, u32[]{:S(2)}, u32[]{:S(2)}) %collective-permute-start.14) | collective-permute-done | bytes 1179680 | tf_op jit(solution)/shard_map/ppermute | solution.py:20
  230.3 3.2 %copy.224 = f32[384,1536]{0,1:T(8,128)} copy(f32[384,1536]{1,0:T(8,128)} %bitcast.265) | data formatting | bytes 4718592 | tf_op jit(solution)/shard_map/mul | solution.py:56
  233.6 4.1 %bitcast_add_fusion = f32[1536,384]{1,0:T(8,128)} fusion(f32[1536,384]{1,0:T(8,128)} %param.6, f32[384,1536]{0,1:T(8,128)} %copy.224, f32[1536,384]{1,0:T(8,128)S(1)} %copy-done.2), kind=kLoop, calls=%fused_computation.10 | loop fusion | flops 1179648 | bytes 9437184 | tf_op jit(solution)/shard_map/add | solution.py:88
  (94 shorter events, 51.5 us)
Async XLA Ops:
  1.1 10.3 %collective-permute-start.1 = (f32[1,3,64,384]{3,2,0,1:T(8,128)S(1)}, f32[1,3,64,384]{3,2,0,1:T(8,128)S(1)}, u32[]{:S(2)}, u32[]{:S(2)}) collective-permute-start(f32[1,3,64,384]{3,2,0,1:T(8,128)S(1)} %bitcast.269), channel_id=1, source_target_pairs={{0,32},{32,64},{64,96},{96,128},{128,160},{160,192},{192,224},{1,3... | collective-permute-start | bytes 884744 | tf_op jit(solution)/shard_map/ppermute | solution.py:19
  5.8 13.9 %collective-permute-start = (f32[1,3,64,384]{3,2,0,1:T(8,128)S(1)}, f32[1,3,64,384]{3,2,0,1:T(8,128)S(1)}, u32[]{:S(2)}, u32[]{:S(2)}) collective-permute-start(f32[1,3,64,384]{3,2,0,1:T(8,128)S(1)} %bitcast.268), channel_id=1, source_target_pairs={{32,0},{64,32},{96,64},{128,96},{160,128},{192,160},{224,192},{33,... | collective-permute-start | bytes 884744 | tf_op jit(solution)/shard_map/ppermute | solution.py:20
  20.1 1.7 copy-start
  22.2 9.4 %collective-permute-start.3 = (f32[1,3,64,384]{3,2,0,1:T(8,128)S(1)}, f32[1,3,64,384]{3,2,0,1:T(8,128)S(1)}, u32[]{:S(2)}, u32[]{:S(2)}) collective-permute-start(f32[1,3,64,384]{3,2,0,1:T(8,128)S(1)} %get-tuple-element.46), channel_id=1, source_target_pairs={{0,32},{32,64},{64,96},{96,128},{128,160},{160,192},{192,224},{1,3... | collective-permute-start | bytes 884744 | tf_op jit(solution)/shard_map/ppermute | solution.py:19
  27.1 12.8 %collective-permute-start.2 = (f32[1,3,64,384]{3,2,0,1:T(8,128)S(1)}, f32[1,3,64,384]{3,2,0,1:T(8,128)S(1)}, u32[]{:S(2)}, u32[]{:S(2)}) collective-permute-start(f32[1,3,64,384]{3,2,0,1:T(8,128)S(1)} %get-tuple-element.45), channel_id=1, source_target_pairs={{32,0},{64,32},{96,64},{128,96},{160,128},{192,160},{224,192},{33,... | collective-permute-start | bytes 884744 | tf_op jit(solution)/shard_map/ppermute | solution.py:20
  41.0 8.3 %collective-permute-start.5 = (f32[1,3,64,384]{3,2,0,1:T(8,128)S(1)}, f32[1,3,64,384]{3,2,0,1:T(8,128)S(1)}, u32[]{:S(2)}, u32[]{:S(2)}) collective-permute-start(f32[1,3,64,384]{3,2,0,1:T(8,128)S(1)} %get-tuple-element.40), channel_id=1, source_target_pairs={{0,32},{32,64},{64,96},{96,128},{128,160},{160,192},{192,224},{1,3... | collective-permute-start | bytes 884744 | tf_op jit(solution)/shard_map/ppermute | solution.py:19
  45.9 12.5 %collective-permute-start.4 = (f32[1,3,64,384]{3,2,0,1:T(8,128)S(1)}, f32[1,3,64,384]{3,2,0,1:T(8,128)S(1)}, u32[]{:S(2)}, u32[]{:S(2)}) collective-permute-start(f32[1,3,64,384]{3,2,0,1:T(8,128)S(1)} %get-tuple-element.39), channel_id=1, source_target_pairs={{32,0},{64,32},{96,64},{128,96},{160,128},{192,160},{224,192},{33,... | collective-permute-start | bytes 884744 | tf_op jit(solution)/shard_map/ppermute | solution.py:20
  59.4 7.4 %collective-permute-start.7 = (f32[1,3,64,384]{3,2,0,1:T(8,128)S(1)}, f32[1,3,64,384]{3,2,0,1:T(8,128)S(1)}, u32[]{:S(2)}, u32[]{:S(2)}) collective-permute-start(f32[1,3,64,384]{3,2,0,1:T(8,128)S(1)} %get-tuple-element.34), channel_id=1, source_target_pairs={{0,32},{32,64},{64,96},{96,128},{128,160},{160,192},{192,224},{1,3... | collective-permute-start | bytes 884744 | tf_op jit(solution)/shard_map/ppermute | solution.py:19
  63.4 12.5 %collective-permute-start.6 = (f32[1,3,64,384]{3,2,0,1:T(8,128)S(1)}, f32[1,3,64,384]{3,2,0,1:T(8,128)S(1)}, u32[]{:S(2)}, u32[]{:S(2)}) collective-permute-start(f32[1,3,64,384]{3,2,0,1:T(8,128)S(1)} %get-tuple-element.33), channel_id=1, source_target_pairs={{32,0},{64,32},{96,64},{128,96},{160,128},{192,160},{224,192},{33,... | collective-permute-start | bytes 884744 | tf_op jit(solution)/shard_map/ppermute | solution.py:20
  77.5 1.4 copy-start.1
  80.4 31.6 %collective-permute-start.9 = (f32[1,3,64,1536]{3,2,0,1:T(8,128)}, f32[1,3,64,1536]{3,2,0,1:T(8,128)S(1)}, u32[]{:S(2)}, u32[]{:S(2)}) collective-permute-start(f32[1,3,64,1536]{3,2,0,1:T(8,128)} %bitcast.266), channel_id=1, source_target_pairs={{0,1},{1,2},{2,3},{3,4},{4,5},{5,6},{6,7},{7,8},{8,9},{9,10},{10,1... | collective-permute-start | bytes 3538952 | tf_op jit(solution)/shard_map/ppermute | solution.py:19
  87.4 39.7 %collective-permute-start.8 = (f32[1,3,64,1536]{3,2,0,1:T(8,128)}, f32[1,3,64,1536]{3,2,0,1:T(8,128)}, u32[]{:S(2)}, u32[]{:S(2)}) collective-permute-start(f32[1,3,64,1536]{3,2,0,1:T(8,128)} %bitcast.267), channel_id=1, source_target_pairs={{1,0},{2,1},{3,2},{4,3},{5,4},{6,5},{7,6},{8,7},{9,8},{10,9},{11,1... | collective-permute-start | bytes 3538952 | tf_op jit(solution)/shard_map/ppermute | solution.py:20
  129.9 27.7 %collective-permute-start.11 = (f32[1,3,64,1536]{3,2,0,1:T(8,128)S(1)}, f32[1,3,64,1536]{3,2,0,1:T(8,128)S(1)}, u32[]{:S(2)}, u32[]{:S(2)}) collective-permute-start(f32[1,3,64,1536]{3,2,0,1:T(8,128)S(1)} %get-tuple-element.20), channel_id=1, source_target_pairs={{0,1},{1,2},{2,3},{3,4},{4,5},{5,6},{6,7},{7,8},{8,9},{9,10},{10,1... | collective-permute-start | bytes 3538952 | tf_op jit(solution)/shard_map/ppermute | solution.py:19
  132.1 26.3 %collective-permute-start.10 = (f32[1,3,64,1536]{3,2,0,1:T(8,128)S(1)}, f32[1,3,64,1536]{3,2,0,1:T(8,128)S(1)}, u32[]{:S(2)}, u32[]{:S(2)}) collective-permute-start(f32[1,3,64,1536]{3,2,0,1:T(8,128)S(1)} %get-tuple-element.19), channel_id=1, source_target_pairs={{1,0},{2,1},{3,2},{4,3},{5,4},{6,5},{7,6},{8,7},{9,8},{10,9},{11,1... | collective-permute-start | bytes 3538952 | tf_op jit(solution)/shard_map/ppermute | solution.py:20
  159.5 42.8 %collective-permute-start.13 = (f32[1,3,64,1536]{3,2,0,1:T(8,128)S(1)}, f32[1,3,64,1536]{3,2,0,1:T(8,128)S(1)}, u32[]{:S(2)}, u32[]{:S(2)}) collective-permute-start(f32[1,3,64,1536]{3,2,0,1:T(8,128)S(1)} %get-tuple-element.14), channel_id=1, source_target_pairs={{0,1},{1,2},{2,3},{3,4},{4,5},{5,6},{6,7},{7,8},{8,9},{9,10},{10,1... | collective-permute-start | bytes 3538952 | tf_op jit(solution)/shard_map/ppermute | solution.py:19
  176.8 30.2 %collective-permute-start.12 = (f32[1,3,64,1536]{3,2,0,1:T(8,128)S(1)}, f32[1,3,64,1536]{3,2,0,1:T(8,128)S(1)}, u32[]{:S(2)}, u32[]{:S(2)}) collective-permute-start(f32[1,3,64,1536]{3,2,0,1:T(8,128)S(1)} %get-tuple-element.13), channel_id=1, source_target_pairs={{1,0},{2,1},{3,2},{4,3},{5,4},{6,5},{7,6},{8,7},{9,8},{10,9},{11,1... | collective-permute-start | bytes 3538952 | tf_op jit(solution)/shard_map/ppermute | solution.py:20
  208.0 15.1 %collective-permute-start.15 = (f32[1,3,64,1536]{3,2,0,1:T(8,128)S(1)}, f32[1,3,64,1536]{3,2,0,1:T(8,128)S(1)}, u32[]{:S(2)}, u32[]{:S(2)}) collective-permute-start(f32[1,3,64,1536]{3,2,0,1:T(8,128)S(1)} %get-tuple-element.8), channel_id=1, source_target_pairs={{0,1},{1,2},{2,3},{3,4},{4,5},{5,6},{6,7},{7,8},{8,9},{9,10},{10,1... | collective-permute-start | bytes 3538952 | tf_op jit(solution)/shard_map/ppermute | solution.py:19
  210.2 17.5 %collective-permute-start.14 = (f32[1,3,64,1536]{3,2,0,1:T(8,128)S(1)}, f32[1,3,64,1536]{3,2,0,1:T(8,128)S(1)}, u32[]{:S(2)}, u32[]{:S(2)}) collective-permute-start(f32[1,3,64,1536]{3,2,0,1:T(8,128)S(1)} %get-tuple-element.7), channel_id=1, source_target_pairs={{1,0},{2,1},{3,2},{4,3},{5,4},{6,5},{7,6},{8,7},{9,8},{10,9},{11,1... | collective-permute-start | bytes 3538952 | tf_op jit(solution)/shard_map/ppermute | solution.py:20
  230.3 3.2 %copy-start.2 = (f32[1536,384]{1,0:T(8,128)S(1)}, f32[1536,384]{1,0:T(8,128)}, u32[]{:S(2)}) copy-start(f32[1536,384]{1,0:T(8,128)} %copy-done.1) | copy-start | bytes 7077892
where the time goes:
time: 239 us; the launch traced here: 238 us
  waiting for transfers between devices  134 us (56%)
  starting transfers between devices  58.4 us (24%)
  other arithmetic  25.3 us (11%)
  local copies, waits for them, and re-layouts  19.5 us (8%)
    ppermute x8, waiting for transfers between devices, extended(): before = lax.ppermute(last, axis, up)  82.1 us
    ppermute x8, waiting for transfers between devices, extended(): after = lax.ppermute(leading, axis, down)  51.7 us
    ppermute x8, starting transfers between devices, extended(): before = lax.ppermute(last, axis, up)  44.1 us
    ppermute x8, starting transfers between devices, extended(): after = lax.ppermute(leading, axis, down)  14.2 us
  transfers between devices with their start and end apart: 16, of which 15 were waited for; matrix products, arithmetic and copies ran while one was open for 8% of the time, Pallas kernels for 0%

commit v1 on v0

v1 whole, which is shorter than its diff:
```python
import functools

import jax
import jax.numpy as jnp
from jax import lax
from jax.experimental import pallas as pl
from jax.experimental.pallas import tpu as pltpu
from jax.sharding import PartitionSpec as P

GX = 64
STEP = 0.9
SEG = 72
LANES = 128
CHUNKS = 2
D, F, R, B = 0, 1, 2, 3
MIB = 1024 * 1024


def at(row, comp):
    return (row * 3 + comp) * SEG + 8


def buffer_rows(rows):
    return rows * 3 * SEG + 8


def zero_gaps(ref, rows):
    for i in range(rows * 3 + 1):
        ref[pl.ds(i * SEG, 8), :] = jnp.zeros((8, LANES), jnp.float32)


def load_coefficients(dep_ref, cor_ref, drag_ref, first, count, coef_ref, slot_of=None, turn=None):
    shift = lax.rem(128 - first + 128, 128)
    lane = lax.broadcasted_iota(jnp.int32, (GX, LANES), 1)
    inside = jnp.where(lane < GX, 1.0, 0.0).astype(jnp.float32)

    def rolled(ref, scale):
        wide = jnp.concatenate([ref[...].T, jnp.zeros((GX, LANES - GX), jnp.float32)], axis=1)
        return pltpu.roll(wide * scale, shift, 1)

    tables = {
        D: rolled(dep_ref, -0.5 * STEP),
        F: rolled(cor_ref, STEP),
        R: rolled(drag_ref, STEP),
        B: pltpu.roll(inside * (-0.5 * STEP), shift, 1),
    }
    if turn is not None:
        tables[F] = tables[F] * turn
    for j in range(count):
        slot = j if slot_of is None else slot_of(j)
        for kind, table in tables.items():
            coef_ref[slot, kind] = jnp.broadcast_to(table[:, j : j + 1], (GX, LANES))


def total(terms):
    terms = [t for t in terms if t is not None]
    if not terms:
        return None
    acc = terms[0]
    for t in terms[1:]:
        acc = acc + t
    return acc


def tendency(src, have, row, base, coef, slot, ghost=False, want=(0, 1, 2), turn=1):
    def get(r, c, shift=0):
        return src[pl.ds(at(r + base, c) + shift, GX), :]

    def diff_x(c):
        return get(row, c, 1) - get(row, c, -1)

    def diff_y(c):
        above, below = (row + 1, c) in have, (row - 1, c) in have
        if above and below:
            return get(row + 1, c) - get(row - 1, c)
        if above:
            return get(row + 1, c)
        if below:
            return -get(row - 1, c)
        return None

    half = coef[slot, B] if ghost else jnp.float32(-0.5 * STEP)
    center = [get(row, c) if (row, c) in have else None for c in range(3)]
    out = {}
    if 0 in want:
        s = total([diff_x(1) if center[1] is not None else None, diff_y(2)])
        out[0] = None if s is None else coef[slot, D] * s
    if 1 in want:
        dx = half * diff_x(0) if center[0] is not None else None
        spin = None if center[2] is None else (turn * coef[slot, F] if turn != 1 else coef[slot, F]) * center[2]
        drag = None if center[1] is None else -(coef[slot, R] * center[1])
        out[1] = total([dx, spin, drag])
    if 2 in want:
        dy = diff_y(0)
        dy = None if dy is None else half * dy
        spin = None if center[1] is None else (-turn * coef[slot, F]) * center[1]
        drag = None if center[2] is None else -(coef[slot, R] * center[2])
        out[2] = total([dy, spin, drag])
    return out


def powers(bufs, rows, base, coef, finish):
    have = {(r, c) for r in range(rows) for c in range(3)}
    for j, reach in ((1, 1), (2, 2), (3, 1)):
        new = set()
        for r in range(-reach, rows + reach):
            ghost = r < 0 or r >= rows
            want = (0, 2) if ghost and j == 3 else (0, 1, 2)
            out = tendency(bufs[j - 1], have, r, base, coef, r + 2, ghost, want)
            for c, v in out.items():
                if v is not None:
                    bufs[j][pl.ds(at(r + base, c), GX), :] = v if j == 1 else v * (1.0 / j)
                    new.add((r, c))
        have = new
    for r in range(rows):
        out = tendency(bufs[3], have, r, base, coef, r + 2)
        for c in range(3):
            finish(r, c, out[c] * 0.25)


FACT = [1.0, 1.0, 2.0, 6.0, 24.0]


def response(message, bufs, base, coef, slot_of, finish, turn=1):
    heights = [message(j, 0) for j in range(4)]
    norths = [message(j, 1) for j in range(4)]
    forces = []
    for m in range(4):
        weights = [FACT[j] / FACT[j + 1 + m] for j in range(4 - m)]
        fh = total([w * heights[j] for j, w in enumerate(weights)])
        fn = total([w * norths[j] for j, w in enumerate(weights)])
        forces.append((-(coef[slot_of(0), D] * fn), (0.5 * STEP) * fh))
    have = set()
    src = None
    for step, m in enumerate((3, 2, 1, 0)):
        new = set()
        for d in range(step + 1):
            out = {0: None, 1: None, 2: None}
            if src is not None:
                out = tendency(src, have, d, base, coef, slot_of(d), turn=turn)
            if d == 0:
                out[0] = total([out[0], forces[m][0]])
                out[2] = total([out[2], forces[m][1]])
            for c, v in out.items():
                if m == 0:
                    finish(d, c, v)
                elif v is not None:
                    bufs[step % 2][pl.ds(at(d + base, c), GX), :] = v
                    new.add((d, c))
        have, src = new, bufs[step % 2]


def rows_kernel(scal, x_ref, dep, cor, drag, s00, s01, s10, s11, b0, b1, coef, v0, v1, v2, v3, acc, top, bottom):
    rows, base = 8, 2

    @pl.when(pl.program_id(0) == 0)
    def _():
        load_coefficients(dep, cor, drag, scal[0] - 2, rows + 4, coef)
        for ref in (v0, v1, v2, v3):
            zero_gaps(ref, rows + 4)

    for r in range(rows):
        for c in range(3):
            v0[pl.ds(at(r + base, c), GX), :] = x_ref[pl.ds((r * 3 + c) * GX, GX), :]

    def finish(r, c, v4):
        place = r if r < 4 else 4 + (7 - r)
        i = at(r + base, c)
        v = v4 + v3[pl.ds(i, GX), :] + v2[pl.ds(i, GX), :] + v1[pl.ds(i, GX), :] + v0[pl.ds(i, GX), :]
        acc[pl.ds((place * 3 + c) * GX, GX), :] = v

    powers((v0, v1, v2, v3), rows, base, coef, finish)
    for j, ref in enumerate((v0, v1, v2, v3)):
        for i, c in enumerate((0, 2)):
            top[pl.ds((j * 2 + i) * GX, GX), :] = ref[pl.ds(at(base, c), GX), :]
            bottom[pl.ds((j * 2 + i) * GX, GX), :] = ref[pl.ds(at(rows - 1 + base, c), GX), :]

    half, part = 768, 768 // CHUNKS
    core = scal[1]

    @pl.when(core == 0)
    def _():
        s00[...] = acc[pl.ds(0, part), :]
        s01[...] = acc[pl.ds(part, part), :]
        s10[...] = acc[pl.ds(half, part), :]
        s11[...] = acc[pl.ds(half + part, part), :]
        b0[...] = bottom[...]
        b1[...] = top[...]

    @pl.when(core == 1)
    def _():
        s10[...] = acc[pl.ds(0, part), :]
        s11[...] = acc[pl.ds(part, part), :]
        s00[...] = acc[pl.ds(half, part), :]
        s01[...] = acc[pl.ds(half + part, part), :]
        b1[...] = bottom[...]
        b0[...] = top[...]


def whole(ref_shape):
    return pl.BlockSpec(ref_shape, lambda i, *_: tuple(0 for _ in ref_shape))


def vmem(rows, cols=LANES):
    return pltpu.VMEM((rows, cols), jnp.float32)


def shape(rows, cols):
    return jax.ShapeDtypeStruct((rows, cols), jnp.float32)


def params(mib):
    return pltpu.CompilerParams(vmem_limit_bytes=mib * MIB)


def lane_block(rows):
    return pl.BlockSpec((rows, LANES), lambda i, *_: (0, i))


def rows_step(scal, block, fields):
    table = whole((GX, GX))
    part = 768 // CHUNKS
    buf = vmem(buffer_rows(12))
    return pl.pallas_call(
        rows_kernel,
        grid_spec=pltpu.PrefetchScalarGridSpec(
            num_scalar_prefetch=1,
            grid=(3,),
            in_specs=[lane_block(1536), table, table, table],
            out_specs=[lane_block(part)] * 4 + [lane_block(512)] * 2,
            scratch_shapes=[pltpu.VMEM((12, 4, GX, LANES), jnp.float32), buf, buf, buf, buf, vmem(1536), vmem(512), vmem(512)],
        ),
        out_shape=[shape(part, 384)] * 4 + [shape(512, 384)] * 2,
        compiler_params=params(24),
        name="rows_step",
    )(scal, block, *fields)


def rows_response_kernel(scal, m0, m1, dep, cor, drag, r0, r1, coef, t0, t1):
    half = scal[1]
    turn = 1.0 - 2.0 * half.astype(jnp.float32)

    @pl.when(pl.program_id(0) == 0)
    def _():
        load_coefficients(dep, cor, drag, scal[0], 4, coef, lambda j: jnp.where(half == 0, j, 3 - j), turn)
        for ref in (t0, t1):
            zero_gaps(ref, 4)

    for m_ref, r_ref in ((m0, r0), (m1, r1)):

        def message(j, i, m_ref=m_ref):
            v = m_ref[pl.ds((j * 2 + i) * GX, GX), :]
            return v * turn if i == 1 else v

        def finish(d, c, v, r_ref=r_ref):
            v = jnp.zeros((GX, LANES), jnp.float32) if v is None else v
            r_ref[pl.ds((d * 3 + c) * GX, GX), :] = v * turn if c == 2 else v

        response(message, (t0, t1), 0, coef, lambda d: d, finish)


def rows_response(scal, m0, m1, fields):
    table = whole((GX, GX))
    buf = vmem(buffer_rows(4))
    return pl.pallas_call(
        rows_response_kernel,
        grid_spec=pltpu.PrefetchScalarGridSpec(
            num_scalar_prefetch=1,
            grid=(3,),
            in_specs=[lane_block(512)] * 2 + [table] * 3,
            out_specs=[lane_block(768)] * 2,
            scratch_shapes=[pltpu.VMEM((4, 4, GX, LANES), jnp.float32), buf, buf],
        ),
        out_shape=[shape(768, 384)] * 2,
        compiler_params=params(16),
        name="rows_response",
    )(scal, m0, m1, *fields)


def columns_kernel(scal, s0, s1, r0, r1, dep, cor, drag, out, left, right, coef, v0, v1, v2, v3):
    rows, base = 4, 2
    half = scal[1]

    @pl.when(pl.program_id(0) == 0)
    def _():
        load_coefficients(dep, cor, drag, scal[0] - 2, rows + 4, coef)
        for ref in (v0, v1, v2, v3):
            zero_gaps(ref, rows + 4)

    for k, (s_ref, r_ref) in enumerate(((s0, r0), (s1, r1))):
        core = half if k == 0 else 1 - half
        start = pl.multiple_of(core * (2 * 3 * SEG), 8)
        for t in range(3):
            piece = (s_ref[:, t * LANES : (t + 1) * LANES] + r_ref[:, t * LANES : (t + 1) * LANES]).T
            for i in range(2):
                seg = t * 2 + i
                place = pl.multiple_of(start + (base * 3 + seg) * SEG + 8, 8)
                v0[pl.ds(place, GX), :] = piece[i * GX : (i + 1) * GX, :]

    def finish(r, c, v4):
        i = at(r + base, c)
        v = v4 + v3[pl.ds(i, GX), :] + v2[pl.ds(i, GX), :] + v1[pl.ds(i, GX), :] + v0[pl.ds(i, GX), :]
        out[pl.ds((r * 3 + c) * GX, GX), :] = v

    powers((v0, v1, v2, v3), rows, base, coef, finish)
    for j, ref in enumerate((v0, v1, v2, v3)):
        for i, c in enumerate((0, 2)):
            left[pl.ds((j * 2 + i) * GX, GX), :] = ref[pl.ds(at(base, c), GX), :]
            right[pl.ds((j * 2 + i) * GX, GX), :] = ref[pl.ds(at(rows - 1 + base, c), GX), :]


def columns_step(scal, s0, s1, r0, r1, fields, chunk):
    table = whole((GX, GX))
    part = 768 // CHUNKS
    tiles = part // LANES
    buf = vmem(buffer_rows(8))
    return pl.pallas_call(
        columns_kernel,
        grid_spec=pltpu.PrefetchScalarGridSpec(
            num_scalar_prefetch=1,
            grid=(tiles,),
            in_specs=[pl.BlockSpec((LANES, 384), lambda i, *_: (i, 0))] * 2
            + [pl.BlockSpec((LANES, 384), lambda i, *_: (i + chunk * tiles, 0))] * 2
            + [table] * 3,
            out_specs=[lane_block(768), lane_block(512), lane_block(512)],
            scratch_shapes=[pltpu.VMEM((8, 4, GX, LANES), jnp.float32), buf, buf, buf, buf],
        ),
        out_shape=[shape(768, part), shape(512, part), shape(512, part)],
        compiler_params=params(24),
        name="columns_step",
    )(scal, s0, s1, r0, r1, *fields)


def columns_response_kernel(scal, own, from_left, from_right, dep, cor, drag, z0, z1, coef, t0, t1, acc):
    half = scal[1]

    @pl.when(pl.program_id(0) == 0)
    def _():
        load_coefficients(dep, cor, drag, scal[0], 4, coef)
        for ref in (t0, t1):
            zero_gaps(ref, 4)

    def message_left(j, i):
        return from_left[pl.ds((j * 2 + i) * GX, GX), :]

    def finish_left(d, c, v):
        i = pl.ds((d * 3 + c) * GX, GX)
        acc[i, :] = own[i, :] if v is None else own[i, :] + v

    response(message_left, (t0, t1), 0, coef, lambda d: d, finish_left)

    def message_right(j, i):
        v = from_right[pl.ds((j * 2 + i) * GX, GX), :]
        return -v if i == 1 else v

    def finish_right(d, c, v):
        i = pl.ds(((3 - d) * 3 + c) * GX, GX)
        if v is not None:
            acc[i, :] = acc[i, :] + (-v if c == 2 else v)

    response(message_right, (t0, t1), 0, coef, lambda d: 3 - d, finish_right, turn=-1)
    for k, z_ref in enumerate((z0, z1)):
        core = half if k == 0 else 1 - half
        for t in range(3):
            place = pl.multiple_of(core * 384 + t * LANES, LANES)
            z_ref[:, t * LANES : (t + 1) * LANES] = acc[pl.ds(place, LANES), :].T


def columns_response(scal, own, from_left, from_right, fields):
    table = whole((GX, GX))
    part = 768 // CHUNKS
    buf = vmem(buffer_rows(4))
    return pl.pallas_call(
        columns_response_kernel,
        grid_spec=pltpu.PrefetchScalarGridSpec(
            num_scalar_prefetch=1,
            grid=(part // LANES,),
            in_specs=[lane_block(768), lane_block(512), lane_block(512)] + [table] * 3,
            out_specs=[pl.BlockSpec((LANES, 384), lambda i, *_: (i, 0))] * 2,
            scratch_shapes=[pltpu.VMEM((4, 4, GX, LANES), jnp.float32), buf, buf, vmem(768)],
        ),
        out_shape=[shape(part, 384)] * 2,
        compiler_params=params(16),
        name="columns_response",
    )(scal, own, from_left, from_right, *fields)


def finish_kernel(scal, z0, z1, noise, *rest):
    out = rest[-1]
    k = pl.program_id(0)

    @pl.when(k == 0)
    def _():
        out[...] = z0[...] + noise[...]

    @pl.when(k == 1)
    def _():
        out[...] = z1[...] + noise[...]


def finish_step(scal, z0, z1, noise, chunk, out=None):
    per = 4 // CHUNKS

    def place(k, i, scal):
        d = chunk * per + i
        half = jnp.where(k == 0, scal[1], 1 - scal[1])
        return (jnp.where(half == 0, d, 7 - d), 0)

    first = pl.BlockSpec((192, 384), lambda k, i, scal: (jnp.where(k == 0, i, per - 1), 0))
    second = pl.BlockSpec((192, 384), lambda k, i, scal: (jnp.where(k == 1, i, 0), 0))
    block = pl.BlockSpec((192, 384), place)
    extra = [] if out is None else [out]
    return pl.pallas_call(
        finish_kernel,
        grid_spec=pltpu.PrefetchScalarGridSpec(
            num_scalar_prefetch=1,
            grid=(2, per),
            in_specs=[first, second, block] + [pl.BlockSpec(memory_space=pl.ANY)] * len(extra),
            out_specs=block,
        ),
        out_shape=shape(1536, 384),
        input_output_aliases={} if out is None else {4: 0},
        compiler_params=params(12),
        name="finish_step",
    )(scal, z0, z1, noise, *extra)


def permutations(rows, cols):
    def joint(r, z, a, b):
        return r * cols + z * 4 + a * 2 + b

    split, boundary, back = [[], []], [[], []], [[], []]
    for k in range(2):
        for r in range(rows):
            for z in range(cols // 4):
                for lo in range(2):
                    for core in range(2):
                        me = joint(r, z, lo, core)
                        split[k].append((me, joint(r, z, core ^ k, lo)))
                        if core == k and r + 1 < rows:
                            boundary[k].append((me, joint(r + 1, z, 0, lo)))
                        if core != k and r > 0:
                            boundary[k].append((me, joint(r - 1, z, 1, lo)))
                        back[k].append((me, joint(r, z, core, lo ^ k)))
    rightward = []
    for z in range(cols // 4):
        for p in range(2):
            rightward.append((z * 4 + p * 2, z * 4 + p * 2 + 1))
            if z + 1 < cols // 4:
                rightward.append((z * 4 + p * 2 + 1, (z + 1) * 4 + p * 2))
    leftward = [(b, a) for a, b in rightward]
    return split, boundary, back, rightward, leftward


def shards(covariance, process_noise, depth_field, coriolis, drag_rate):
    fields = (depth_field, coriolis, drag_rate)
    rows, cols = lax.axis_size("row"), lax.axis_size("col")
    split, boundary, back, rightward, leftward = permutations(rows, cols)
    row, col = lax.axis_index("row"), lax.axis_index("col")
    z, second, core = col // 4, (col // 2) % 2, col % 2
    both = ("row", "col")

    scal = jnp.stack([row * 8, core]).astype(jnp.int32)
    s00, s01, s10, s11, b0, b1 = rows_step(scal, covariance, fields)
    m0 = lax.ppermute(b0, both, boundary[0])
    m1 = lax.ppermute(b1, both, boundary[1])
    pieces = [
        [lax.ppermute(s, both, split[k]) for k, s in enumerate(pair)] for pair in ((s00, s10), (s01, s11))
    ]
    rscal = jnp.stack([row * 8 + second * 4, second]).astype(jnp.int32)
    r0, r1 = rows_response(rscal, m0, m1, fields)

    cscal = jnp.stack([(z * 2 + core) * 4, second]).astype(jnp.int32)
    result = None
    fscal = jnp.stack([row, core]).astype(jnp.int32)
    for chunk, (s0, s1) in enumerate(pieces):
        own, left, right = columns_step(cscal, s0, s1, r0, r1, fields, chunk)
        from_left = lax.ppermute(right, "col", rightward)
        from_right = lax.ppermute(left, "col", leftward)
        z0, z1 = columns_response(cscal, own, from_left, from_right, fields)
        z0 = lax.ppermute(z0, both, back[0])
        z1 = lax.ppermute(z1, both, back[1])
        result = finish_step(fscal, z0, z1, process_noise, chunk, result)
    return result


def solution(mesh):
    return jax.shard_map(
        shards,
        mesh=mesh,
        in_specs=(P("row", "col"), P("row", "col"), P(), P(), P()),
        out_specs=P("row", "col"),
        check_vma=False,
    )
```

time: 239 us -> 115 us (0.48)
  the two profiles are of different devices: /device:TPU:193 before, /device:TPU:100 now
where the time goes in v1:
time: 115 us; the launch traced here: 114 us
  starting transfers between devices  59.7 us (52%)
  Pallas kernels  27.1 us (24%)
  waiting for transfers between devices  22.9 us (20%)
  local copies, waits for them, and re-layouts  3.95 us (3%)
    ppermute x4, starting transfers between devices, shards(): lax.ppermute(s, both, split[k])  29.2 us
    ppermute x2, waiting for transfers between devices, shards(): z1 = lax.ppermute(z1, both, back[1])  15.6 us
    ppermute x2, starting transfers between devices, shards(): z1 = lax.ppermute(z1, both, back[1])  12.7 us
    pallas_call x2, Pallas kernels, columns_step(): pl.pallas_call(columns_kernel, grid_spec=pltpu.PrefetchScalarGridSpec(num...  8.21 us
    ppermute x1, waiting for transfers between devices, shards(): m0 = lax.ppermute(b0, both, boundary[0])  6.99 us
    pallas_call x1, Pallas kernels, rows_step(): pl.pallas_call(rows_kernel, grid_spec=pltpu.PrefetchScalarGridSpec(num_sc...  6.18 us
    pallas_call x2, Pallas kernels, columns_response(): pl.pallas_call(columns_response_kernel, grid_spec=pltpu.PrefetchScalarGri...  5.92 us
    ppermute x2, starting transfers between devices, shards(): from_right = lax.ppermute(left, 'col', leftward)  5.79 us
  transfers between devices with their start and end apart: 14, of which 4 were waited for; matrix products, arithmetic and copies ran while one was open for 0% of the time, Pallas kernels for 16%

profile of v1, /device:TPU:100, one launch (start us, length us, event | category | flops | bytes accessed | tf_op | source)
XLA Modules:
  0.0 114.1 jit_solution(11275309336565385557)
XLA Ops:
  0.1 1.7 %copy-done.1 = f32[1536,384]{1,0:T(8,128)S(1)} copy-done((f32[1536,384]{1,0:T(8,128)S(1)}, f32[1536,384]{1,0:T(8,128)}, u32[]{:S(2)}) %copy-start.1) | copy-done | bytes 2359320
  4.0 6.2 %rows_step.1 = (f32[384,384]{1,0:T(8,128)}, f32[384,384]{1,0:T(8,128)}, f32[384,384]{1,0:T(8,128)}, f32[384,384]{1,0:T(8,128)}, f32[512,384]{1,0:T(8,128)S(1)}, /*index=5*/f32[512,384]{1,0:T(8,128)}) custom-call(s32[2]{0:T(128)S(1)} %pad_add_fusion.2.scal, f32[1536,384]{1,0:T(8,128)S(1)} %copy-done.1, f32[64,64]{1,0:T(8,128)S(1)} %copy-done.2, ...), custom_call_target="tpu_custom_call" | custom-call | tf_op jit(solution)/shard_map/rows_step/pallas_call | solution.py:224
  10.2 3.4 %collective-permute-start.2 = (f32[512,384]{1,0:T(8,128)S(1)}, f32[512,384]{1,0:T(8,128)S(1)}, u32[]{:S(2)}, u32[]{:S(2)}) collective-permute-start(f32[512,384]{1,0:T(8,128)S(1)} %get-tuple-element.25), channel_id=1, source_target_pairs={{0,32},{2,33},{4,36},{6,37},{8,40},{10,41},{12,44},{14,45},{16,48}... | collective-permute-start | bytes 2359304 | tf_op jit(solution)/shard_map/ppermute | solution.py:465
  13.6 1.9 %collective-permute-start.3 = (f32[512,384]{1,0:T(8,128)}, f32[512,384]{1,0:T(8,128)S(1)}, u32[]{:S(2)}, u32[]{:S(2)}) collective-permute-start(f32[512,384]{1,0:T(8,128)} %get-tuple-element.26), channel_id=1, source_target_pairs={{1,32},{3,33},{5,36},{7,37},{9,40},{11,41},{13,44},{15,45},{17,48}... | collective-permute-start | bytes 2359304 | tf_op jit(solution)/shard_map/ppermute | solution.py:466
  15.6 1.7 %collective-permute-start.8 = (f32[384,384]{1,0:T(8,128)}, f32[384,384]{1,0:T(8,128)S(1)}, u32[]{:S(2)}, u32[]{:S(2)}) collective-permute-start(f32[384,384]{1,0:T(8,128)} %get-tuple-element.34), channel_id=1, source_target_pairs={{0,0},{1,2},{2,1},{3,3},{4,4},{5,6},{6,5},{7,7},{8,8},{9,10},{10,9... | collective-permute-start | bytes 1769480 | tf_op jit(solution)/shard_map/ppermute | solution.py:468
  17.3 5.0 %collective-permute-start.9 = (f32[384,384]{1,0:T(8,128)}, f32[384,384]{1,0:T(8,128)}, u32[]{:S(2)}, u32[]{:S(2)}) collective-permute-start(f32[384,384]{1,0:T(8,128)} %get-tuple-element.35), channel_id=1, source_target_pairs={{0,2},{1,0},{2,3},{3,1},{4,6},{5,4},{6,7},{7,5},{8,10},{9,8},{10,1... | collective-permute-start | bytes 1769480 | tf_op jit(solution)/shard_map/ppermute | solution.py:468
  22.3 1.7 %collective-permute-start = (f32[384,384]{1,0:T(8,128)}, f32[384,384]{1,0:T(8,128)S(1)}, u32[]{:S(2)}, u32[]{:S(2)}) collective-permute-start(f32[384,384]{1,0:T(8,128)} %get-tuple-element.23), channel_id=1, source_target_pairs={{0,0},{1,2},{2,1},{3,3},{4,4},{5,6},{6,5},{7,7},{8,8},{9,10},{10,9... | collective-permute-start | bytes 1769480 | tf_op jit(solution)/shard_map/ppermute | solution.py:468
  24.0 7.0 %collective-permute-done.2.m0 = f32[512,384]{1,0:T(8,128)S(1)} collective-permute-done((f32[512,384]{1,0:T(8,128)S(1)}, f32[512,384]{1,0:T(8,128)S(1)}, u32[]{:S(2)}, u32[]{:S(2)}) %collective-permute-start.2) | collective-permute-done | bytes 786464 | tf_op jit(solution)/shard_map/ppermute | solution.py:465
  31.0 20.7 %collective-permute-start.1 = (f32[384,384]{1,0:T(8,128)}, f32[384,384]{1,0:T(8,128)S(1)}, u32[]{:S(2)}, u32[]{:S(2)}) collective-permute-start(f32[384,384]{1,0:T(8,128)} %get-tuple-element.24), channel_id=1, source_target_pairs={{0,2},{1,0},{2,3},{3,1},{4,6},{5,4},{6,7},{7,5},{8,10},{9,8},{10,1... | collective-permute-start | bytes 1769480 | tf_op jit(solution)/shard_map/ppermute | solution.py:468
  51.9 2.5 %rows_response.1 = (f32[768,384]{1,0:T(8,128)S(1)}, f32[768,384]{1,0:T(8,128)S(1)}) custom-call(s32[2]{0:T(128)S(1)} %pad_add_fusion.3.scal, f32[512,384]{1,0:T(8,128)S(1)} %collective-permute-done.2.m0, f32[512,384]{1,0:T(8,128)S(1)} %collective-permute-done.3.m1, f32[64,64]{1,0:T(8,128)S(1)} %copy-done.3, f32[64,64]{1,0:T(8,128)S(1)} %copy-done.5, ...), custom_call_target="tpu_custom_call" | custom-call | tf_op jit(solution)/shard_map/rows_response/pallas_call | solution.py:265
  54.4 4.6 %columns_step.3 = (f32[768,384]{1,0:T(8,128)S(1)}, f32[512,384]{1,0:T(8,128)S(1)}, f32[512,384]{1,0:T(8,128)S(1)}) custom-call(s32[2]{0:T(128)S(1)} %pad_add_fusion.1.scal, f32[384,384]{1,0:T(8,128)S(1)} %collective-permute-done.8.s0, f32[384,384]{1,0:T(8,128)} %collective-permute-done.9.s1, f32[768,384]{1,0:T(8,128)S(1)} %get-tuple-element.27.r0, ...), custom_call_target="tpu_custom_call" | custom-call | tf_op jit(solution)/shard_map/columns_step/pallas_call | solution.py:317
  59.0 1.9 %collective-permute-start.10 = (f32[512,384]{1,0:T(8,128)S(1)}, f32[512,384]{1,0:T(8,128)S(1)}, u32[]{:S(2)}, u32[]{:S(2)}) collective-permute-start(f32[512,384]{1,0:T(8,128)S(1)} %get-tuple-element.37), channel_id=1, source_target_pairs={{0,1},{1,4},{2,3},{3,6},{4,5},{5,8},{6,7},{7,10},{8,9},{9,12},{10,... | collective-permute-start | bytes 2359304 | tf_op jit(solution)/shard_map/ppermute | solution.py:478
  60.9 3.6 %collective-permute-start.11 = (f32[512,384]{1,0:T(8,128)S(1)}, f32[512,384]{1,0:T(8,128)S(1)}, u32[]{:S(2)}, u32[]{:S(2)}) collective-permute-start(f32[512,384]{1,0:T(8,128)S(1)} %get-tuple-element.38), channel_id=1, source_target_pairs={{1,0},{4,1},{3,2},{6,3},{5,4},{8,5},{7,6},{10,7},{9,8},{12,9},{11,... | collective-permute-start | bytes 2359304 | tf_op jit(solution)/shard_map/ppermute | solution.py:479
  64.6 3.6 %columns_step.2 = (f32[768,384]{1,0:T(8,128)S(1)}, f32[512,384]{1,0:T(8,128)S(1)}, f32[512,384]{1,0:T(8,128)S(1)}) custom-call(s32[2]{0:T(128)S(1)} %pad_add_fusion.1.scal, f32[384,384]{1,0:T(8,128)S(1)} %collective-permute-done.s0, f32[384,384]{1,0:T(8,128)S(1)} %collective-permute-done.1.s1, f32[768,384]{1,0:T(8,128)S(1)} %get-tuple-element.27.r0, ...), custom_call_target="tpu_custom_call" | custom-call | tf_op jit(solution)/shard_map/columns_step/pallas_call | solution.py:317
  68.2 3.4 %collective-permute-start.4 = (f32[512,384]{1,0:T(8,128)S(1)}, f32[512,384]{1,0:T(8,128)S(1)}, u32[]{:S(2)}, u32[]{:S(2)}) collective-permute-start(f32[512,384]{1,0:T(8,128)S(1)} %get-tuple-element.30), channel_id=1, source_target_pairs={{0,1},{1,4},{2,3},{3,6},{4,5},{5,8},{6,7},{7,10},{8,9},{9,12},{10,... | collective-permute-start | bytes 2359304 | tf_op jit(solution)/shard_map/ppermute | solution.py:478
  71.6 2.1 %collective-permute-start.5 = (f32[512,384]{1,0:T(8,128)S(1)}, f32[512,384]{1,0:T(8,128)S(1)}, u32[]{:S(2)}, u32[]{:S(2)}) collective-permute-start(f32[512,384]{1,0:T(8,128)S(1)} %get-tuple-element.31), channel_id=1, source_target_pairs={{1,0},{4,1},{3,2},{6,3},{5,4},{8,5},{7,6},{10,7},{9,8},{12,9},{11,... | collective-permute-start | bytes 2359304 | tf_op jit(solution)/shard_map/ppermute | solution.py:479
  74.0 3.0 %columns_response.3 = (f32[384,384]{1,0:T(8,128)S(1)}, f32[384,384]{1,0:T(8,128)S(1)}) custom-call(s32[2]{0:T(128)S(1)} %pad_add_fusion.1.scal, f32[768,384]{1,0:T(8,128)S(1)} %get-tuple-element.36.own, f32[512,384]{1,0:T(8,128)S(1)} %collective-permute-done.10.from_left, f32[512,384]{1,0:T(8,128)S(1)} %collective-permute-done.11.from_right, ...), custom_call_target="tpu_custom_call" | custom-call | tf_op jit(solution)/shard_map/columns_response/pallas_call | solution.py:373
  77.7 5.9 %collective-permute-start.13 = (f32[384,384]{1,0:T(8,128)S(1)}, f32[384,384]{1,0:T(8,128)S(1)}, u32[]{:S(2)}, u32[]{:S(2)}) collective-permute-start(f32[384,384]{1,0:T(8,128)S(1)} %get-tuple-element.40), channel_id=1, source_target_pairs={{0,1},{1,3},{2,0},{3,2},{4,5},{5,7},{6,4},{7,6},{8,9},{9,11},{10,8... | collective-permute-start | bytes 1769480 | tf_op jit(solution)/shard_map/ppermute | solution.py:482
  83.6 3.0 %columns_response.2 = (f32[384,384]{1,0:T(8,128)S(1)}, f32[384,384]{1,0:T(8,128)S(1)}) custom-call(s32[2]{0:T(128)S(1)} %pad_add_fusion.1.scal, f32[768,384]{1,0:T(8,128)S(1)} %get-tuple-element.29.own, f32[512,384]{1,0:T(8,128)S(1)} %collective-permute-done.4.from_left, f32[512,384]{1,0:T(8,128)S(1)} %collective-permute-done.5.from_right, ...), custom_call_target="tpu_custom_call" | custom-call | tf_op jit(solution)/shard_map/columns_response/pallas_call | solution.py:373
  87.3 6.8 %collective-permute-start.7 = (f32[384,384]{1,0:T(8,128)S(1)}, f32[384,384]{1,0:T(8,128)S(1)}, u32[]{:S(2)}, u32[]{:S(2)}) collective-permute-start(f32[384,384]{1,0:T(8,128)S(1)} %get-tuple-element.33), channel_id=1, source_target_pairs={{0,1},{1,3},{2,0},{3,2},{4,5},{5,7},{6,4},{7,6},{8,9},{9,11},{10,8... | collective-permute-start | bytes 1769480 | tf_op jit(solution)/shard_map/ppermute | solution.py:482
  94.1 5.2 %collective-permute-done.13.z1 = f32[384,384]{1,0:T(8,128)S(1)} collective-permute-done((f32[384,384]{1,0:T(8,128)S(1)}, f32[384,384]{1,0:T(8,128)S(1)}, u32[]{:S(2)}, u32[]{:S(2)}) %collective-permute-start.13) | collective-permute-done | bytes 589856 | tf_op jit(solution)/shard_map/ppermute | solution.py:482
  99.3 2.2 %finish_step.2.rest_0_ = f32[1536,384]{1,0:T(8,128)} custom-call(s32[2]{0:T(128)S(1)} %pad_add_fusion.scal, f32[384,384]{1,0:T(8,128)S(1)} %collective-permute-done.12.z0, f32[384,384]{1,0:T(8,128)S(1)} %collective-permute-done.13.z1, f32[1536,384]{1,0:T(8,128)S(1)} %copy-done), custom_call_target="tpu_custom_call" | custom-call | tf_op jit(solution)/shard_map/finish_step/pallas_call | solution.py:413
  101.5 10.4 %collective-permute-done.7.z1 = f32[384,384]{1,0:T(8,128)S(1)} collective-permute-done((f32[384,384]{1,0:T(8,128)S(1)}, f32[384,384]{1,0:T(8,128)S(1)}, u32[]{:S(2)}, u32[]{:S(2)}) %collective-permute-start.7) | collective-permute-done | bytes 589856 | tf_op jit(solution)/shard_map/ppermute | solution.py:482
  112.0 2.2 %finish_step.3 = f32[1536,384]{1,0:T(8,128)} custom-call(s32[2]{0:T(128)S(1)} %pad_add_fusion.scal, f32[384,384]{1,0:T(8,128)S(1)} %collective-permute-done.6.z0, f32[384,384]{1,0:T(8,128)S(1)} %collective-permute-done.7.z1, f32[1536,384]{1,0:T(8,128)S(1)} %copy-done, f32[1536,384]{1,0:T(8,128)} %finish_step.2.rest_0_), custom_call_target="tpu_custom_call", output_to_operand_aliasing={{}: (4, {})} | custom-call | tf_op jit(solution)/shard_map/finish_step/pallas_call | solution.py:413
  (32 shorter events, 4.3 us)
Async XLA Ops:
  0.0 51.9 %copy-start.3 = (f32[64,64]{1,0:T(8,128)S(1)}, f32[64,64]{1,0:T(8,128)}, u32[]{:S(2)}) copy-start(f32[64,64]{1,0:T(8,128)} %dep.11) | copy-start | bytes 49156
  0.1 1.7 %copy-start.1 = (f32[1536,384]{1,0:T(8,128)S(1)}, f32[1536,384]{1,0:T(8,128)}, u32[]{:S(2)}) copy-start(f32[1536,384]{1,0:T(8,128)} %x_ref.1) | copy-start | bytes 7077892
  1.7 0.8 copy-start.2
  2.5 0.8 copy-start.4
  3.3 0.8 copy-start.6
  4.0 47.8 %copy-start.5 = (f32[64,64]{1,0:T(8,128)S(1)}, f32[64,64]{1,0:T(8,128)}, u32[]{:S(2)}) copy-start(f32[64,64]{1,0:T(8,128)} %cor.11) | copy-start | bytes 49156
  4.0 47.9 %copy-start.7 = (f32[64,64]{1,0:T(8,128)S(1)}, f32[64,64]{1,0:T(8,128)}, u32[]{:S(2)}) copy-start(f32[64,64]{1,0:T(8,128)} %drag.11) | copy-start | bytes 49156
  10.2 20.8 %collective-permute-start.2 = (f32[512,384]{1,0:T(8,128)S(1)}, f32[512,384]{1,0:T(8,128)S(1)}, u32[]{:S(2)}, u32[]{:S(2)}) collective-permute-start(f32[512,384]{1,0:T(8,128)S(1)} %get-tuple-element.25), channel_id=1, source_target_pairs={{0,32},{2,33},{4,36},{6,37},{8,40},{10,41},{12,44},{14,45},{16,48}... | collective-permute-start | bytes 2359304 | tf_op jit(solution)/shard_map/ppermute | solution.py:465
  13.6 38.2 %collective-permute-start.3 = (f32[512,384]{1,0:T(8,128)}, f32[512,384]{1,0:T(8,128)S(1)}, u32[]{:S(2)}, u32[]{:S(2)}) collective-permute-start(f32[512,384]{1,0:T(8,128)} %get-tuple-element.26), channel_id=1, source_target_pairs={{1,32},{3,33},{5,36},{7,37},{9,40},{11,41},{13,44},{15,45},{17,48}... | collective-permute-start | bytes 2359304 | tf_op jit(solution)/shard_map/ppermute | solution.py:466
  15.6 38.8 %collective-permute-start.8 = (f32[384,384]{1,0:T(8,128)}, f32[384,384]{1,0:T(8,128)S(1)}, u32[]{:S(2)}, u32[]{:S(2)}) collective-permute-start(f32[384,384]{1,0:T(8,128)} %get-tuple-element.34), channel_id=1, source_target_pairs={{0,0},{1,2},{2,1},{3,3},{4,4},{5,6},{6,5},{7,7},{8,8},{9,10},{10,9... | collective-permute-start | bytes 1769480 | tf_op jit(solution)/shard_map/ppermute | solution.py:468
  17.3 37.1 %collective-permute-start.9 = (f32[384,384]{1,0:T(8,128)}, f32[384,384]{1,0:T(8,128)}, u32[]{:S(2)}, u32[]{:S(2)}) collective-permute-start(f32[384,384]{1,0:T(8,128)} %get-tuple-element.35), channel_id=1, source_target_pairs={{0,2},{1,0},{2,3},{3,1},{4,6},{5,4},{6,7},{7,5},{8,10},{9,8},{10,1... | collective-permute-start | bytes 1769480 | tf_op jit(solution)/shard_map/ppermute | solution.py:468
  22.3 42.2 %collective-permute-start = (f32[384,384]{1,0:T(8,128)}, f32[384,384]{1,0:T(8,128)S(1)}, u32[]{:S(2)}, u32[]{:S(2)}) collective-permute-start(f32[384,384]{1,0:T(8,128)} %get-tuple-element.23), channel_id=1, source_target_pairs={{0,0},{1,2},{2,1},{3,3},{4,4},{5,6},{6,5},{7,7},{8,8},{9,10},{10,9... | collective-permute-start | bytes 1769480 | tf_op jit(solution)/shard_map/ppermute | solution.py:468
  31.0 33.5 %collective-permute-start.1 = (f32[384,384]{1,0:T(8,128)}, f32[384,384]{1,0:T(8,128)S(1)}, u32[]{:S(2)}, u32[]{:S(2)}) collective-permute-start(f32[384,384]{1,0:T(8,128)} %get-tuple-element.24), channel_id=1, source_target_pairs={{0,2},{1,0},{2,3},{3,1},{4,6},{5,4},{6,7},{7,5},{8,10},{9,8},{10,1... | collective-permute-start | bytes 1769480 | tf_op jit(solution)/shard_map/ppermute | solution.py:468
  59.0 14.8 %collective-permute-start.10 = (f32[512,384]{1,0:T(8,128)S(1)}, f32[512,384]{1,0:T(8,128)S(1)}, u32[]{:S(2)}, u32[]{:S(2)}) collective-permute-start(f32[512,384]{1,0:T(8,128)S(1)} %get-tuple-element.37), channel_id=1, source_target_pairs={{0,1},{1,4},{2,3},{3,6},{4,5},{5,8},{6,7},{7,10},{8,9},{9,12},{10,... | collective-permute-start | bytes 2359304 | tf_op jit(solution)/shard_map/ppermute | solution.py:478
  60.9 13.1 %collective-permute-start.11 = (f32[512,384]{1,0:T(8,128)S(1)}, f32[512,384]{1,0:T(8,128)S(1)}, u32[]{:S(2)}, u32[]{:S(2)}) collective-permute-start(f32[512,384]{1,0:T(8,128)S(1)} %get-tuple-element.38), channel_id=1, source_target_pairs={{1,0},{4,1},{3,2},{6,3},{5,4},{8,5},{7,6},{10,7},{9,8},{12,9},{11,... | collective-permute-start | bytes 2359304 | tf_op jit(solution)/shard_map/ppermute | solution.py:479
  68.2 15.4 %collective-permute-start.4 = (f32[512,384]{1,0:T(8,128)S(1)}, f32[512,384]{1,0:T(8,128)S(1)}, u32[]{:S(2)}, u32[]{:S(2)}) collective-permute-start(f32[512,384]{1,0:T(8,128)S(1)} %get-tuple-element.30), channel_id=1, source_target_pairs={{0,1},{1,4},{2,3},{3,6},{4,5},{5,8},{6,7},{7,10},{8,9},{9,12},{10,... | collective-permute-start | bytes 2359304 | tf_op jit(solution)/shard_map/ppermute | solution.py:478
  71.6 12.0 %collective-permute-start.5 = (f32[512,384]{1,0:T(8,128)S(1)}, f32[512,384]{1,0:T(8,128)S(1)}, u32[]{:S(2)}, u32[]{:S(2)}) collective-permute-start(f32[512,384]{1,0:T(8,128)S(1)} %get-tuple-element.31), channel_id=1, source_target_pairs={{1,0},{4,1},{3,2},{6,3},{5,4},{8,5},{7,6},{10,7},{9,8},{12,9},{11,... | collective-permute-start | bytes 2359304 | tf_op jit(solution)/shard_map/ppermute | solution.py:479
  74.0 25.3 %copy-start = (f32[1536,384]{1,0:T(8,128)S(1)}, f32[1536,384]{1,0:T(8,128)}, u32[]{:S(2)}) copy-start(f32[1536,384]{1,0:T(8,128)} %noise.3) | copy-start | bytes 7077892
  77.0 17.1 %collective-permute-start.12 = (f32[384,384]{1,0:T(8,128)S(1)}, f32[384,384]{1,0:T(8,128)S(1)}, u32[]{:S(2)}, u32[]{:S(2)}) collective-permute-start(f32[384,384]{1,0:T(8,128)S(1)} %get-tuple-element.39), channel_id=1, source_target_pairs={{0,0},{1,2},{2,1},{3,3},{4,4},{5,6},{6,5},{7,7},{8,8},{9,10},{10,9... | collective-permute-start | bytes 1769480 | tf_op jit(solution)/shard_map/ppermute | solution.py:481
  77.7 21.6 %collective-permute-start.13 = (f32[384,384]{1,0:T(8,128)S(1)}, f32[384,384]{1,0:T(8,128)S(1)}, u32[]{:S(2)}, u32[]{:S(2)}) collective-permute-start(f32[384,384]{1,0:T(8,128)S(1)} %get-tuple-element.40), channel_id=1, source_target_pairs={{0,1},{1,3},{2,0},{3,2},{4,5},{5,7},{6,4},{7,6},{8,9},{9,11},{10,8... | collective-permute-start | bytes 1769480 | tf_op jit(solution)/shard_map/ppermute | solution.py:482
  86.6 14.9 %collective-permute-start.6 = (f32[384,384]{1,0:T(8,128)S(1)}, f32[384,384]{1,0:T(8,128)S(1)}, u32[]{:S(2)}, u32[]{:S(2)}) collective-permute-start(f32[384,384]{1,0:T(8,128)S(1)} %get-tuple-element.32), channel_id=1, source_target_pairs={{0,0},{1,2},{2,1},{3,3},{4,4},{5,6},{6,5},{7,7},{8,8},{9,10},{10,9... | collective-permute-start | bytes 1769480 | tf_op jit(solution)/shard_map/ppermute | solution.py:481
  87.3 24.6 %collective-permute-start.7 = (f32[384,384]{1,0:T(8,128)S(1)}, f32[384,384]{1,0:T(8,128)S(1)}, u32[]{:S(2)}, u32[]{:S(2)}) collective-permute-start(f32[384,384]{1,0:T(8,128)S(1)} %get-tuple-element.33), channel_id=1, source_target_pairs={{0,1},{1,3},{2,0},{3,2},{4,5},{5,7},{6,4},{7,6},{8,9},{9,11},{10,8... | collective-permute-start | bytes 1769480 | tf_op jit(solution)/shard_map/ppermute | solution.py:482

commit v2 on v1

--- a/solution.py
+++ b/solution.py
@@ -29,7 +29,7 @@
         ref[pl.ds(i * SEG, 8), :] = jnp.zeros((8, LANES), jnp.float32)
 
 
-def load_coefficients(dep_ref, cor_ref, drag_ref, first, count, coef_ref, slot_of=None, turn=None):
+def load_coefficients(dep_ref, cor_ref, drag_ref, first, count, coef_ref, slot_of=None, turn=None, only=None):
     shift = lax.rem(128 - first + 128, 128)
     lane = lax.broadcasted_iota(jnp.int32, (GX, LANES), 1)
     inside = jnp.where(lane < GX, 1.0, 0.0).astype(jnp.float32)
@@ -46,7 +46,7 @@
     }
     if turn is not None:
         tables[F] = tables[F] * turn
-    for j in range(count):
+    for j in only or range(count):
         slot = j if slot_of is None else slot_of(j)
         for kind, table in tables.items():
             coef_ref[slot, kind] = jnp.broadcast_to(table[:, j : j + 1], (GX, LANES))
@@ -121,15 +121,18 @@
 FACT = [1.0, 1.0, 2.0, 6.0, 24.0]
 
 
-def response(message, bufs, base, coef, slot_of, finish, turn=1):
-    heights = [message(j, 0) for j in range(4)]
-    norths = [message(j, 1) for j in range(4)]
-    forces = []
-    for m in range(4):
-        weights = [FACT[j] / FACT[j + 1 + m] for j in range(4 - m)]
-        fh = total([w * heights[j] for j, w in enumerate(weights)])
-        fn = total([w * norths[j] for j, w in enumerate(weights)])
-        forces.append((-(coef[slot_of(0), D] * fn), (0.5 * STEP) * fh))
+def response(message, bufs, base, coef, slot_of, finish, turn=1, powers_in=(0, 1, 2, 3)):
+    heights = {j: message(j, 0) for j in powers_in}
+    norths = {j: message(j, 1) for j in powers_in}
+
+    def force(m):
+        weights = {j: FACT[j] / FACT[j + 1 + m] for j in powers_in if j <= 3 - m}
+        if not weights:
+            return None, None
+        fh = total([w * heights[j] for j, w in weights.items()])
+        fn = total([w * norths[j] for j, w in weights.items()])
+        return -(coef[slot_of(0), D] * fn), (0.5 * STEP) * fh
+
     have = set()
     src = None
     for step, m in enumerate((3, 2, 1, 0)):
@@ -139,8 +142,9 @@
             if src is not None:
                 out = tendency(src, have, d, base, coef, slot_of(d), turn=turn)
             if d == 0:
-                out[0] = total([out[0], forces[m][0]])
-                out[2] = total([out[2], forces[m][1]])
+                fh, fn = force(m)
+                out[0] = total([out[0], fh])
+                out[2] = total([out[2], fn])
             for c, v in out.items():
                 if m == 0:
                     finish(d, c, v)
@@ -150,12 +154,12 @@
         have, src = new, bufs[step % 2]
 
 
-def rows_kernel(scal, x_ref, dep, cor, drag, s00, s01, s10, s11, b0, b1, coef, v0, v1, v2, v3, acc, top, bottom):
+def rows_kernel(x_ref, dep, cor, drag, s00, s01, s10, s11, e0, e1, b0, b1, coef, v0, v1, v2, v3, acc):
     rows, base = 8, 2
 
     @pl.when(pl.program_id(0) == 0)
     def _():
-        load_coefficients(dep, cor, drag, scal[0] - 2, rows + 4, coef)
+        load_coefficients(dep, cor, drag, lax.axis_index("row") * rows - 2, rows + 4, coef)
         for ref in (v0, v1, v2, v3):
             zero_gaps(ref, rows + 4)
 
@@ -164,19 +168,22 @@
             v0[pl.ds(at(r + base, c), GX), :] = x_ref[pl.ds((r * 3 + c) * GX, GX), :]
 
     def finish(r, c, v4):
-        place = r if r < 4 else 4 + (7 - r)
+        half, d = (0, r) if r < 4 else (1, 7 - r)
+        place = half * 4 + (d + 2) % 4
         i = at(r + base, c)
         v = v4 + v3[pl.ds(i, GX), :] + v2[pl.ds(i, GX), :] + v1[pl.ds(i, GX), :] + v0[pl.ds(i, GX), :]
         acc[pl.ds((place * 3 + c) * GX, GX), :] = v
 
     powers((v0, v1, v2, v3), rows, base, coef, finish)
-    for j, ref in enumerate((v0, v1, v2, v3)):
-        for i, c in enumerate((0, 2)):
-            top[pl.ds((j * 2 + i) * GX, GX), :] = ref[pl.ds(at(base, c), GX), :]
-            bottom[pl.ds((j * 2 + i) * GX, GX), :] = ref[pl.ds(at(rows - 1 + base, c), GX), :]
-
-    half, part = 768, 768 // CHUNKS
-    core = scal[1]
+
+    def put(e_ref, b_ref, row):
+        for j, ref in enumerate((v0, v1, v2, v3)):
+            for i, c in enumerate((0, 2)):
+                to = e_ref if j < 2 else b_ref
+                to[pl.ds((j % 2 * 2 + i) * GX, GX), :] = ref[pl.ds(at(row + base, c), GX), :]
+
+    half, part = 768, 384
+    core = lax.axis_index("col") % 2
 
     @pl.when(core == 0)
     def _():
@@ -184,8 +191,8 @@
         s01[...] = acc[pl.ds(part, part), :]
         s10[...] = acc[pl.ds(half, part), :]
         s11[...] = acc[pl.ds(half + part, part), :]
-        b0[...] = bottom[...]
-        b1[...] = top[...]
+        put(e0, b0, 7)
+        put(e1, b1, 0)
 
     @pl.when(core == 1)
     def _():
@@ -193,8 +200,8 @@
         s11[...] = acc[pl.ds(part, part), :]
         s00[...] = acc[pl.ds(half, part), :]
         s01[...] = acc[pl.ds(half + part, part), :]
-        b1[...] = bottom[...]
-        b0[...] = top[...]
+        put(e1, b1, 7)
+        put(e0, b0, 0)
 
 
 def whole(ref_shape):
@@ -217,26 +224,28 @@
     return pl.BlockSpec((rows, LANES), lambda i, *_: (0, i))
 
 
-def rows_step(scal, block, fields):
+def rows_step(block, fields):
     table = whole((GX, GX))
-    part = 768 // CHUNKS
     buf = vmem(buffer_rows(12))
     return pl.pallas_call(
         rows_kernel,
         grid_spec=pltpu.PrefetchScalarGridSpec(
-            num_scalar_prefetch=1,
+            num_scalar_prefetch=0,
             grid=(3,),
             in_specs=[lane_block(1536), table, table, table],
-            out_specs=[lane_block(part)] * 4 + [lane_block(512)] * 2,
-            scratch_shapes=[pltpu.VMEM((12, 4, GX, LANES), jnp.float32), buf, buf, buf, buf, vmem(1536), vmem(512), vmem(512)],
+            out_specs=[lane_block(384)] * 4 + [lane_block(256)] * 4,
+            scratch_shapes=[pltpu.VMEM((12, 4, GX, LANES), jnp.float32), buf, buf, buf, buf, vmem(1536)],
         ),
-        out_shape=[shape(part, 384)] * 4 + [shape(512, 384)] * 2,
-        compiler_params=params(24),
+        out_shape=[shape(384, 384)] * 4 + [shape(256, 384)] * 4,
+        compiler_params=params(58),
         name="rows_step",
-    )(scal, block, *fields)
-
-
-def rows_response_kernel(scal, m0, m1, dep, cor, drag, r0, r1, coef, t0, t1):
+    )(block, *fields)
+
+
+def rows_response_kernel(powers_in, scal, m0, m1, *refs):
+    late = powers_in[0] > 0
+    before, (dep, cor, drag), refs = refs[: 3 * late], refs[3 * late : 3 * late + 3], refs[3 * late + 3 :]
+    outs, (coef, t0, t1) = refs[:-3], refs[-3:]
     half = scal[1]
     turn = 1.0 - 2.0 * half.astype(jnp.float32)
 
@@ -246,38 +255,49 @@
         for ref in (t0, t1):
             zero_gaps(ref, 4)
 
-    for m_ref, r_ref in ((m0, r0), (m1, r1)):
+    for k, m_ref in enumerate((m0, m1)):
 
         def message(j, i, m_ref=m_ref):
-            v = m_ref[pl.ds((j * 2 + i) * GX, GX), :]
+            v = m_ref[pl.ds(((j % 2) * 2 + i) * GX, GX), :]
             return v * turn if i == 1 else v
 
-        def finish(d, c, v, r_ref=r_ref):
+        def finish(d, c, v, k=k):
+            if late and d > 1:
+                return
+            i = pl.ds((d % 2 * 3 + c) * GX, GX)
             v = jnp.zeros((GX, LANES), jnp.float32) if v is None else v
-            r_ref[pl.ds((d * 3 + c) * GX, GX), :] = v * turn if c == 2 else v
-
-        response(message, (t0, t1), 0, coef, lambda d: d, finish)
-
-
-def rows_response(scal, m0, m1, fields):
+            v = v * turn if c == 2 else v
+            if late:
+                outs[k][i, :] = before[k][i, :] + v
+            else:
+                outs[k + 2 * (d < 2)][i, :] = v
+
+        response(message, (t0, t1), 0, coef, lambda d: d, finish, powers_in=powers_in)
+
+
+def rows_response(scal, messages, fields, powers_in, before=(), after=()):
     table = whole((GX, GX))
     buf = vmem(buffer_rows(4))
+    count = 2 if before else 4
     return pl.pallas_call(
-        rows_response_kernel,
+        functools.partial(rows_response_kernel, powers_in),
         grid_spec=pltpu.PrefetchScalarGridSpec(
             num_scalar_prefetch=1,
             grid=(3,),
-            in_specs=[lane_block(512)] * 2 + [table] * 3,
-            out_specs=[lane_block(768)] * 2,
+            in_specs=[lane_block(256)] * 2
+            + [lane_block(384)] * len(before)
+            + [pl.BlockSpec(memory_space=pl.ANY)] * len(after)
+            + [table] * 3,
+            out_specs=[lane_block(384)] * count,
             scratch_shapes=[pltpu.VMEM((4, 4, GX, LANES), jnp.float32), buf, buf],
         ),
-        out_shape=[shape(768, 384)] * 2,
+        out_shape=[shape(384, 384)] * count,
         compiler_params=params(16),
         name="rows_response",
-    )(scal, m0, m1, *fields)
-
-
-def columns_kernel(scal, s0, s1, r0, r1, dep, cor, drag, out, left, right, coef, v0, v1, v2, v3):
+    )(scal, *messages, *before, *after, *fields)
+
+
+def columns_kernel(scal, s0, s1, r0, r1, dep, cor, drag, out, inner, outer, coef, v0, v1, v2, v3):
     rows, base = 4, 2
     half = scal[1]
 
@@ -303,13 +323,24 @@
         out[pl.ds((r * 3 + c) * GX, GX), :] = v
 
     powers((v0, v1, v2, v3), rows, base, coef, finish)
-    for j, ref in enumerate((v0, v1, v2, v3)):
-        for i, c in enumerate((0, 2)):
-            left[pl.ds((j * 2 + i) * GX, GX), :] = ref[pl.ds(at(base, c), GX), :]
-            right[pl.ds((j * 2 + i) * GX, GX), :] = ref[pl.ds(at(rows - 1 + base, c), GX), :]
-
-
-def columns_step(scal, s0, s1, r0, r1, fields, chunk):
+
+    def put(to, row):
+        for j, ref in enumerate((v0, v1, v2, v3)):
+            for i, c in enumerate((0, 2)):
+                to[pl.ds((j * 2 + i) * GX, GX), :] = ref[pl.ds(at(row + base, c), GX), :]
+
+    @pl.when(scal[2] == 0)
+    def _():
+        put(inner, rows - 1)
+        put(outer, 0)
+
+    @pl.when(scal[2] == 1)
+    def _():
+        put(inner, 0)
+        put(outer, rows - 1)
+
+
+def columns_step(scal, s0, s1, r0, r1, fields):
     table = whole((GX, GX))
     part = 768 // CHUNKS
     tiles = part // LANES
@@ -319,9 +350,7 @@
         grid_spec=pltpu.PrefetchScalarGridSpec(
             num_scalar_prefetch=1,
             grid=(tiles,),
-            in_specs=[pl.BlockSpec((LANES, 384), lambda i, *_: (i, 0))] * 2
-            + [pl.BlockSpec((LANES, 384), lambda i, *_: (i + chunk * tiles, 0))] * 2
-            + [table] * 3,
+            in_specs=[pl.BlockSpec((LANES, 384), lambda i, *_: (i, 0))] * 4 + [table] * 3,
             out_specs=[lane_block(768), lane_block(512), lane_block(512)],
             scratch_shapes=[pltpu.VMEM((8, 4, GX, LANES), jnp.float32), buf, buf, buf, buf],
         ),
@@ -331,7 +360,7 @@
     )(scal, s0, s1, r0, r1, *fields)
 
 
-def columns_response_kernel(scal, own, from_left, from_right, dep, cor, drag, z0, z1, coef, t0, t1, acc):
+def columns_response_kernel(scal, own, inner, outer, dep, cor, drag, z0, z1, coef, t0, t1, acc):
     half = scal[1]
 
     @pl.when(pl.program_id(0) == 0)
@@ -341,7 +370,8 @@
             zero_gaps(ref, 4)
 
     def message_left(j, i):
-        return from_left[pl.ds((j * 2 + i) * GX, GX), :]
+        place = pl.ds((j * 2 + i) * GX, GX)
+        return jnp.where(scal[2] == 0, outer[place, :], inner[place, :])
 
     def finish_left(d, c, v):
         i = pl.ds((d * 3 + c) * GX, GX)
@@ -350,7 +380,8 @@
     response(message_left, (t0, t1), 0, coef, lambda d: d, finish_left)
 
     def message_right(j, i):
-        v = from_right[pl.ds((j * 2 + i) * GX, GX), :]
+        place = pl.ds((j * 2 + i) * GX, GX)
+        v = jnp.where(scal[2] == 0, inner[place, :], outer[place, :])
         return -v if i == 1 else v
 
     def finish_right(d, c, v):
@@ -366,7 +397,7 @@
             z_ref[:, t * LANES : (t + 1) * LANES] = acc[pl.ds(place, LANES), :].T
 
 
-def columns_response(scal, own, from_left, from_right, fields):
+def columns_response(scal, own, inner, outer, fields):
     table = whole((GX, GX))
     part = 768 // CHUNKS
     buf = vmem(buffer_rows(4))
@@ -382,40 +413,38 @@
         out_shape=[shape(part, 384)] * 2,
         compiler_params=params(16),
         name="columns_response",
-    )(scal, own, from_left, from_right, *fields)
+    )(scal, own, inner, outer, *fields)
 
 
 def finish_kernel(scal, z0, z1, noise, *rest):
     out = rest[-1]
     k = pl.program_id(0)
-
-    @pl.when(k == 0)
-    def _():
-        out[...] = z0[...] + noise[...]
-
-    @pl.when(k == 1)
-    def _():
-        out[...] = z1[...] + noise[...]
-
-
-def finish_step(scal, z0, z1, noise, chunk, out=None):
-    per = 4 // CHUNKS
-
-    def place(k, i, scal):
-        d = chunk * per + i
+    half = jnp.where(k == 0, scal[1], 1 - scal[1])
+
+    def put(z, flip):
+        for d in range(2):
+            place = pl.ds((1 - d if flip else d) * 192, 192)
+            out[place, :] = z[pl.ds(d * 192, 192), :] + noise[place, :]
+
+    for i, z in enumerate((z0, z1)):
+        for flip in (False, True):
+            pl.when(jnp.logical_and(k == i, half == int(flip)))(functools.partial(put, z, flip))
+
+
+def finish_step(scal, z0, z1, noise, near, out=None):
+    def place(k, scal):
         half = jnp.where(k == 0, scal[1], 1 - scal[1])
-        return (jnp.where(half == 0, d, 7 - d), 0)
-
-    first = pl.BlockSpec((192, 384), lambda k, i, scal: (jnp.where(k == 0, i, per - 1), 0))
-    second = pl.BlockSpec((192, 384), lambda k, i, scal: (jnp.where(k == 1, i, 0), 0))
-    block = pl.BlockSpec((192, 384), place)
+        return (jnp.where(half == 0, 0, 3) if near else 1 + half, 0)
+
+    full = pl.BlockSpec((384, 384), lambda k, scal: (0, 0))
+    block = pl.BlockSpec((384, 384), place)
     extra = [] if out is None else [out]
     return pl.pallas_call(
         finish_kernel,
         grid_spec=pltpu.PrefetchScalarGridSpec(
             num_scalar_prefetch=1,
-            grid=(2, per),
-            in_specs=[first, second, block] + [pl.BlockSpec(memory_space=pl.ANY)] * len(extra),
+            grid=(2,),
+            in_specs=[full, full, block] + [pl.BlockSpec(memory_space=pl.ANY)] * len(extra),
             out_specs=block,
         ),
         out_shape=shape(1536, 384),
@@ -442,45 +471,45 @@
                         if core != k and r > 0:
                             boundary[k].append((me, joint(r - 1, z, 1, lo)))
                         back[k].append((me, joint(r, z, core, lo ^ k)))
-    rightward = []
-    for z in range(cols // 4):
+    inner = [(i, i ^ 1) for i in range(cols)]
+    outer = []
+    for z in range(cols // 4 - 1):
         for p in range(2):
-            rightward.append((z * 4 + p * 2, z * 4 + p * 2 + 1))
-            if z + 1 < cols // 4:
-                rightward.append((z * 4 + p * 2 + 1, (z + 1) * 4 + p * 2))
-    leftward = [(b, a) for a, b in rightward]
-    return split, boundary, back, rightward, leftward
+            a, b = z * 4 + p * 2 + 1, (z + 1) * 4 + p * 2
+            outer += [(a, b), (b, a)]
+    return split, boundary, back, inner, outer
 
 
 def shards(covariance, process_noise, depth_field, coriolis, drag_rate):
     fields = (depth_field, coriolis, drag_rate)
     rows, cols = lax.axis_size("row"), lax.axis_size("col")
-    split, boundary, back, rightward, leftward = permutations(rows, cols)
+    split, boundary, back, inner, outer = permutations(rows, cols)
     row, col = lax.axis_index("row"), lax.axis_index("col")
     z, second, core = col // 4, (col // 2) % 2, col % 2
     both = ("row", "col")
 
-    scal = jnp.stack([row * 8, core]).astype(jnp.int32)
-    s00, s01, s10, s11, b0, b1 = rows_step(scal, covariance, fields)
-    m0 = lax.ppermute(b0, both, boundary[0])
-    m1 = lax.ppermute(b1, both, boundary[1])
-    pieces = [
-        [lax.ppermute(s, both, split[k]) for k, s in enumerate(pair)] for pair in ((s00, s10), (s01, s11))
-    ]
+    def send(pair, pairs):
+        return [lax.ppermute(v, both, pairs[k]) for k, v in enumerate(pair)]
+
+    s00, s01, s10, s11, e0, e1, b0, b1 = rows_step(covariance, fields)
+    early = send((e0, e1), boundary)
+    far = send((s00, s10), split)
+    b0, b1, *early = lax.optimization_barrier((b0, b1, *early))
+    late = send((b0, b1), boundary)
+    near = send((s01, s11), split)
     rscal = jnp.stack([row * 8 + second * 4, second]).astype(jnp.int32)
-    r0, r1 = rows_response(rscal, m0, m1, fields)
-
-    cscal = jnp.stack([(z * 2 + core) * 4, second]).astype(jnp.int32)
+    cscal = jnp.stack([(z * 2 + core) * 4, second, core]).astype(jnp.int32)
+    fscal = jnp.stack([row, core]).astype(jnp.int32)
+    r02, r12, r00, r10 = rows_response(rscal, early, fields, (0, 1))
     result = None
-    fscal = jnp.stack([row, core]).astype(jnp.int32)
-    for chunk, (s0, s1) in enumerate(pieces):
-        own, left, right = columns_step(cscal, s0, s1, r0, r1, fields, chunk)
-        from_left = lax.ppermute(right, "col", rightward)
-        from_right = lax.ppermute(left, "col", leftward)
-        z0, z1 = columns_response(cscal, own, from_left, from_right, fields)
-        z0 = lax.ppermute(z0, both, back[0])
-        z1 = lax.ppermute(z1, both, back[1])
-        result = finish_step(fscal, z0, z1, process_noise, chunk, result)
+    for chunk, halves, moved in ((0, far, (r02, r12)), (1, near, None)):
+        if chunk == 1:
+            moved = rows_response(rscal, late, fields, (2, 3), (r00, r10), (own,))
+        own, inside, outside = columns_step(cscal, *halves, *moved, fields)
+        outside = lax.ppermute(outside, "col", outer)
+        inside = lax.ppermute(inside, "col", inner)
+        ready = send(columns_response(cscal, own, inside, outside, fields), back)
+        result = finish_step(fscal, *ready, process_noise, chunk == 1, result)
     return result
 
 

time: 115 us -> 108 us (0.939)
  the two profiles are of different devices: /device:TPU:100 before, /device:TPU:120 now
where the time goes in v2:
time: 108 us; the launch traced here: 107 us
  starting transfers between devices  41.9 us (39%)
  waiting for transfers between devices  35.6 us (33%)
  Pallas kernels  29.2 us (27%)
    ppermute x12, starting transfers between devices, send(): return [lax.ppermute(v, both, pairs[k]) for k, v in enumerate(pair)]  34.5 us
    ppermute x12, waiting for transfers between devices, send(): return [lax.ppermute(v, both, pairs[k]) for k, v in enumerate(pair)]  30.6 us
    pallas_call x2, Pallas kernels, columns_step(): pl.pallas_call(columns_kernel, grid_spec=pltpu.PrefetchScalarGridSpec(num...  7.3 us
    pallas_call x1, Pallas kernels, rows_step(): pl.pallas_call(rows_kernel, grid_spec=pltpu.PrefetchScalarGridSpec(num_sc...  6.98 us
    pallas_call x2, Pallas kernels, columns_response(): pl.pallas_call(columns_response_kernel, grid_spec=pltpu.PrefetchScalarGri...  6.1 us
    pallas_call x2, Pallas kernels, rows_response(): pl.pallas_call(functools.partial(rows_response_kernel, powers_in), grid_s...  5.45 us
    ppermute x2, waiting for transfers between devices, shards(): outside = lax.ppermute(outside, 'col', outer)  4.98 us
    ppermute x2, starting transfers between devices, shards(): outside = lax.ppermute(outside, 'col', outer)  3.95 us
  transfers between devices with their start and end apart: 16, of which 6 were waited for; matrix products, arithmetic and copies ran while one was open for 0% of the time, Pallas kernels for 19%

profile of v2, /device:TPU:120, one launch (start us, length us, event | category | flops | bytes accessed | tf_op | source)
XLA Modules:
  0.0 107.1 jit_solution(3613654839044082839)
XLA Ops:
  0.0 7.0 %rows_step.1 = (f32[384,384]{1,0:T(8,128)}, f32[384,384]{1,0:T(8,128)}, f32[384,384]{1,0:T(8,128)}, f32[384,384]{1,0:T(8,128)}, f32[256,384]{1,0:T(8,128)}, /*in...) custom-call(f32[1536,384]{1,0:T(8,128)} %x_ref.1, f32[64,64]{1,0:T(8,128)} %dep.9, f32[64,64]{1,0:T(8,128)} %cor.9, ...), custom_call_target="tpu_custom_call" | custom-call | tf_op jit(solution)/shard_map/rows_step/pallas_call | solution.py:230
  7.0 1.7 %collective-permute-start.6 = (f32[384,384]{1,0:T(8,128)}, f32[384,384]{1,0:T(8,128)S(1)}, u32[]{:S(2)}, u32[]{:S(2)}) collective-permute-start(f32[384,384]{1,0:T(8,128)} %get-tuple-element.45), channel_id=1, source_target_pairs={{0,0},{1,2},{2,1},{3,3},{4,4},{5,6},{6,5},{7,7},{8,8},{9,10},{10,9... | collective-permute-start | bytes 1769480 | tf_op jit(solution)/shard_map/ppermute | solution.py:492
  8.7 4.9 %collective-permute-start.2 = (f32[256,384]{1,0:T(8,128)}, f32[256,384]{1,0:T(8,128)S(1)}, u32[]{:S(2)}, u32[]{:S(2)}) collective-permute-start(f32[256,384]{1,0:T(8,128)} %get-tuple-element.37), channel_id=1, source_target_pairs={{0,32},{2,33},{4,36},{6,37},{8,40},{10,41},{12,44},{14,45},{16,48}... | collective-permute-start | bytes 1179656 | tf_op jit(solution)/shard_map/ppermute | solution.py:492
  13.6 4.4 %collective-permute-start.3 = (f32[256,384]{1,0:T(8,128)}, f32[256,384]{1,0:T(8,128)S(1)}, u32[]{:S(2)}, u32[]{:S(2)}) collective-permute-start(f32[256,384]{1,0:T(8,128)} %get-tuple-element.38), channel_id=1, source_target_pairs={{1,32},{3,33},{5,36},{7,37},{9,40},{11,41},{13,44},{15,45},{17,48}... | collective-permute-start | bytes 1179656 | tf_op jit(solution)/shard_map/ppermute | solution.py:492
  18.2 1.7 %collective-permute-start = (f32[384,384]{1,0:T(8,128)}, f32[384,384]{1,0:T(8,128)S(1)}, u32[]{:S(2)}, u32[]{:S(2)}) collective-permute-start(f32[384,384]{1,0:T(8,128)} %get-tuple-element.33), channel_id=1, source_target_pairs={{0,0},{1,2},{2,1},{3,3},{4,4},{5,6},{6,5},{7,7},{8,8},{9,10},{10,9... | collective-permute-start | bytes 1769480 | tf_op jit(solution)/shard_map/ppermute | solution.py:492
  19.9 5.5 %collective-permute-done.2.m0 = f32[256,384]{1,0:T(8,128)S(1)} collective-permute-done((f32[256,384]{1,0:T(8,128)}, f32[256,384]{1,0:T(8,128)S(1)}, u32[]{:S(2)}, u32[]{:S(2)}) %collective-permute-start.2) | collective-permute-done | bytes 393248 | tf_op jit(solution)/shard_map/ppermute | solution.py:492
  25.4 6.6 %collective-permute-start.1 = (f32[384,384]{1,0:T(8,128)}, f32[384,384]{1,0:T(8,128)S(1)}, u32[]{:S(2)}, u32[]{:S(2)}) collective-permute-start(f32[384,384]{1,0:T(8,128)} %get-tuple-element.34), channel_id=1, source_target_pairs={{0,2},{1,0},{2,3},{3,1},{4,6},{5,4},{6,7},{7,5},{8,10},{9,8},{10,1... | collective-permute-start | bytes 1769480 | tf_op jit(solution)/shard_map/ppermute | solution.py:492
  33.1 1.9 %collective-permute-start.4 = (f32[256,384]{1,0:T(8,128)}, f32[256,384]{1,0:T(8,128)}, u32[]{:S(2)}, u32[]{:S(2)}) collective-permute-start(f32[256,384]{1,0:T(8,128)} %get-tuple-element.39), channel_id=1, source_target_pairs={{0,32},{2,33},{4,36},{6,37},{8,40},{10,41},{12,44},{14,45},{16,48}... | collective-permute-start | bytes 1179656 | tf_op jit(solution)/shard_map/ppermute | solution.py:492
  35.1 6.5 %collective-permute-start.5 = (f32[256,384]{1,0:T(8,128)}, f32[256,384]{1,0:T(8,128)}, u32[]{:S(2)}, u32[]{:S(2)}) collective-permute-start(f32[256,384]{1,0:T(8,128)} %get-tuple-element.40), channel_id=1, source_target_pairs={{1,32},{3,33},{5,36},{7,37},{9,40},{11,41},{13,44},{15,45},{17,48}... | collective-permute-start | bytes 1179656 | tf_op jit(solution)/shard_map/ppermute | solution.py:492
  41.8 2.3 %rows_response.2 = (f32[384,384]{1,0:T(8,128)S(1)}, f32[384,384]{1,0:T(8,128)S(1)}, f32[384,384]{1,0:T(8,128)S(1)}, f32[384,384]{1,0:T(8,128)S(1)}) custom-call(s32[2]{0:T(128)S(1)} %pad_add_fusion.2.scal, f32[256,384]{1,0:T(8,128)S(1)} %collective-permute-done.2.m0, f32[256,384]{1,0:T(8,128)S(1)} %collective-permute-done.3.m1, f32[64,64]{1,0:T(8,128)S(1)} %copy-done.1, ...), custom_call_target="tpu_custom_call" | custom-call | tf_op jit(solution)/shard_map/rows_response/pallas_call | solution.py:282
  44.1 3.6 %columns_step.2 = (f32[768,384]{1,0:T(8,128)S(1)}, f32[512,384]{1,0:T(8,128)S(1)}, f32[512,384]{1,0:T(8,128)S(1)}) custom-call(s32[3]{0:T(128)S(1)} %pad_add_fusion.1.scal, f32[384,384]{1,0:T(8,128)S(1)} %collective-permute-done.6.s0, f32[384,384]{1,0:T(8,128)S(1)} %collective-permute-done.7.s1, f32[384,384]{1,0:T(8,128)S(1)} %get-tuple-element.47.r0, ...), custom_call_target="tpu_custom_call" | custom-call | tf_op jit(solution)/shard_map/columns_step/pallas_call | solution.py:348
  47.9 8.9 %collective-permute-done.4.m0 = f32[256,384]{1,0:T(8,128)} collective-permute-done((f32[256,384]{1,0:T(8,128)}, f32[256,384]{1,0:T(8,128)}, u32[]{:S(2)}, u32[]{:S(2)}) %collective-permute-start.4) | collective-permute-done | bytes 393248 | tf_op jit(solution)/shard_map/ppermute | solution.py:492
  56.8 1.9 %collective-permute-start.13 = (f32[512,384]{1,0:T(8,128)S(1)}, f32[512,384]{1,0:T(8,128)S(1)}, u32[]{:S(2)}, u32[]{:S(2)}) collective-permute-start(f32[512,384]{1,0:T(8,128)S(1)} %get-tuple-element.58), channel_id=1, source_target_pairs={{1,4},{4,1},{3,6},{6,3},{5,8},{8,5},{7,10},{10,7},{9,12},{12,9},{1... | collective-permute-start | bytes 2359304 | tf_op jit(solution)/shard_map/ppermute | solution.py:509
  58.7 3.2 %rows_response.3 = (f32[384,384]{1,0:T(8,128)S(1)}, f32[384,384]{1,0:T(8,128)S(1)}) custom-call(s32[2]{0:T(128)S(1)} %pad_add_fusion.2.scal, f32[256,384]{1,0:T(8,128)} %collective-permute-done.4.m0, f32[256,384]{1,0:T(8,128)} %collective-permute-done.5.m1, f32[384,384]{1,0:T(8,128)S(1)} %get-tuple-element.43.refs_0_, ...), custom_call_target="tpu_custom_call" | custom-call | tf_op jit(solution)/shard_map/rows_response/pallas_call | solution.py:282
  61.9 3.6 %columns_step.3 = (f32[768,384]{1,0:T(8,128)S(1)}, f32[512,384]{1,0:T(8,128)S(1)}, f32[512,384]{1,0:T(8,128)S(1)}) custom-call(s32[3]{0:T(128)S(1)} %pad_add_fusion.1.scal, f32[384,384]{1,0:T(8,128)S(1)} %collective-permute-done.s0, f32[384,384]{1,0:T(8,128)S(1)} %collective-permute-done.1.s1, f32[384,384]{1,0:T(8,128)S(1)} %get-tuple-element.50.r0, ...), custom_call_target="tpu_custom_call" | custom-call | tf_op jit(solution)/shard_map/columns_step/pallas_call | solution.py:348
  65.6 3.3 %collective-permute-start.8 = (f32[512,384]{1,0:T(8,128)S(1)}, f32[512,384]{1,0:T(8,128)S(1)}, u32[]{:S(2)}, u32[]{:S(2)}) collective-permute-start(f32[512,384]{1,0:T(8,128)S(1)} %get-tuple-element.53), channel_id=1, source_target_pairs={{0,1},{1,0},{2,3},{3,2},{4,5},{5,4},{6,7},{7,6},{8,9},{9,8},{10,11... | collective-permute-start | bytes 2359304 | tf_op jit(solution)/shard_map/ppermute | solution.py:510
  68.9 2.0 %collective-permute-start.9 = (f32[512,384]{1,0:T(8,128)S(1)}, f32[512,384]{1,0:T(8,128)S(1)}, u32[]{:S(2)}, u32[]{:S(2)}) collective-permute-start(f32[512,384]{1,0:T(8,128)S(1)} %get-tuple-element.54), channel_id=1, source_target_pairs={{1,4},{4,1},{3,6},{6,3},{5,8},{8,5},{7,10},{10,7},{9,12},{12,9},{1... | collective-permute-start | bytes 2359304 | tf_op jit(solution)/shard_map/ppermute | solution.py:509
  70.9 3.1 %columns_response.3 = (f32[384,384]{1,0:T(8,128)S(1)}, f32[384,384]{1,0:T(8,128)S(1)}) custom-call(s32[3]{0:T(128)S(1)} %pad_add_fusion.1.scal, f32[768,384]{1,0:T(8,128)S(1)} %get-tuple-element.49.refs_2_.own, f32[512,384]{1,0:T(8,128)S(1)} %collective-permute-done.12.inner, f32[512,384]{1,0:T(8,128)S(1)} %collective-permute-done.13.outer, ...), custom_call_target="tpu_custom_call" | custom-call | tf_op jit(solution)/shard_map/columns_response/pallas_call | solution.py:404
  74.7 2.6 %collective-permute-start.15 = (f32[384,384]{1,0:T(8,128)S(1)}, f32[384,384]{1,0:T(8,128)S(1)}, u32[]{:S(2)}, u32[]{:S(2)}) collective-permute-start(f32[384,384]{1,0:T(8,128)S(1)} %get-tuple-element.60), channel_id=1, source_target_pairs={{0,1},{1,3},{2,0},{3,2},{4,5},{5,7},{6,4},{7,6},{8,9},{9,11},{10,8... | collective-permute-start | bytes 1769480 | tf_op jit(solution)/shard_map/ppermute | solution.py:492
  77.3 5.0 %collective-permute-done.9.outer = f32[512,384]{1,0:T(8,128)S(1)} collective-permute-done((f32[512,384]{1,0:T(8,128)S(1)}, f32[512,384]{1,0:T(8,128)S(1)}, u32[]{:S(2)}, u32[]{:S(2)}) %collective-permute-start.9) | collective-permute-done | bytes 786464 | tf_op jit(solution)/shard_map/ppermute | solution.py:509
  82.3 3.0 %columns_response.2 = (f32[384,384]{1,0:T(8,128)S(1)}, f32[384,384]{1,0:T(8,128)S(1)}) custom-call(s32[3]{0:T(128)S(1)} %pad_add_fusion.1.scal, f32[768,384]{1,0:T(8,128)S(1)} %get-tuple-element.52.own, f32[512,384]{1,0:T(8,128)S(1)} %collective-permute-done.8.inner, f32[512,384]{1,0:T(8,128)S(1)} %collective-permute-done.9.outer, f32[64,64]{1,0:T(8,128)S(1)} %copy-done.1, ...), custom_call_target="tpu_custom_call" | custom-call | tf_op jit(solution)/shard_map/columns_response/pallas_call | solution.py:404
  86.1 2.6 %collective-permute-start.11 = (f32[384,384]{1,0:T(8,128)S(1)}, f32[384,384]{1,0:T(8,128)S(1)}, u32[]{:S(2)}, u32[]{:S(2)}) collective-permute-start(f32[384,384]{1,0:T(8,128)S(1)} %get-tuple-element.56), channel_id=1, source_target_pairs={{0,1},{1,3},{2,0},{3,2},{4,5},{5,7},{6,4},{7,6},{8,9},{9,11},{10,8... | collective-permute-start | bytes 1769480 | tf_op jit(solution)/shard_map/ppermute | solution.py:492
  88.7 4.1 %collective-permute-done.15.z1 = f32[384,384]{1,0:T(8,128)S(1)} collective-permute-done((f32[384,384]{1,0:T(8,128)S(1)}, f32[384,384]{1,0:T(8,128)S(1)}, u32[]{:S(2)}, u32[]{:S(2)}) %collective-permute-start.15) | collective-permute-done | bytes 589856 | tf_op jit(solution)/shard_map/ppermute | solution.py:492
  94.5 11.0 %collective-permute-done.11.z1 = f32[384,384]{1,0:T(8,128)S(1)} collective-permute-done((f32[384,384]{1,0:T(8,128)S(1)}, f32[384,384]{1,0:T(8,128)S(1)}, u32[]{:S(2)}, u32[]{:S(2)}) %collective-permute-start.11) | collective-permute-done | bytes 589856 | tf_op jit(solution)/shard_map/ppermute | solution.py:492
  (28 shorter events, 6.3 us)
Async XLA Ops:
  0.0 41.8 %copy-start.3 = (f32[64,64]{1,0:T(8,128)S(1)}, f32[64,64]{1,0:T(8,128)}, u32[]{:S(2)}) copy-start(f32[64,64]{1,0:T(8,128)} %drag.9) | copy-start | bytes 49156
  0.0 41.8 %copy-start.2 = (f32[64,64]{1,0:T(8,128)S(1)}, f32[64,64]{1,0:T(8,128)}, u32[]{:S(2)}) copy-start(f32[64,64]{1,0:T(8,128)} %cor.9) | copy-start | bytes 49156
  0.0 41.8 %copy-start.1 = (f32[64,64]{1,0:T(8,128)S(1)}, f32[64,64]{1,0:T(8,128)}, u32[]{:S(2)}) copy-start(f32[64,64]{1,0:T(8,128)} %dep.9) | copy-start | bytes 49156
  7.0 28.1 %collective-permute-start.6 = (f32[384,384]{1,0:T(8,128)}, f32[384,384]{1,0:T(8,128)S(1)}, u32[]{:S(2)}, u32[]{:S(2)}) collective-permute-start(f32[384,384]{1,0:T(8,128)} %get-tuple-element.45), channel_id=1, source_target_pairs={{0,0},{1,2},{2,1},{3,3},{4,4},{5,6},{6,5},{7,7},{8,8},{9,10},{10,9... | collective-permute-start | bytes 1769480 | tf_op jit(solution)/shard_map/ppermute | solution.py:492
  8.7 16.7 %collective-permute-start.2 = (f32[256,384]{1,0:T(8,128)}, f32[256,384]{1,0:T(8,128)S(1)}, u32[]{:S(2)}, u32[]{:S(2)}) collective-permute-start(f32[256,384]{1,0:T(8,128)} %get-tuple-element.37), channel_id=1, source_target_pairs={{0,32},{2,33},{4,36},{6,37},{8,40},{10,41},{12,44},{14,45},{16,48}... | collective-permute-start | bytes 1179656 | tf_op jit(solution)/shard_map/ppermute | solution.py:492
  13.6 19.5 %collective-permute-start.3 = (f32[256,384]{1,0:T(8,128)}, f32[256,384]{1,0:T(8,128)S(1)}, u32[]{:S(2)}, u32[]{:S(2)}) collective-permute-start(f32[256,384]{1,0:T(8,128)} %get-tuple-element.38), channel_id=1, source_target_pairs={{1,32},{3,33},{5,36},{7,37},{9,40},{11,41},{13,44},{15,45},{17,48}... | collective-permute-start | bytes 1179656 | tf_op jit(solution)/shard_map/ppermute | solution.py:492
  18.1 26.0 %collective-permute-start.7 = (f32[384,384]{1,0:T(8,128)}, f32[384,384]{1,0:T(8,128)S(1)}, u32[]{:S(2)}, u32[]{:S(2)}) collective-permute-start(f32[384,384]{1,0:T(8,128)} %get-tuple-element.46), channel_id=1, source_target_pairs={{0,2},{1,0},{2,3},{3,1},{4,6},{5,4},{6,7},{7,5},{8,10},{9,8},{10,1... | collective-permute-start | bytes 1769480 | tf_op jit(solution)/shard_map/ppermute | solution.py:492
  18.2 43.7 %collective-permute-start = (f32[384,384]{1,0:T(8,128)}, f32[384,384]{1,0:T(8,128)S(1)}, u32[]{:S(2)}, u32[]{:S(2)}) collective-permute-start(f32[384,384]{1,0:T(8,128)} %get-tuple-element.33), channel_id=1, source_target_pairs={{0,0},{1,2},{2,1},{3,3},{4,4},{5,6},{6,5},{7,7},{8,8},{9,10},{10,9... | collective-permute-start | bytes 1769480 | tf_op jit(solution)/shard_map/ppermute | solution.py:492
  25.4 36.5 %collective-permute-start.1 = (f32[384,384]{1,0:T(8,128)}, f32[384,384]{1,0:T(8,128)S(1)}, u32[]{:S(2)}, u32[]{:S(2)}) collective-permute-start(f32[384,384]{1,0:T(8,128)} %get-tuple-element.34), channel_id=1, source_target_pairs={{0,2},{1,0},{2,3},{3,1},{4,6},{5,4},{6,7},{7,5},{8,10},{9,8},{10,1... | collective-permute-start | bytes 1769480 | tf_op jit(solution)/shard_map/ppermute | solution.py:492
  33.1 23.7 %collective-permute-start.4 = (f32[256,384]{1,0:T(8,128)}, f32[256,384]{1,0:T(8,128)}, u32[]{:S(2)}, u32[]{:S(2)}) collective-permute-start(f32[256,384]{1,0:T(8,128)} %get-tuple-element.39), channel_id=1, source_target_pairs={{0,32},{2,33},{4,36},{6,37},{8,40},{10,41},{12,44},{14,45},{16,48}... | collective-permute-start | bytes 1179656 | tf_op jit(solution)/shard_map/ppermute | solution.py:492
  35.1 23.6 %collective-permute-start.5 = (f32[256,384]{1,0:T(8,128)}, f32[256,384]{1,0:T(8,128)}, u32[]{:S(2)}, u32[]{:S(2)}) collective-permute-start(f32[256,384]{1,0:T(8,128)} %get-tuple-element.40), channel_id=1, source_target_pairs={{1,32},{3,33},{5,36},{7,37},{9,40},{11,41},{13,44},{15,45},{17,48}... | collective-permute-start | bytes 1179656 | tf_op jit(solution)/shard_map/ppermute | solution.py:492
  47.8 23.1 %collective-permute-start.12 = (f32[512,384]{1,0:T(8,128)S(1)}, f32[512,384]{1,0:T(8,128)S(1)}, u32[]{:S(2)}, u32[]{:S(2)}) collective-permute-start(f32[512,384]{1,0:T(8,128)S(1)} %get-tuple-element.57), channel_id=1, source_target_pairs={{0,1},{1,0},{2,3},{3,2},{4,5},{5,4},{6,7},{7,6},{8,9},{9,8},{10,11... | collective-permute-start | bytes 2359304 | tf_op jit(solution)/shard_map/ppermute | solution.py:510
  56.8 14.1 %collective-permute-start.13 = (f32[512,384]{1,0:T(8,128)S(1)}, f32[512,384]{1,0:T(8,128)S(1)}, u32[]{:S(2)}, u32[]{:S(2)}) collective-permute-start(f32[512,384]{1,0:T(8,128)S(1)} %get-tuple-element.58), channel_id=1, source_target_pairs={{1,4},{4,1},{3,6},{6,3},{5,8},{8,5},{7,10},{10,7},{9,12},{12,9},{1... | collective-permute-start | bytes 2359304 | tf_op jit(solution)/shard_map/ppermute | solution.py:509
  65.6 11.8 %collective-permute-start.8 = (f32[512,384]{1,0:T(8,128)S(1)}, f32[512,384]{1,0:T(8,128)S(1)}, u32[]{:S(2)}, u32[]{:S(2)}) collective-permute-start(f32[512,384]{1,0:T(8,128)S(1)} %get-tuple-element.53), channel_id=1, source_target_pairs={{0,1},{1,0},{2,3},{3,2},{4,5},{5,4},{6,7},{7,6},{8,9},{9,8},{10,11... | collective-permute-start | bytes 2359304 | tf_op jit(solution)/shard_map/ppermute | solution.py:510
  68.9 24.0 %copy-start = (f32[1536,384]{1,0:T(8,128)S(1)}, f32[1536,384]{1,0:T(8,128)}, u32[]{:S(2)}) copy-start(f32[1536,384]{1,0:T(8,128)} %noise.3) | copy-start | bytes 7077892
  68.9 13.4 %collective-permute-start.9 = (f32[512,384]{1,0:T(8,128)S(1)}, f32[512,384]{1,0:T(8,128)S(1)}, u32[]{:S(2)}, u32[]{:S(2)}) collective-permute-start(f32[512,384]{1,0:T(8,128)S(1)} %get-tuple-element.54), channel_id=1, source_target_pairs={{1,4},{4,1},{3,6},{6,3},{5,8},{8,5},{7,10},{10,7},{9,12},{12,9},{1... | collective-permute-start | bytes 2359304 | tf_op jit(solution)/shard_map/ppermute | solution.py:509
  74.0 14.7 %collective-permute-start.14 = (f32[384,384]{1,0:T(8,128)S(1)}, f32[384,384]{1,0:T(8,128)S(1)}, u32[]{:S(2)}, u32[]{:S(2)}) collective-permute-start(f32[384,384]{1,0:T(8,128)S(1)} %get-tuple-element.59), channel_id=1, source_target_pairs={{0,0},{1,2},{2,1},{3,3},{4,4},{5,6},{6,5},{7,7},{8,8},{9,10},{10,9... | collective-permute-start | bytes 1769480 | tf_op jit(solution)/shard_map/ppermute | solution.py:492
  74.7 18.1 %collective-permute-start.15 = (f32[384,384]{1,0:T(8,128)S(1)}, f32[384,384]{1,0:T(8,128)S(1)}, u32[]{:S(2)}, u32[]{:S(2)}) collective-permute-start(f32[384,384]{1,0:T(8,128)S(1)} %get-tuple-element.60), channel_id=1, source_target_pairs={{0,1},{1,3},{2,0},{3,2},{4,5},{5,7},{6,4},{7,6},{8,9},{9,11},{10,8... | collective-permute-start | bytes 1769480 | tf_op jit(solution)/shard_map/ppermute | solution.py:492
  85.3 9.1 %collective-permute-start.10 = (f32[384,384]{1,0:T(8,128)S(1)}, f32[384,384]{1,0:T(8,128)S(1)}, u32[]{:S(2)}, u32[]{:S(2)}) collective-permute-start(f32[384,384]{1,0:T(8,128)S(1)} %get-tuple-element.55), channel_id=1, source_target_pairs={{0,0},{1,2},{2,1},{3,3},{4,4},{5,6},{6,5},{7,7},{8,8},{9,10},{10,9... | collective-permute-start | bytes 1769480 | tf_op jit(solution)/shard_map/ppermute | solution.py:492
  86.1 19.4 %collective-permute-start.11 = (f32[384,384]{1,0:T(8,128)S(1)}, f32[384,384]{1,0:T(8,128)S(1)}, u32[]{:S(2)}, u32[]{:S(2)}) collective-permute-start(f32[384,384]{1,0:T(8,128)S(1)} %get-tuple-element.56), channel_id=1, source_target_pairs={{0,1},{1,3},{2,0},{3,2},{4,5},{5,7},{6,4},{7,6},{8,9},{9,11},{10,8... | collective-permute-start | bytes 1769480 | tf_op jit(solution)/shard_map/ppermute | solution.py:492

commit v3 on v2

--- a/solution.py
+++ b/solution.py
@@ -154,7 +154,67 @@
         have, src = new, bufs[step % 2]
 
 
-def rows_kernel(x_ref, dep, cor, drag, s00, s01, s10, s11, e0, e1, b0, b1, coef, v0, v1, v2, v3, acc):
+EDGE_ROWS = (0, 1, 2, 5, 6, 7)
+
+
+def edge_kernel(*refs):
+    rows, (dep, cor, drag, e0, e1, coef, u0, u1) = refs[:6], refs[6:]
+    base = 1
+    load_coefficients(dep, cor, drag, lax.axis_index("row") * 8 - base, 10, coef, only=(0, 1, 2, 7, 8, 9))
+    for ref in (u0, u1):
+        zero_gaps(ref, 10)
+    core = lax.axis_index("col") % 2
+    have = {(r, c) for r in EDGE_ROWS for c in range(3)}
+
+    @pl.loop(0, 3)
+    def _(tile):
+        lanes = pl.ds(pl.multiple_of(tile * LANES, LANES), LANES)
+        for r, ref in zip(EDGE_ROWS, rows):
+            for c in range(3):
+                u0[pl.ds(at(r + base, c), GX), :] = ref[pl.ds(c * GX, GX), lanes]
+        new = set()
+        for r in (-1, 0, 1, 6, 7, 8):
+            out = tendency(u0, have, r, base, coef, r + base, ghost=r in (-1, 8))
+            for c, v in out.items():
+                if v is not None:
+                    u1[pl.ds(at(r + base, c), GX), :] = v
+                    new.add((r, c))
+
+        def put(to, row):
+            out = tendency(u1, new, row, base, coef, row + base, want=(0, 2))
+            for i, c in enumerate((0, 2)):
+                place = pl.multiple_of(tile * 384 + i * GX, GX)
+                to[pl.ds(place, GX), :] = u0[pl.ds(at(row + base, c), GX), :]
+                to[pl.ds(place + 2 * GX, GX), :] = u1[pl.ds(at(row + base, c), GX), :]
+                to[pl.ds(place + 4 * GX, GX), :] = out[c] * 0.5
+
+        @pl.when(core == 0)
+        def _():
+            put(e0, 7)
+            put(e1, 0)
+
+        @pl.when(core == 1)
+        def _():
+            put(e1, 7)
+            put(e0, 0)
+
+
+def edge_step(block, fields):
+    table = whole((GX, GX))
+    buf = vmem(buffer_rows(10))
+    return pl.pallas_call(
+        edge_kernel,
+        grid=(1,),
+        in_specs=[pl.BlockSpec((192, 384), lambda i, r=r: (r, 0)) for r in EDGE_ROWS] + [table] * 3,
+        out_specs=[whole((1152, LANES))] * 2,
+        scratch_shapes=[pltpu.VMEM((10, 4, GX, LANES), jnp.float32), buf, buf],
+        out_shape=[shape(1152, LANES)] * 2,
+        compiler_params=params(58),
+        name="edge_step",
+    )(*[block] * 6, *fields)
+
+
+def rows_kernel(x_ref, after, dep, cor, drag, s00, s01, s10, s11, b0, b1, coef, v0, v1, v2, v3, acc):
     rows, base = 8, 2
 
     @pl.when(pl.program_id(0) == 0)
@@ -176,11 +236,9 @@
 
     powers((v0, v1, v2, v3), rows, base, coef, finish)
 
-    def put(e_ref, b_ref, row):
-        for j, ref in enumerate((v0, v1, v2, v3)):
-            for i, c in enumerate((0, 2)):
-                to = e_ref if j < 2 else b_ref
-                to[pl.ds((j % 2 * 2 + i) * GX, GX), :] = ref[pl.ds(at(row + base, c), GX), :]
+    def put(to, row):
+        for i, c in enumerate((0, 2)):
+            to[pl.ds(i * GX, GX), :] = v3[pl.ds(at(row + base, c), GX), :]
 
     half, part = 768, 384
     core = lax.axis_index("col") % 2
@@ -191,8 +249,8 @@
         s01[...] = acc[pl.ds(part, part), :]
         s10[...] = acc[pl.ds(half, part), :]
         s11[...] = acc[pl.ds(half + part, part), :]
-        put(e0, b0, 7)
-        put(e1, b1, 0)
+        put(b0, 7)
+        put(b1, 0)
 
     @pl.when(core == 1)
     def _():
@@ -200,8 +258,8 @@
         s11[...] = acc[pl.ds(part, part), :]
         s00[...] = acc[pl.ds(half, part), :]
         s01[...] = acc[pl.ds(half + part, part), :]
-        put(e1, b1, 7)
-        put(e0, b0, 0)
+        put(b1, 7)
+        put(b0, 0)
 
 
 def whole(ref_shape):
@@ -224,7 +282,11 @@
     return pl.BlockSpec((rows, LANES), lambda i, *_: (0, i))
 
 
-def rows_step(block, fields):
+def stacked(rows):
+    return pl.BlockSpec((rows, LANES), lambda i, *_: (i, 0))
+
+
+def rows_step(block, after, fields):
     table = whole((GX, GX))
     buf = vmem(buffer_rows(12))
     return pl.pallas_call(
@@ -232,19 +294,17 @@
         grid_spec=pltpu.PrefetchScalarGridSpec(
             num_scalar_prefetch=0,
             grid=(3,),
-            in_specs=[lane_block(1536), table, table, table],
-            out_specs=[lane_block(384)] * 4 + [lane_block(256)] * 4,
+            in_specs=[lane_block(1536), pl.BlockSpec(memory_space=pl.ANY), table, table, table],
+            out_specs=[lane_block(384)] * 4 + [lane_block(128)] * 2,
             scratch_shapes=[pltpu.VMEM((12, 4, GX, LANES), jnp.float32), buf, buf, buf, buf, vmem(1536)],
         ),
-        out_shape=[shape(384, 384)] * 4 + [shape(256, 384)] * 4,
+        out_shape=[shape(384, 384)] * 4 + [shape(128, 384)] * 2,
         compiler_params=params(58),
         name="rows_step",
-    )(block, *fields)
-
-
-def rows_response_kernel(powers_in, scal, m0, m1, *refs):
-    late = powers_in[0] > 0
-    before, (dep, cor, drag), refs = refs[: 3 * late], refs[3 * late : 3 * late + 3], refs[3 * late + 3 :]
+    )(block, after, *fields)
+
+
+def rows_response_kernel(scal, m0, m1, dep, cor, drag, *refs):
     outs, (coef, t0, t1) = refs[:-3], refs[-3:]
     half = scal[1]
     turn = 1.0 - 2.0 * half.astype(jnp.float32)
@@ -258,46 +318,36 @@
     for k, m_ref in enumerate((m0, m1)):
 
         def message(j, i, m_ref=m_ref):
-            v = m_ref[pl.ds(((j % 2) * 2 + i) * GX, GX), :]
+            v = m_ref[pl.ds((j * 2 + i) * GX, GX), :]
             return v * turn if i == 1 else v
 
         def finish(d, c, v, k=k):
-            if late and d > 1:
-                return
-            i = pl.ds((d % 2 * 3 + c) * GX, GX)
             v = jnp.zeros((GX, LANES), jnp.float32) if v is None else v
-            v = v * turn if c == 2 else v
-            if late:
-                outs[k][i, :] = before[k][i, :] + v
-            else:
-                outs[k + 2 * (d < 2)][i, :] = v
-
-        response(message, (t0, t1), 0, coef, lambda d: d, finish, powers_in=powers_in)
-
-
-def rows_response(scal, messages, fields, powers_in, before=(), after=()):
+            outs[k + 2 * (d < 2)][pl.ds((d % 2 * 3 + c) * GX, GX), :] = v * turn if c == 2 else v
+
+        response(message, (t0, t1), 0, coef, lambda d: d, finish, powers_in=(0, 1, 2))
+
+
+def rows_response(scal, messages, fields):
     table = whole((GX, GX))
     buf = vmem(buffer_rows(4))
-    count = 2 if before else 4
     return pl.pallas_call(
-        functools.partial(rows_response_kernel, powers_in),
+        rows_response_kernel,
         grid_spec=pltpu.PrefetchScalarGridSpec(
             num_scalar_prefetch=1,
             grid=(3,),
-            in_specs=[lane_block(256)] * 2
-            + [lane_block(384)] * len(before)
-            + [pl.BlockSpec(memory_space=pl.ANY)] * len(after)
-            + [table] * 3,
-            out_specs=[lane_block(384)] * count,
+            in_specs=[stacked(384)] * 2 + [table] * 3,
+            out_specs=[lane_block(384)] * 4,
             scratch_shapes=[pltpu.VMEM((4, 4, GX, LANES), jnp.float32), buf, buf],
         ),
-        out_shape=[shape(384, 384)] * count,
+        out_shape=[shape(384, 384)] * 4,
         compiler_params=params(16),
         name="rows_response",
-    )(scal, *messages, *before, *after, *fields)
-
-
-def columns_kernel(scal, s0, s1, r0, r1, dep, cor, drag, out, inner, outer, coef, v0, v1, v2, v3):
+    )(scal, *messages, *fields)
+
+
+def columns_kernel(scal, s0, s1, r0, r1, *refs):
+    late, (dep, cor, drag, out, inner, outer, coef, v0, v1, v2, v3, near, extra) = refs[:-13], refs[-13:]
     rows, base = 4, 2
     half = scal[1]
 
@@ -306,12 +356,37 @@
         load_coefficients(dep, cor, drag, scal[0] - 2, rows + 4, coef)
         for ref in (v0, v1, v2, v3):
             zero_gaps(ref, rows + 4)
+
+    if late:
+        turn = 1.0 - 2.0 * half.astype(jnp.float32)
+
+        @pl.when(pl.program_id(0) == 0)
+        def _():
+            load_coefficients(dep, cor, drag, scal[3], 4, near, lambda j: jnp.where(half == 0, j, 3 - j))
+            for k in range(2):
+                for t in range(3):
+                    lanes = pl.ds(t * LANES, LANES)
+                    extra[pl.ds(k * GX, GX), lanes] = near[0, D] * (late[k][pl.ds(GX, GX), lanes] * (-0.25 * turn))
+
+        @pl.when(pl.program_id(0) == 1)
+        def _():
+            for k in range(2):
+                extra[pl.ds(k * GX, GX), :] = late[k][pl.ds(0, GX), :] * (0.125 * STEP * turn)
+
+        @pl.when(pl.program_id(0) == 2)
+        def _():
+            extra[...] = jnp.zeros_like(extra)
 
     for k, (s_ref, r_ref) in enumerate(((s0, r0), (s1, r1))):
         core = half if k == 0 else 1 - half
         start = pl.multiple_of(core * (2 * 3 * SEG), 8)
         for t in range(3):
-            piece = (s_ref[:, t * LANES : (t + 1) * LANES] + r_ref[:, t * LANES : (t + 1) * LANES]).T
+            lanes = slice(t * LANES, (t + 1) * LANES)
+            piece = s_ref[:, lanes] + r_ref[:, lanes]
+            if late:
+                more = extra[pl.ds(k * GX, GX), lanes]
+                piece = jnp.concatenate([piece[:GX] + more, piece[GX:]], axis=0)
+            piece = piece.T
             for i in range(2):
                 seg = t * 2 + i
                 place = pl.multiple_of(start + (base * 3 + seg) * SEG + 8, 8)
@@ -340,24 +415,30 @@
         put(outer, rows - 1)
 
 
-def columns_step(scal, s0, s1, r0, r1, fields):
+def columns_step(scal, s0, s1, r0, r1, late, fields):
     table = whole((GX, GX))
     part = 768 // CHUNKS
-    tiles = part // LANES
     buf = vmem(buffer_rows(8))
     return pl.pallas_call(
         columns_kernel,
         grid_spec=pltpu.PrefetchScalarGridSpec(
             num_scalar_prefetch=1,
-            grid=(tiles,),
-            in_specs=[pl.BlockSpec((LANES, 384), lambda i, *_: (i, 0))] * 4 + [table] * 3,
-            out_specs=[lane_block(768), lane_block(512), lane_block(512)],
-            scratch_shapes=[pltpu.VMEM((8, 4, GX, LANES), jnp.float32), buf, buf, buf, buf],
+            grid=(part // LANES,),
+            in_specs=[pl.BlockSpec((LANES, 384), lambda i, *_: (i, 0))] * 4
+            + [whole((128, 384))] * len(late)
+            + [table] * 3,
+            out_specs=[stacked(768), stacked(512), stacked(512)],
+            scratch_shapes=[
+                pltpu.VMEM((8, 4, GX, LANES), jnp.float32),
+                *[buf] * 4,
+                pltpu.VMEM((4, 4, GX, LANES), jnp.float32),
+                vmem(2 * GX, 384),
+            ],
         ),
-        out_shape=[shape(768, part), shape(512, part), shape(512, part)],
+        out_shape=[shape(part * 6, LANES), shape(part * 4, LANES), shape(part * 4, LANES)],
         compiler_params=params(24),
         name="columns_step",
-    )(scal, s0, s1, r0, r1, *fields)
+    )(scal, s0, s1, r0, r1, *late, *fields)
 
 
 def columns_response_kernel(scal, own, inner, outer, dep, cor, drag, z0, z1, coef, t0, t1, acc):
@@ -406,7 +487,7 @@
         grid_spec=pltpu.PrefetchScalarGridSpec(
             num_scalar_prefetch=1,
             grid=(part // LANES,),
-            in_specs=[lane_block(768), lane_block(512), lane_block(512)] + [table] * 3,
+            in_specs=[stacked(768), stacked(512), stacked(512)] + [table] * 3,
             out_specs=[pl.BlockSpec((LANES, 384), lambda i, *_: (i, 0))] * 2,
             scratch_shapes=[pltpu.VMEM((4, 4, GX, LANES), jnp.float32), buf, buf, vmem(768)],
         ),
@@ -491,21 +572,19 @@
     def send(pair, pairs):
         return [lax.ppermute(v, both, pairs[k]) for k, v in enumerate(pair)]
 
-    s00, s01, s10, s11, e0, e1, b0, b1 = rows_step(covariance, fields)
-    early = send((e0, e1), boundary)
+    edges = edge_step(covariance, fields)
+    early = send(edges, boundary)
+    s00, s01, s10, s11, b0, b1 = rows_step(covariance, edges[0], fields)
     far = send((s00, s10), split)
-    b0, b1, *early = lax.optimization_barrier((b0, b1, *early))
     late = send((b0, b1), boundary)
     near = send((s01, s11), split)
     rscal = jnp.stack([row * 8 + second * 4, second]).astype(jnp.int32)
-    cscal = jnp.stack([(z * 2 + core) * 4, second, core]).astype(jnp.int32)
+    cscal = jnp.stack([(z * 2 + core) * 4, second, core, row * 8 + second * 4]).astype(jnp.int32)
     fscal = jnp.stack([row, core]).astype(jnp.int32)
-    r02, r12, r00, r10 = rows_response(rscal, early, fields, (0, 1))
+    r02, r12, r00, r10 = rows_response(rscal, early, fields)
     result = None
-    for chunk, halves, moved in ((0, far, (r02, r12)), (1, near, None)):
-        if chunk == 1:
-            moved = rows_response(rscal, late, fields, (2, 3), (r00, r10), (own,))
-        own, inside, outside = columns_step(cscal, *halves, *moved, fields)
+    for chunk, halves, moved, rest in ((0, far, (r02, r12), ()), (1, near, (r00, r10), late)):
+        own, inside, outside = columns_step(cscal, *halves, *moved, rest, fields)
         outside = lax.ppermute(outside, "col", outer)
         inside = lax.ppermute(inside, "col", inner)
         ready = send(columns_response(cscal, own, inside, outside, fields), back)

time: 108 us -> 105 us (0.972)
  starting transfers between devices: 41.9 us -> 35.8 us
  waiting for transfers between devices: 35.6 us -> 38.6 us
    ppermute x12, starting transfers between devices: 34.5 us -> 28.5 us  [send(): return [lax.ppermute(v, both, pairs[k]) for k, v in enumerate(pair)]]
    ppermute x12, waiting for transfers between devices: 30.6 us -> 33.8 us  [send(): return [lax.ppermute(v, both, pairs[k]) for k, v in enumerate(pair)]]
    pallas_call x2, Pallas kernels: 7.3 us -> 8.4 us  [columns_step(): pl.pallas_call(columns_kernel, grid_spec=pltpu.PrefetchScalarGridSpec(num...]
  transfers between devices with their start and end apart: 16 -> 16, of which waited for: 6 -> 6; matrix products, arithmetic and copies ran while one was open for 0% -> 0% of each run, Pallas kernels for 19% -> 24%
where the time goes in v3:
time: 105 us
  waiting for transfers between devices  38.6 us (37%)
  starting transfers between devices  35.8 us (34%)
  Pallas kernels  29.8 us (28%)
    ppermute x12, waiting for transfers between devices, send(): return [lax.ppermute(v, both, pairs[k]) for k, v in enumerate(pair)]  33.8 us
    ppermute x12, starting transfers between devices, send(): return [lax.ppermute(v, both, pairs[k]) for k, v in enumerate(pair)]  28.5 us
    pallas_call x2, Pallas kernels, columns_step(): pl.pallas_call(columns_kernel, grid_spec=pltpu.PrefetchScalarGridSpec(num...  8.4 us
    pallas_call x1, Pallas kernels, rows_step(): pl.pallas_call(rows_kernel, grid_spec=pltpu.PrefetchScalarGridSpec(num_sc...  6.64 us
    pallas_call x2, Pallas kernels, columns_response(): pl.pallas_call(columns_response_kernel, grid_spec=pltpu.PrefetchScalarGri...  5.71 us
    ppermute x2, waiting for transfers between devices, shards(): outside = lax.ppermute(outside, 'col', outer)  4.8 us
    ppermute x2, starting transfers between devices, shards(): outside = lax.ppermute(outside, 'col', outer)  3.82 us
    ppermute x2, starting transfers between devices, shards(): inside = lax.ppermute(inside, 'col', inner)  3.5 us
  transfers between devices with their start and end apart: 16, of which 6 were waited for; matrix products, arithmetic and copies ran while one was open for 0% of the time, Pallas kernels for 24%

profile of v3, /device:TPU:120, one launch (start us, length us, event | category | flops | bytes accessed | tf_op | source)
XLA Modules:
  0.0 104.6 jit_solution(15875877881338688843)
XLA Ops:
  0.0 3.4 %edge_step.1 = (f32[1152,128]{1,0:T(8,128)}, f32[1152,128]{1,0:T(8,128)}) custom-call(f32[1536,384]{1,0:T(8,128)} %x_ref.1, f32[1536,384]{1,0:T(8,128)} %x_ref.1, f32[1536,384]{1,0:T(8,128)} %x_ref.1, f32[1536,384]{1,0:T(8,128)} %x_ref.1, f32[1536,384]{1,0:T(8,128)} %x_ref.1, f32[1536,384]{1,0:T(8,128)} %x_ref.1, f32[64,64]{1,0:T(8,128)} %dep.7, ...), custom_call_target="tpu_custom_call" | custom-call | tf_op jit(solution)/shard_map/edge_step/pallas_call | solution.py:205
  3.4 5.0 %collective-permute-start.3 = (f32[1152,128]{1,0:T(8,128)}, f32[1152,128]{1,0:T(8,128)S(1)}, u32[]{:S(2)}, u32[]{:S(2)}) collective-permute-start(f32[1152,128]{1,0:T(8,128)} %get-tuple-element.30), channel_id=1, source_target_pairs={{1,32},{3,33},{5,36},{7,37},{9,40},{11,41},{13,44},{15,45},{17,48}... | collective-permute-start | bytes 1769480 | tf_op jit(solution)/shard_map/ppermute | solution.py:573
  8.4 2.5 %collective-permute-start.2 = (f32[1152,128]{1,0:T(8,128)}, f32[1152,128]{1,0:T(8,128)S(1)}, u32[]{:S(2)}, u32[]{:S(2)}) collective-permute-start(f32[1152,128]{1,0:T(8,128)} %get-tuple-element.27.after), channel_id=1, source_target_pairs={{0,32},{2,33},{4,36},{6,37},{8,40},{10,41},{12,44},{14,45},{16,48}... | collective-permute-start | bytes 1769480 | tf_op jit(solution)/shard_map/ppermute | solution.py:573
  11.0 6.6 %rows_step.1 = (f32[384,384]{1,0:T(8,128)}, f32[384,384]{1,0:T(8,128)}, f32[384,384]{1,0:T(8,128)}, f32[384,384]{1,0:T(8,128)}, f32[128,384]{1,0:T(8,128)}, /*index=5*/f32[128,384]{1,0:T(8,128)}) custom-call(f32[1536,384]{1,0:T(8,128)} %x_ref.1, f32[1152,128]{1,0:T(8,128)} %get-tuple-element.27.after, f32[64,64]{1,0:T(8,128)} %dep.7, f32[64,64]{1,0:T(8,128)} %cor.7, ...), custom_call_target="tpu_custom_call" | custom-call | tf_op jit(solution)/shard_map/rows_step/pallas_call | solution.py:292
  17.6 1.7 %collective-permute-start.10 = (f32[384,384]{1,0:T(8,128)}, f32[384,384]{1,0:T(8,128)S(1)}, u32[]{:S(2)}, u32[]{:S(2)}) collective-permute-start(f32[384,384]{1,0:T(8,128)} %get-tuple-element.40), channel_id=1, source_target_pairs={{0,0},{1,2},{2,1},{3,3},{4,4},{5,6},{6,5},{7,7},{8,8},{9,10},{10,9... | collective-permute-start | bytes 1769480 | tf_op jit(solution)/shard_map/ppermute | solution.py:573
  19.3 2.2 %collective-permute-start.11 = (f32[384,384]{1,0:T(8,128)}, f32[384,384]{1,0:T(8,128)}, u32[]{:S(2)}, u32[]{:S(2)}) collective-permute-start(f32[384,384]{1,0:T(8,128)} %get-tuple-element.41), channel_id=1, source_target_pairs={{0,2},{1,0},{2,3},{3,1},{4,6},{5,4},{6,7},{7,5},{8,10},{9,8},{10,1... | collective-permute-start | bytes 1769480 | tf_op jit(solution)/shard_map/ppermute | solution.py:573
  23.3 11.4 %collective-permute-done.3.m1 = f32[1152,128]{1,0:T(8,128)S(1)} collective-permute-done((f32[1152,128]{1,0:T(8,128)}, f32[1152,128]{1,0:T(8,128)S(1)}, u32[]{:S(2)}, u32[]{:S(2)}) %collective-permute-start.3) | collective-permute-done | bytes 589856 | tf_op jit(solution)/shard_map/ppermute | solution.py:573
  34.9 1.9 %collective-permute-start.4 = (f32[128,384]{1,0:T(8,128)}, f32[128,384]{1,0:T(8,128)S(1)}, u32[]{:S(2)}, u32[]{:S(2)}) collective-permute-start(f32[128,384]{1,0:T(8,128)} %get-tuple-element.33), channel_id=1, source_target_pairs={{0,32},{2,33},{4,36},{6,37},{8,40},{10,41},{12,44},{14,45},{16,48}... | collective-permute-start | bytes 589832 | tf_op jit(solution)/shard_map/ppermute | solution.py:573
  36.8 6.3 %collective-permute-start.5 = (f32[128,384]{1,0:T(8,128)}, f32[128,384]{1,0:T(8,128)S(1)}, u32[]{:S(2)}, u32[]{:S(2)}) collective-permute-start(f32[128,384]{1,0:T(8,128)} %get-tuple-element.34), channel_id=1, source_target_pairs={{1,32},{3,33},{5,36},{7,37},{9,40},{11,41},{13,44},{15,45},{17,48}... | collective-permute-start | bytes 589832 | tf_op jit(solution)/shard_map/ppermute | solution.py:573
  43.3 2.3 %rows_response.1 = (f32[384,384]{1,0:T(8,128)S(1)}, f32[384,384]{1,0:T(8,128)S(1)}, f32[384,384]{1,0:T(8,128)S(1)}, f32[384,384]{1,0:T(8,128)S(1)}) custom-call(s32[2]{0:T(128)S(1)} %pad_add_fusion.2.scal, f32[1152,128]{1,0:T(8,128)S(1)} %collective-permute-done.2.m0, f32[1152,128]{1,0:T(8,128)S(1)} %collective-permute-done.3.m1, f32[64,64]{1,0:T(8,128)S(1)} %copy-done.1, ...), custom_call_target="tpu_custom_call" | custom-call | tf_op jit(solution)/shard_map/rows_response/pallas_call | solution.py:334
  45.6 4.5 %columns_step.3 = (f32[2304,128]{1,0:T(8,128)S(1)}, f32[1536,128]{1,0:T(8,128)S(1)}, f32[1536,128]{1,0:T(8,128)S(1)}) custom-call(s32[4]{0:T(128)S(1)} %pad_add_fusion.1.scal, f32[384,384]{1,0:T(8,128)S(1)} %collective-permute-done.10.s0, f32[384,384]{1,0:T(8,128)} %collective-permute-done.11.s1, f32[384,384]{1,0:T(8,128)S(1)} %get-tuple-element.42.r0, ...), custom_call_target="tpu_custom_call" | custom-call | tf_op jit(solution)/shard_map/columns_step/pallas_call | solution.py:422
  50.3 4.6 %collective-permute-done.4.refs_0_ = f32[128,384]{1,0:T(8,128)S(1)} collective-permute-done((f32[128,384]{1,0:T(8,128)}, f32[128,384]{1,0:T(8,128)S(1)}, u32[]{:S(2)}, u32[]{:S(2)}) %collective-permute-start.4) | collective-permute-done | bytes 196640 | tf_op jit(solution)/shard_map/ppermute | solution.py:573
  54.9 1.9 %collective-permute-start.13 = (f32[1536,128]{1,0:T(8,128)S(1)}, f32[1536,128]{1,0:T(8,128)S(1)}, u32[]{:S(2)}, u32[]{:S(2)}) collective-permute-start(f32[1536,128]{1,0:T(8,128)S(1)} %get-tuple-element.46), channel_id=1, source_target_pairs={{1,4},{4,1},{3,6},{6,3},{5,8},{8,5},{7,10},{10,7},{9,12},{12,9},{1... | collective-permute-start | bytes 2359304 | tf_op jit(solution)/shard_map/ppermute | solution.py:588
  56.9 3.9 %columns_step.2 = (f32[2304,128]{1,0:T(8,128)S(1)}, f32[1536,128]{1,0:T(8,128)S(1)}, f32[1536,128]{1,0:T(8,128)S(1)}) custom-call(s32[4]{0:T(128)S(1)} %pad_add_fusion.1.scal, f32[384,384]{1,0:T(8,128)S(1)} %collective-permute-done.s0, f32[384,384]{1,0:T(8,128)S(1)} %collective-permute-done.1.s1, f32[384,384]{1,0:T(8,128)S(1)} %get-tuple-element.31.r0, ...), custom_call_target="tpu_custom_call" | custom-call | tf_op jit(solution)/shard_map/columns_step/pallas_call | solution.py:422
  60.8 3.3 %collective-permute-start.6 = (f32[1536,128]{1,0:T(8,128)S(1)}, f32[1536,128]{1,0:T(8,128)S(1)}, u32[]{:S(2)}, u32[]{:S(2)}) collective-permute-start(f32[1536,128]{1,0:T(8,128)S(1)} %get-tuple-element.36), channel_id=1, source_target_pairs={{0,1},{1,0},{2,3},{3,2},{4,5},{5,4},{6,7},{7,6},{8,9},{9,8},{10,11... | collective-permute-start | bytes 2359304 | tf_op jit(solution)/shard_map/ppermute | solution.py:589
  64.1 1.9 %collective-permute-start.7 = (f32[1536,128]{1,0:T(8,128)S(1)}, f32[1536,128]{1,0:T(8,128)S(1)}, u32[]{:S(2)}, u32[]{:S(2)}) collective-permute-start(f32[1536,128]{1,0:T(8,128)S(1)} %get-tuple-element.37), channel_id=1, source_target_pairs={{1,4},{4,1},{3,6},{6,3},{5,8},{8,5},{7,10},{10,7},{9,12},{12,9},{1... | collective-permute-start | bytes 2359304 | tf_op jit(solution)/shard_map/ppermute | solution.py:588
  66.0 2.2 %collective-permute-done.13.outer = f32[1536,128]{1,0:T(8,128)S(1)} collective-permute-done((f32[1536,128]{1,0:T(8,128)S(1)}, f32[1536,128]{1,0:T(8,128)S(1)}, u32[]{:S(2)}, u32[]{:S(2)}) %collective-permute-start.13) | collective-permute-done | bytes 786464 | tf_op jit(solution)/shard_map/ppermute | solution.py:588
  68.2 2.9 %columns_response.3 = (f32[384,384]{1,0:T(8,128)S(1)}, f32[384,384]{1,0:T(8,128)S(1)}) custom-call(s32[4]{0:T(128)S(1)} %pad_add_fusion.1.scal, f32[2304,128]{1,0:T(8,128)S(1)} %get-tuple-element.44.own, f32[1536,128]{1,0:T(8,128)S(1)} %collective-permute-done.12.inner, f32[1536,128]{1,0:T(8,128)S(1)} %collective-permute-done.13.outer, ...), custom_call_target="tpu_custom_call" | custom-call | tf_op jit(solution)/shard_map/columns_response/pallas_call | solution.py:485
  71.8 3.0 %collective-permute-start.15 = (f32[384,384]{1,0:T(8,128)S(1)}, f32[384,384]{1,0:T(8,128)S(1)}, u32[]{:S(2)}, u32[]{:S(2)}) collective-permute-start(f32[384,384]{1,0:T(8,128)S(1)} %get-tuple-element.48), channel_id=1, source_target_pairs={{0,1},{1,3},{2,0},{3,2},{4,5},{5,7},{6,4},{7,6},{8,9},{9,11},{10,8... | collective-permute-start | bytes 1769480 | tf_op jit(solution)/shard_map/ppermute | solution.py:573
  74.8 2.6 %collective-permute-done.7.outer = f32[1536,128]{1,0:T(8,128)S(1)} collective-permute-done((f32[1536,128]{1,0:T(8,128)S(1)}, f32[1536,128]{1,0:T(8,128)S(1)}, u32[]{:S(2)}, u32[]{:S(2)}) %collective-permute-start.7) | collective-permute-done | bytes 786464 | tf_op jit(solution)/shard_map/ppermute | solution.py:588
  77.4 2.9 %columns_response.2 = (f32[384,384]{1,0:T(8,128)S(1)}, f32[384,384]{1,0:T(8,128)S(1)}) custom-call(s32[4]{0:T(128)S(1)} %pad_add_fusion.1.scal, f32[2304,128]{1,0:T(8,128)S(1)} %get-tuple-element.35.own, f32[1536,128]{1,0:T(8,128)S(1)} %collective-permute-done.6.inner, f32[1536,128]{1,0:T(8,128)S(1)} %collective-permute-done.7.outer, ...), custom_call_target="tpu_custom_call" | custom-call | tf_op jit(solution)/shard_map/columns_response/pallas_call | solution.py:485
  81.0 2.5 %collective-permute-start.9 = (f32[384,384]{1,0:T(8,128)S(1)}, f32[384,384]{1,0:T(8,128)S(1)}, u32[]{:S(2)}, u32[]{:S(2)}) collective-permute-start(f32[384,384]{1,0:T(8,128)S(1)} %get-tuple-element.39), channel_id=1, source_target_pairs={{0,1},{1,3},{2,0},{3,2},{4,5},{5,7},{6,4},{7,6},{8,9},{9,11},{10,8... | collective-permute-start | bytes 1769480 | tf_op jit(solution)/shard_map/ppermute | solution.py:573
  83.6 6.7 %collective-permute-done.15.z1 = f32[384,384]{1,0:T(8,128)S(1)} collective-permute-done((f32[384,384]{1,0:T(8,128)S(1)}, f32[384,384]{1,0:T(8,128)S(1)}, u32[]{:S(2)}, u32[]{:S(2)}) %collective-permute-start.15) | collective-permute-done | bytes 589856 | tf_op jit(solution)/shard_map/ppermute | solution.py:573
  92.0 11.0 %collective-permute-done.9.z1 = f32[384,384]{1,0:T(8,128)S(1)} collective-permute-done((f32[384,384]{1,0:T(8,128)S(1)}, f32[384,384]{1,0:T(8,128)S(1)}, u32[]{:S(2)}, u32[]{:S(2)}) %collective-permute-start.9) | collective-permute-done | bytes 589856 | tf_op jit(solution)/shard_map/ppermute | solution.py:573
  (28 shorter events, 7.1 us)
Async XLA Ops:
  3.4 39.9 %copy-start.1 = (f32[64,64]{1,0:T(8,128)S(1)}, f32[64,64]{1,0:T(8,128)}, u32[]{:S(2)}) copy-start(f32[64,64]{1,0:T(8,128)} %dep.7) | copy-start | bytes 49156
  3.4 39.9 %copy-start.2 = (f32[64,64]{1,0:T(8,128)S(1)}, f32[64,64]{1,0:T(8,128)}, u32[]{:S(2)}) copy-start(f32[64,64]{1,0:T(8,128)} %cor.7) | copy-start | bytes 49156
  3.4 39.9 %copy-start.3 = (f32[64,64]{1,0:T(8,128)S(1)}, f32[64,64]{1,0:T(8,128)}, u32[]{:S(2)}) copy-start(f32[64,64]{1,0:T(8,128)} %drag.7) | copy-start | bytes 49156
  3.4 31.3 %collective-permute-start.3 = (f32[1152,128]{1,0:T(8,128)}, f32[1152,128]{1,0:T(8,128)S(1)}, u32[]{:S(2)}, u32[]{:S(2)}) collective-permute-start(f32[1152,128]{1,0:T(8,128)} %get-tuple-element.30), channel_id=1, source_target_pairs={{1,32},{3,33},{5,36},{7,37},{9,40},{11,41},{13,44},{15,45},{17,48}... | collective-permute-start | bytes 1769480 | tf_op jit(solution)/shard_map/ppermute | solution.py:573
  8.4 26.5 %collective-permute-start.2 = (f32[1152,128]{1,0:T(8,128)}, f32[1152,128]{1,0:T(8,128)S(1)}, u32[]{:S(2)}, u32[]{:S(2)}) collective-permute-start(f32[1152,128]{1,0:T(8,128)} %get-tuple-element.27.after), channel_id=1, source_target_pairs={{0,32},{2,33},{4,36},{6,37},{8,40},{10,41},{12,44},{14,45},{16,48}... | collective-permute-start | bytes 1769480 | tf_op jit(solution)/shard_map/ppermute | solution.py:573
  17.6 19.2 %collective-permute-start.10 = (f32[384,384]{1,0:T(8,128)}, f32[384,384]{1,0:T(8,128)S(1)}, u32[]{:S(2)}, u32[]{:S(2)}) collective-permute-start(f32[384,384]{1,0:T(8,128)} %get-tuple-element.40), channel_id=1, source_target_pairs={{0,0},{1,2},{2,1},{3,3},{4,4},{5,6},{6,5},{7,7},{8,8},{9,10},{10,9... | collective-permute-start | bytes 1769480 | tf_op jit(solution)/shard_map/ppermute | solution.py:573
  19.3 26.3 %collective-permute-start.11 = (f32[384,384]{1,0:T(8,128)}, f32[384,384]{1,0:T(8,128)}, u32[]{:S(2)}, u32[]{:S(2)}) collective-permute-start(f32[384,384]{1,0:T(8,128)} %get-tuple-element.41), channel_id=1, source_target_pairs={{0,2},{1,0},{2,3},{3,1},{4,6},{5,4},{6,7},{7,5},{8,10},{9,8},{10,1... | collective-permute-start | bytes 1769480 | tf_op jit(solution)/shard_map/ppermute | solution.py:573
  21.5 35.3 %collective-permute-start = (f32[384,384]{1,0:T(8,128)}, f32[384,384]{1,0:T(8,128)S(1)}, u32[]{:S(2)}, u32[]{:S(2)}) collective-permute-start(f32[384,384]{1,0:T(8,128)} %get-tuple-element.28), channel_id=1, source_target_pairs={{0,0},{1,2},{2,1},{3,3},{4,4},{5,6},{6,5},{7,7},{8,8},{9,10},{10,9... | collective-permute-start | bytes 1769480 | tf_op jit(solution)/shard_map/ppermute | solution.py:573
  34.7 22.2 %collective-permute-start.1 = (f32[384,384]{1,0:T(8,128)}, f32[384,384]{1,0:T(8,128)S(1)}, u32[]{:S(2)}, u32[]{:S(2)}) collective-permute-start(f32[384,384]{1,0:T(8,128)} %get-tuple-element.29), channel_id=1, source_target_pairs={{0,2},{1,0},{2,3},{3,1},{4,6},{5,4},{6,7},{7,5},{8,10},{9,8},{10,1... | collective-permute-start | bytes 1769480 | tf_op jit(solution)/shard_map/ppermute | solution.py:573
  34.9 20.0 %collective-permute-start.4 = (f32[128,384]{1,0:T(8,128)}, f32[128,384]{1,0:T(8,128)S(1)}, u32[]{:S(2)}, u32[]{:S(2)}) collective-permute-start(f32[128,384]{1,0:T(8,128)} %get-tuple-element.33), channel_id=1, source_target_pairs={{0,32},{2,33},{4,36},{6,37},{8,40},{10,41},{12,44},{14,45},{16,48}... | collective-permute-start | bytes 589832 | tf_op jit(solution)/shard_map/ppermute | solution.py:573
  36.8 20.0 %collective-permute-start.5 = (f32[128,384]{1,0:T(8,128)}, f32[128,384]{1,0:T(8,128)S(1)}, u32[]{:S(2)}, u32[]{:S(2)}) collective-permute-start(f32[128,384]{1,0:T(8,128)} %get-tuple-element.34), channel_id=1, source_target_pairs={{1,32},{3,33},{5,36},{7,37},{9,40},{11,41},{13,44},{15,45},{17,48}... | collective-permute-start | bytes 589832 | tf_op jit(solution)/shard_map/ppermute | solution.py:573
  50.1 15.9 %collective-permute-start.12 = (f32[1536,128]{1,0:T(8,128)S(1)}, f32[1536,128]{1,0:T(8,128)S(1)}, u32[]{:S(2)}, u32[]{:S(2)}) collective-permute-start(f32[1536,128]{1,0:T(8,128)S(1)} %get-tuple-element.45), channel_id=1, source_target_pairs={{0,1},{1,0},{2,3},{3,2},{4,5},{5,4},{6,7},{7,6},{8,9},{9,8},{10,11... | collective-permute-start | bytes 2359304 | tf_op jit(solution)/shard_map/ppermute | solution.py:589
  54.9 13.3 %collective-permute-start.13 = (f32[1536,128]{1,0:T(8,128)S(1)}, f32[1536,128]{1,0:T(8,128)S(1)}, u32[]{:S(2)}, u32[]{:S(2)}) collective-permute-start(f32[1536,128]{1,0:T(8,128)S(1)} %get-tuple-element.46), channel_id=1, source_target_pairs={{1,4},{4,1},{3,6},{6,3},{5,8},{8,5},{7,10},{10,7},{9,12},{12,9},{1... | collective-permute-start | bytes 2359304 | tf_op jit(solution)/shard_map/ppermute | solution.py:588
  60.8 14.0 %collective-permute-start.6 = (f32[1536,128]{1,0:T(8,128)S(1)}, f32[1536,128]{1,0:T(8,128)S(1)}, u32[]{:S(2)}, u32[]{:S(2)}) collective-permute-start(f32[1536,128]{1,0:T(8,128)S(1)} %get-tuple-element.36), channel_id=1, source_target_pairs={{0,1},{1,0},{2,3},{3,2},{4,5},{5,4},{6,7},{7,6},{8,9},{9,8},{10,11... | collective-permute-start | bytes 2359304 | tf_op jit(solution)/shard_map/ppermute | solution.py:589
  64.1 13.3 %collective-permute-start.7 = (f32[1536,128]{1,0:T(8,128)S(1)}, f32[1536,128]{1,0:T(8,128)S(1)}, u32[]{:S(2)}, u32[]{:S(2)}) collective-permute-start(f32[1536,128]{1,0:T(8,128)S(1)} %get-tuple-element.37), channel_id=1, source_target_pairs={{1,4},{4,1},{3,6},{6,3},{5,8},{8,5},{7,10},{10,7},{9,12},{12,9},{1... | collective-permute-start | bytes 2359304 | tf_op jit(solution)/shard_map/ppermute | solution.py:588
  68.2 22.1 %copy-start = (f32[1536,384]{1,0:T(8,128)S(1)}, f32[1536,384]{1,0:T(8,128)}, u32[]{:S(2)}) copy-start(f32[1536,384]{1,0:T(8,128)} %noise.3) | copy-start | bytes 7077892
  71.1 12.5 %collective-permute-start.14 = (f32[384,384]{1,0:T(8,128)S(1)}, f32[384,384]{1,0:T(8,128)S(1)}, u32[]{:S(2)}, u32[]{:S(2)}) collective-permute-start(f32[384,384]{1,0:T(8,128)S(1)} %get-tuple-element.47), channel_id=1, source_target_pairs={{0,0},{1,2},{2,1},{3,3},{4,4},{5,6},{6,5},{7,7},{8,8},{9,10},{10,9... | collective-permute-start | bytes 1769480 | tf_op jit(solution)/shard_map/ppermute | solution.py:573
  71.8 18.5 %collective-permute-start.15 = (f32[384,384]{1,0:T(8,128)S(1)}, f32[384,384]{1,0:T(8,128)S(1)}, u32[]{:S(2)}, u32[]{:S(2)}) collective-permute-start(f32[384,384]{1,0:T(8,128)S(1)} %get-tuple-element.48), channel_id=1, source_target_pairs={{0,1},{1,3},{2,0},{3,2},{4,5},{5,7},{6,4},{7,6},{8,9},{9,11},{10,8... | collective-permute-start | bytes 1769480 | tf_op jit(solution)/shard_map/ppermute | solution.py:573
  80.3 11.7 %collective-permute-start.8 = (f32[384,384]{1,0:T(8,128)S(1)}, f32[384,384]{1,0:T(8,128)S(1)}, u32[]{:S(2)}, u32[]{:S(2)}) collective-permute-start(f32[384,384]{1,0:T(8,128)S(1)} %get-tuple-element.38), channel_id=1, source_target_pairs={{0,0},{1,2},{2,1},{3,3},{4,4},{5,6},{6,5},{7,7},{8,8},{9,10},{10,9... | collective-permute-start | bytes 1769480 | tf_op jit(solution)/shard_map/ppermute | solution.py:573
  81.0 22.0 %collective-permute-start.9 = (f32[384,384]{1,0:T(8,128)S(1)}, f32[384,384]{1,0:T(8,128)S(1)}, u32[]{:S(2)}, u32[]{:S(2)}) collective-permute-start(f32[384,384]{1,0:T(8,128)S(1)} %get-tuple-element.39), channel_id=1, source_target_pairs={{0,1},{1,3},{2,0},{3,2},{4,5},{5,7},{6,4},{7,6},{8,9},{9,11},{10,8... | collective-permute-start | bytes 1769480 | tf_op jit(solution)/shard_map/ppermute | solution.py:573

commit v4 on v3

--- a/solution.py
+++ b/solution.py
@@ -154,67 +154,7 @@
         have, src = new, bufs[step % 2]
 
 
-EDGE_ROWS = (0, 1, 2, 5, 6, 7)
-
-
-def edge_kernel(*refs):
-    rows, (dep, cor, drag, e0, e1, coef, u0, u1) = refs[:6], refs[6:]
-    base = 1
-    load_coefficients(dep, cor, drag, lax.axis_index("row") * 8 - base, 10, coef, only=(0, 1, 2, 7, 8, 9))
-    for ref in (u0, u1):
-        zero_gaps(ref, 10)
-    core = lax.axis_index("col") % 2
-    have = {(r, c) for r in EDGE_ROWS for c in range(3)}
-
-    @pl.loop(0, 3)
-    def _(tile):
-        lanes = pl.ds(pl.multiple_of(tile * LANES, LANES), LANES)
-        for r, ref in zip(EDGE_ROWS, rows):
-            for c in range(3):
-                u0[pl.ds(at(r + base, c), GX), :] = ref[pl.ds(c * GX, GX), lanes]
-        new = set()
-        for r in (-1, 0, 1, 6, 7, 8):
-            out = tendency(u0, have, r, base, coef, r + base, ghost=r in (-1, 8))
-            for c, v in out.items():
-                if v is not None:
-                    u1[pl.ds(at(r + base, c), GX), :] = v
-                    new.add((r, c))
-
-        def put(to, row):
-            out = tendency(u1, new, row, base, coef, row + base, want=(0, 2))
-            for i, c in enumerate((0, 2)):
-                place = pl.multiple_of(tile * 384 + i * GX, GX)
-                to[pl.ds(place, GX), :] = u0[pl.ds(at(row + base, c), GX), :]
-                to[pl.ds(place + 2 * GX, GX), :] = u1[pl.ds(at(row + base, c), GX), :]
-                to[pl.ds(place + 4 * GX, GX), :] = out[c] * 0.5
-
-        @pl.when(core == 0)
-        def _():
-            put(e0, 7)
-            put(e1, 0)
-
-        @pl.when(core == 1)
-        def _():
-            put(e1, 7)
-            put(e0, 0)
-
-
-def edge_step(block, fields):
-    table = whole((GX, GX))
-    buf = vmem(buffer_rows(10))
-    return pl.pallas_call(
-        edge_kernel,
-        grid=(1,),
-        in_specs=[pl.BlockSpec((192, 384), lambda i, r=r: (r, 0)) for r in EDGE_ROWS] + [table] * 3,
-        out_specs=[whole((1152, LANES))] * 2,
-        scratch_shapes=[pltpu.VMEM((10, 4, GX, LANES), jnp.float32), buf, buf],
-        out_shape=[shape(1152, LANES)] * 2,
-        compiler_params=params(58),
-        name="edge_step",
-    )(*[block] * 6, *fields)
-
-
-def rows_kernel(x_ref, after, dep, cor, drag, s00, s01, s10, s11, b0, b1, coef, v0, v1, v2, v3, acc):
+def rows_kernel(x_ref, dep, cor, drag, s00, s01, s10, s11, e0, e1, b0, b1, coef, v0, v1, v2, v3, acc):
     rows, base = 8, 2
 
     @pl.when(pl.program_id(0) == 0)
@@ -236,9 +176,11 @@
 
     powers((v0, v1, v2, v3), rows, base, coef, finish)
 
-    def put(to, row):
-        for i, c in enumerate((0, 2)):
-            to[pl.ds(i * GX, GX), :] = v3[pl.ds(at(row + base, c), GX), :]
+    def put(e_ref, b_ref, row):
+        for j, ref in enumerate((v0, v1, v2, v3)):
+            for i, c in enumerate((0, 2)):
+                to = e_ref if j < 3 else b_ref
+                to[pl.ds((j % 3 * 2 + i) * GX, GX), :] = ref[pl.ds(at(row + base, c), GX), :]
 
     half, part = 768, 384
     core = lax.axis_index("col") % 2
@@ -249,8 +191,8 @@
         s01[...] = acc[pl.ds(part, part), :]
         s10[...] = acc[pl.ds(half, part), :]
         s11[...] = acc[pl.ds(half + part, part), :]
-        put(b0, 7)
-        put(b1, 0)
+        put(e0, b0, 7)
+        put(e1, b1, 0)
 
     @pl.when(core == 1)
     def _():
@@ -258,8 +200,8 @@
         s11[...] = acc[pl.ds(part, part), :]
         s00[...] = acc[pl.ds(half, part), :]
         s01[...] = acc[pl.ds(half + part, part), :]
-        put(b1, 7)
-        put(b0, 0)
+        put(e1, b1, 7)
+        put(e0, b0, 0)
 
 
 def whole(ref_shape):
@@ -282,11 +224,7 @@
     return pl.BlockSpec((rows, LANES), lambda i, *_: (0, i))
 
 
-def stacked(rows):
-    return pl.BlockSpec((rows, LANES), lambda i, *_: (i, 0))
-
-
-def rows_step(block, after, fields):
+def rows_step(block, fields):
     table = whole((GX, GX))
     buf = vmem(buffer_rows(12))
     return pl.pallas_call(
@@ -294,14 +232,14 @@
         grid_spec=pltpu.PrefetchScalarGridSpec(
             num_scalar_prefetch=0,
             grid=(3,),
-            in_specs=[lane_block(1536), pl.BlockSpec(memory_space=pl.ANY), table, table, table],
-            out_specs=[lane_block(384)] * 4 + [lane_block(128)] * 2,
+            in_specs=[lane_block(1536), table, table, table],
+            out_specs=[lane_block(384)] * 6 + [lane_block(128)] * 2,
             scratch_shapes=[pltpu.VMEM((12, 4, GX, LANES), jnp.float32), buf, buf, buf, buf, vmem(1536)],
         ),
-        out_shape=[shape(384, 384)] * 4 + [shape(128, 384)] * 2,
+        out_shape=[shape(384, 384)] * 6 + [shape(128, 384)] * 2,
         compiler_params=params(58),
         name="rows_step",
-    )(block, after, *fields)
+    )(block, *fields)
 
 
 def rows_response_kernel(scal, m0, m1, dep, cor, drag, *refs):
@@ -336,7 +274,7 @@
         grid_spec=pltpu.PrefetchScalarGridSpec(
             num_scalar_prefetch=1,
             grid=(3,),
-            in_specs=[stacked(384)] * 2 + [table] * 3,
+            in_specs=[lane_block(384)] * 2 + [table] * 3,
             out_specs=[lane_block(384)] * 4,
             scratch_shapes=[pltpu.VMEM((4, 4, GX, LANES), jnp.float32), buf, buf],
         ),
@@ -427,7 +365,7 @@
             in_specs=[pl.BlockSpec((LANES, 384), lambda i, *_: (i, 0))] * 4
             + [whole((128, 384))] * len(late)
             + [table] * 3,
-            out_specs=[stacked(768), stacked(512), stacked(512)],
+            out_specs=[lane_block(768), lane_block(512), lane_block(512)],
             scratch_shapes=[
                 pltpu.VMEM((8, 4, GX, LANES), jnp.float32),
                 *[buf] * 4,
@@ -435,7 +373,7 @@
                 vmem(2 * GX, 384),
             ],
         ),
-        out_shape=[shape(part * 6, LANES), shape(part * 4, LANES), shape(part * 4, LANES)],
+        out_shape=[shape(768, part), shape(512, part), shape(512, part)],
         compiler_params=params(24),
         name="columns_step",
     )(scal, s0, s1, r0, r1, *late, *fields)
@@ -487,7 +425,7 @@
         grid_spec=pltpu.PrefetchScalarGridSpec(
             num_scalar_prefetch=1,
             grid=(part // LANES,),
-            in_specs=[stacked(768), stacked(512), stacked(512)] + [table] * 3,
+            in_specs=[lane_block(768), lane_block(512), lane_block(512)] + [table] * 3,
             out_specs=[pl.BlockSpec((LANES, 384), lambda i, *_: (i, 0))] * 2,
             scratch_shapes=[pltpu.VMEM((4, 4, GX, LANES), jnp.float32), buf, buf, vmem(768)],
         ),
@@ -572,12 +510,13 @@
     def send(pair, pairs):
         return [lax.ppermute(v, both, pairs[k]) for k, v in enumerate(pair)]
 
-    edges = edge_step(covariance, fields)
-    early = send(edges, boundary)
-    s00, s01, s10, s11, b0, b1 = rows_step(covariance, edges[0], fields)
+    s00, s01, s10, s11, e0, e1, b0, b1 = rows_step(covariance, fields)
+    early = send((e0, e1), boundary)
     far = send((s00, s10), split)
     late = send((b0, b1), boundary)
-    near = send((s01, s11), split)
+    near = [lax.ppermute(s01, both, split[0])]
+    far[1], s11 = lax.optimization_barrier((far[1], s11))
+    near.append(lax.ppermute(s11, both, split[1]))
     rscal = jnp.stack([row * 8 + second * 4, second]).astype(jnp.int32)
     cscal = jnp.stack([(z * 2 + core) * 4, second, core, row * 8 + second * 4]).astype(jnp.int32)
     fscal = jnp.stack([row, core]).astype(jnp.int32)

time: 105 us -> 102 us (0.971)
  waiting for transfers between devices: 38.6 us -> 34.3 us
  starting transfers between devices: 35.8 us -> 39.5 us
  Pallas kernels: 29.8 us -> 27.5 us
    ppermute x12 -> x10, waiting for transfers between devices: 33.8 us -> 29.9 us  [send(): return [lax.ppermute(v, both, pairs[k]) for k, v in enumerate(pair)]]
    ppermute x12 -> x10, starting transfers between devices: 28.5 us -> 32.1 us  [send(): return [lax.ppermute(v, both, pairs[k]) for k, v in enumerate(pair)]]
    pallas_call x1 -> x0, Pallas kernels: 3.42 us -> none  [edge_step(): pl.pallas_call(edge_kernel, grid=(1,), in_specs=[pl.BlockSpec((192, 384),...]
    ppermute x2, starting transfers between devices: 3.5 us -> 1.68 us  [shards(): inside = lax.ppermute(inside, 'col', inner)]
    ppermute x0 -> x2, starting transfers between devices: none -> 1.71 us  [the longest x1 1.71 us: shards(): near = [lax.ppermute(s01, both, split[0])]]
  transfers between devices with their start and end apart: 16 -> 16, of which waited for: 6 -> 7; matrix products, arithmetic and copies ran while one was open for 0% -> 0% of each run, Pallas kernels for 24% -> 19%
where the time goes in v4:
time: 102 us
  starting transfers between devices  39.5 us (39%)
  waiting for transfers between devices  34.3 us (34%)
  Pallas kernels  27.5 us (27%)
    ppermute x10, starting transfers between devices, send(): return [lax.ppermute(v, both, pairs[k]) for k, v in enumerate(pair)]  32.1 us
    ppermute x10, waiting for transfers between devices, send(): return [lax.ppermute(v, both, pairs[k]) for k, v in enumerate(pair)]  29.9 us
    pallas_call x2, Pallas kernels, columns_step(): pl.pallas_call(columns_kernel, grid_spec=pltpu.PrefetchScalarGridSpec(num...  8.73 us
    pallas_call x1, Pallas kernels, rows_step(): pl.pallas_call(rows_kernel, grid_spec=pltpu.PrefetchScalarGridSpec(num_sc...  6.95 us
    pallas_call x2, Pallas kernels, columns_response(): pl.pallas_call(columns_response_kernel, grid_spec=pltpu.PrefetchScalarGri...  6.1 us
    ppermute x2, waiting for transfers between devices, shards(): outside = lax.ppermute(outside, 'col', outer)  4.42 us
    ppermute x2, starting transfers between devices, shards(): outside = lax.ppermute(outside, 'col', outer)  4.01 us
    pallas_call x2, Pallas kernels, finish_step(): pl.pallas_call(finish_kernel, grid_spec=pltpu.PrefetchScalarGridSpec(num_...  3.32 us
  transfers between devices with their start and end apart: 16, of which 7 were waited for; matrix products, arithmetic and copies ran while one was open for 0% of the time, Pallas kernels for 19%

profile of v4, /device:TPU:120, one launch (start us, length us, event | category | flops | bytes accessed | tf_op | source)
XLA Modules:
  0.0 101.7 jit_solution(8637766217961235373)
XLA Ops:
  0.0 6.9 %rows_step.1 = (f32[384,384]{1,0:T(8,128)}, f32[384,384]{1,0:T(8,128)}, f32[384,384]{1,0:T(8,128)}, f32[384,384]{1,0:T(8,128)}, f32[384,384]{1,0:T(8,128)}, /*in...) custom-call(f32[1536,384]{1,0:T(8,128)} %x_ref.1, f32[64,64]{1,0:T(8,128)} %dep.7, f32[64,64]{1,0:T(8,128)} %cor.7, ...), custom_call_target="tpu_custom_call" | custom-call | tf_op jit(solution)/shard_map/rows_step/pallas_call | solution.py:230
  8.5 4.6 %collective-permute-start.3 = (f32[384,384]{1,0:T(8,128)}, f32[384,384]{1,0:T(8,128)S(1)}, u32[]{:S(2)}, u32[]{:S(2)}) collective-permute-start(f32[384,384]{1,0:T(8,128)} %get-tuple-element.33), channel_id=1, source_target_pairs={{0,32},{2,33},{4,36},{6,37},{8,40},{10,41},{12,44},{14,45},{16,48}... | collective-permute-start | bytes 1769480 | tf_op jit(solution)/shard_map/ppermute | solution.py:511
  13.2 1.9 %collective-permute-start.4 = (f32[384,384]{1,0:T(8,128)}, f32[384,384]{1,0:T(8,128)S(1)}, u32[]{:S(2)}, u32[]{:S(2)}) collective-permute-start(f32[384,384]{1,0:T(8,128)} %get-tuple-element.34), channel_id=1, source_target_pairs={{1,32},{3,33},{5,36},{7,37},{9,40},{11,41},{13,44},{15,45},{17,48}... | collective-permute-start | bytes 1769480 | tf_op jit(solution)/shard_map/ppermute | solution.py:511
  15.1 6.0 %collective-permute-start.11 = (f32[384,384]{1,0:T(8,128)}, f32[384,384]{1,0:T(8,128)}, u32[]{:S(2)}, u32[]{:S(2)}) collective-permute-start(f32[384,384]{1,0:T(8,128)} %get-tuple-element.44), channel_id=1, source_target_pairs={{0,0},{1,2},{2,1},{3,3},{4,4},{5,6},{6,5},{7,7},{8,8},{9,10},{10,9... | collective-permute-start | bytes 1769480 | tf_op jit(solution)/shard_map/ppermute | solution.py:511
  21.1 1.7 %collective-permute-start = (f32[384,384]{1,0:T(8,128)}, f32[384,384]{1,0:T(8,128)S(1)}, u32[]{:S(2)}, u32[]{:S(2)}) collective-permute-start(f32[384,384]{1,0:T(8,128)} %get-tuple-element.29), channel_id=1, source_target_pairs={{0,0},{1,2},{2,1},{3,3},{4,4},{5,6},{6,5},{7,7},{8,8},{9,10},{10,9... | collective-permute-start | bytes 1769480 | tf_op jit(solution)/shard_map/ppermute | solution.py:517
  22.8 8.3 %collective-permute-done.3.m0 = f32[384,384]{1,0:T(8,128)S(1)} collective-permute-done((f32[384,384]{1,0:T(8,128)}, f32[384,384]{1,0:T(8,128)S(1)}, u32[]{:S(2)}, u32[]{:S(2)}) %collective-permute-start.3) | collective-permute-done | bytes 589856 | tf_op jit(solution)/shard_map/ppermute | solution.py:511
  31.1 4.5 %collective-permute-start.5 = (f32[128,384]{1,0:T(8,128)}, f32[128,384]{1,0:T(8,128)S(1)}, u32[]{:S(2)}, u32[]{:S(2)}) collective-permute-start(f32[128,384]{1,0:T(8,128)} %get-tuple-element.37), channel_id=1, source_target_pairs={{0,32},{2,33},{4,36},{6,37},{8,40},{10,41},{12,44},{14,45},{16,48}... | collective-permute-start | bytes 589832 | tf_op jit(solution)/shard_map/ppermute | solution.py:511
  35.6 2.4 %collective-permute-done.4.m1 = f32[384,384]{1,0:T(8,128)S(1)} collective-permute-done((f32[384,384]{1,0:T(8,128)}, f32[384,384]{1,0:T(8,128)S(1)}, u32[]{:S(2)}, u32[]{:S(2)}) %collective-permute-start.4) | collective-permute-done | bytes 589856 | tf_op jit(solution)/shard_map/ppermute | solution.py:511
  38.0 6.4 %collective-permute-start.6 = (f32[128,384]{1,0:T(8,128)}, f32[128,384]{1,0:T(8,128)S(1)}, u32[]{:S(2)}, u32[]{:S(2)}) collective-permute-start(f32[128,384]{1,0:T(8,128)} %get-tuple-element.38), channel_id=1, source_target_pairs={{1,32},{3,33},{5,36},{7,37},{9,40},{11,41},{13,44},{15,45},{17,48}... | collective-permute-start | bytes 589832 | tf_op jit(solution)/shard_map/ppermute | solution.py:511
  44.5 2.4 %rows_response.1 = (f32[384,384]{1,0:T(8,128)S(1)}, f32[384,384]{1,0:T(8,128)S(1)}, f32[384,384]{1,0:T(8,128)S(1)}, f32[384,384]{1,0:T(8,128)S(1)}) custom-call(s32[2]{0:T(128)S(1)} %pad_add_fusion.2.scal, f32[384,384]{1,0:T(8,128)S(1)} %collective-permute-done.3.m0, f32[384,384]{1,0:T(8,128)S(1)} %collective-permute-done.4.m1, f32[64,64]{1,0:T(8,128)S(1)} %copy-done.1, ...), custom_call_target="tpu_custom_call" | custom-call | tf_op jit(solution)/shard_map/rows_response/pallas_call | solution.py:272
  46.9 4.6 %columns_step.3 = (f32[768,384]{1,0:T(8,128)S(1)}, f32[512,384]{1,0:T(8,128)S(1)}, f32[512,384]{1,0:T(8,128)S(1)}) custom-call(s32[4]{0:T(128)S(1)} %pad_add_fusion.1.scal, f32[384,384]{1,0:T(8,128)} %collective-permute-done.11.s0, f32[384,384]{1,0:T(8,128)S(1)} %collective-permute-done.1.s1, f32[384,384]{1,0:T(8,128)S(1)} %get-tuple-element.46.r0, ...), custom_call_target="tpu_custom_call" | custom-call | tf_op jit(solution)/shard_map/columns_step/pallas_call | solution.py:360
  51.7 2.1 %collective-permute-start.13 = (f32[512,384]{1,0:T(8,128)S(1)}, f32[512,384]{1,0:T(8,128)S(1)}, u32[]{:S(2)}, u32[]{:S(2)}) collective-permute-start(f32[512,384]{1,0:T(8,128)S(1)} %get-tuple-element.50), channel_id=1, source_target_pairs={{1,4},{4,1},{3,6},{6,3},{5,8},{8,5},{7,10},{10,7},{9,12},{12,9},{1... | collective-permute-start | bytes 2359304 | tf_op jit(solution)/shard_map/ppermute | solution.py:527
  55.4 4.1 %columns_step.2 = (f32[768,384]{1,0:T(8,128)S(1)}, f32[512,384]{1,0:T(8,128)S(1)}, f32[512,384]{1,0:T(8,128)S(1)}) custom-call(s32[4]{0:T(128)S(1)} %pad_add_fusion.1.scal, f32[384,384]{1,0:T(8,128)S(1)} %collective-permute-done.s0, f32[384,384]{1,0:T(8,128)S(1)} %collective-permute-done.2.s1, f32[384,384]{1,0:T(8,128)S(1)} %get-tuple-element.35.r0, ...), custom_call_target="tpu_custom_call" | custom-call | tf_op jit(solution)/shard_map/columns_step/pallas_call | solution.py:360
  61.1 1.9 %collective-permute-start.8 = (f32[512,384]{1,0:T(8,128)S(1)}, f32[512,384]{1,0:T(8,128)S(1)}, u32[]{:S(2)}, u32[]{:S(2)}) collective-permute-start(f32[512,384]{1,0:T(8,128)S(1)} %get-tuple-element.41), channel_id=1, source_target_pairs={{1,4},{4,1},{3,6},{6,3},{5,8},{8,5},{7,10},{10,7},{9,12},{12,9},{1... | collective-permute-start | bytes 2359304 | tf_op jit(solution)/shard_map/ppermute | solution.py:527
  63.0 2.0 %collective-permute-done.13.outer = f32[512,384]{1,0:T(8,128)S(1)} collective-permute-done((f32[512,384]{1,0:T(8,128)S(1)}, f32[512,384]{1,0:T(8,128)S(1)}, u32[]{:S(2)}, u32[]{:S(2)}) %collective-permute-start.13) | collective-permute-done | bytes 786464 | tf_op jit(solution)/shard_map/ppermute | solution.py:527
  65.0 3.0 %columns_response.3 = (f32[384,384]{1,0:T(8,128)S(1)}, f32[384,384]{1,0:T(8,128)S(1)}) custom-call(s32[4]{0:T(128)S(1)} %pad_add_fusion.1.scal, f32[768,384]{1,0:T(8,128)S(1)} %get-tuple-element.48.own, f32[512,384]{1,0:T(8,128)S(1)} %collective-permute-done.12.inner, f32[512,384]{1,0:T(8,128)S(1)} %collective-permute-done.13.outer, f32[64,64]{1,0:T(8,128)S(1)} %copy-done.1, ...), custom_call_target="tpu_custom_call" | custom-call | tf_op jit(solution)/shard_map/columns_response/pallas_call | solution.py:423
  68.7 3.2 %collective-permute-start.15 = (f32[384,384]{1,0:T(8,128)S(1)}, f32[384,384]{1,0:T(8,128)S(1)}, u32[]{:S(2)}, u32[]{:S(2)}) collective-permute-start(f32[384,384]{1,0:T(8,128)S(1)} %get-tuple-element.52), channel_id=1, source_target_pairs={{0,1},{1,3},{2,0},{3,2},{4,5},{5,7},{6,4},{7,6},{8,9},{9,11},{10,8... | collective-permute-start | bytes 1769480 | tf_op jit(solution)/shard_map/ppermute | solution.py:511
  71.9 2.4 %collective-permute-done.8.outer = f32[512,384]{1,0:T(8,128)S(1)} collective-permute-done((f32[512,384]{1,0:T(8,128)S(1)}, f32[512,384]{1,0:T(8,128)S(1)}, u32[]{:S(2)}, u32[]{:S(2)}) %collective-permute-start.8) | collective-permute-done | bytes 786464 | tf_op jit(solution)/shard_map/ppermute | solution.py:527
  74.4 3.0 %columns_response.2 = (f32[384,384]{1,0:T(8,128)S(1)}, f32[384,384]{1,0:T(8,128)S(1)}) custom-call(s32[4]{0:T(128)S(1)} %pad_add_fusion.1.scal, f32[768,384]{1,0:T(8,128)S(1)} %get-tuple-element.39.own, f32[512,384]{1,0:T(8,128)S(1)} %collective-permute-done.7.inner, f32[512,384]{1,0:T(8,128)S(1)} %collective-permute-done.8.outer, f32[64,64]{1,0:T(8,128)S(1)} %copy-done.1, ...), custom_call_target="tpu_custom_call" | custom-call | tf_op jit(solution)/shard_map/columns_response/pallas_call | solution.py:423
  78.1 2.5 %collective-permute-start.10 = (f32[384,384]{1,0:T(8,128)S(1)}, f32[384,384]{1,0:T(8,128)S(1)}, u32[]{:S(2)}, u32[]{:S(2)}) collective-permute-start(f32[384,384]{1,0:T(8,128)S(1)} %get-tuple-element.43), channel_id=1, source_target_pairs={{0,1},{1,3},{2,0},{3,2},{4,5},{5,7},{6,4},{7,6},{8,9},{9,11},{10,8... | collective-permute-start | bytes 1769480 | tf_op jit(solution)/shard_map/ppermute | solution.py:511
  80.7 6.7 %collective-permute-done.15.z1 = f32[384,384]{1,0:T(8,128)S(1)} collective-permute-done((f32[384,384]{1,0:T(8,128)S(1)}, f32[384,384]{1,0:T(8,128)S(1)}, u32[]{:S(2)}, u32[]{:S(2)}) %collective-permute-start.15) | collective-permute-done | bytes 589856 | tf_op jit(solution)/shard_map/ppermute | solution.py:511
  87.4 1.7 %finish_step.2.rest_0_ = f32[1536,384]{1,0:T(8,128)} custom-call(s32[2]{0:T(128)S(1)} %pad_add_fusion.scal, f32[384,384]{1,0:T(8,128)S(1)} %collective-permute-done.14.z0, f32[384,384]{1,0:T(8,128)S(1)} %collective-permute-done.15.z1, f32[1536,384]{1,0:T(8,128)S(1)} %copy-done), custom_call_target="tpu_custom_call" | custom-call | tf_op jit(solution)/shard_map/finish_step/pallas_call | solution.py:461
  89.1 11.0 %collective-permute-done.10.z1 = f32[384,384]{1,0:T(8,128)S(1)} collective-permute-done((f32[384,384]{1,0:T(8,128)S(1)}, f32[384,384]{1,0:T(8,128)S(1)}, u32[]{:S(2)}, u32[]{:S(2)}) %collective-permute-start.10) | collective-permute-done | bytes 589856 | tf_op jit(solution)/shard_map/ppermute | solution.py:511
  100.1 1.7 %finish_step.3 = f32[1536,384]{1,0:T(8,128)} custom-call(s32[2]{0:T(128)S(1)} %pad_add_fusion.scal, f32[384,384]{1,0:T(8,128)S(1)} %collective-permute-done.9.z0, f32[384,384]{1,0:T(8,128)S(1)} %collective-permute-done.10.z1, f32[1536,384]{1,0:T(8,128)S(1)} %copy-done, f32[1536,384]{1,0:T(8,128)} %finish_step.2.rest_0_), custom_call_target="tpu_custom_call", output_to_operand_aliasing={{}: (4, {})} | custom-call | tf_op jit(solution)/shard_map/finish_step/pallas_call | solution.py:461
  (27 shorter events, 6.5 us)
Async XLA Ops:
  0.0 44.5 %copy-start.3 = (f32[64,64]{1,0:T(8,128)S(1)}, f32[64,64]{1,0:T(8,128)}, u32[]{:S(2)}) copy-start(f32[64,64]{1,0:T(8,128)} %drag.7) | copy-start | bytes 49156
  0.0 44.5 %copy-start.2 = (f32[64,64]{1,0:T(8,128)S(1)}, f32[64,64]{1,0:T(8,128)}, u32[]{:S(2)}) copy-start(f32[64,64]{1,0:T(8,128)} %cor.7) | copy-start | bytes 49156
  0.0 44.5 %copy-start.1 = (f32[64,64]{1,0:T(8,128)S(1)}, f32[64,64]{1,0:T(8,128)}, u32[]{:S(2)}) copy-start(f32[64,64]{1,0:T(8,128)} %dep.7) | copy-start | bytes 49156
  7.0 15.8 %collective-permute-start.1 = (f32[384,384]{1,0:T(8,128)}, f32[384,384]{1,0:T(8,128)S(1)}, u32[]{:S(2)}, u32[]{:S(2)}) collective-permute-start(f32[384,384]{1,0:T(8,128)} %get-tuple-element.30), channel_id=1, source_target_pairs={{0,2},{1,0},{2,3},{3,1},{4,6},{5,4},{6,7},{7,5},{8,10},{9,8},{10,1... | collective-permute-start | bytes 1769480 | tf_op jit(solution)/shard_map/ppermute | solution.py:511
  8.5 22.5 %collective-permute-start.3 = (f32[384,384]{1,0:T(8,128)}, f32[384,384]{1,0:T(8,128)S(1)}, u32[]{:S(2)}, u32[]{:S(2)}) collective-permute-start(f32[384,384]{1,0:T(8,128)} %get-tuple-element.33), channel_id=1, source_target_pairs={{0,32},{2,33},{4,36},{6,37},{8,40},{10,41},{12,44},{14,45},{16,48}... | collective-permute-start | bytes 1769480 | tf_op jit(solution)/shard_map/ppermute | solution.py:511
  13.2 24.8 %collective-permute-start.4 = (f32[384,384]{1,0:T(8,128)}, f32[384,384]{1,0:T(8,128)S(1)}, u32[]{:S(2)}, u32[]{:S(2)}) collective-permute-start(f32[384,384]{1,0:T(8,128)} %get-tuple-element.34), channel_id=1, source_target_pairs={{1,32},{3,33},{5,36},{7,37},{9,40},{11,41},{13,44},{15,45},{17,48}... | collective-permute-start | bytes 1769480 | tf_op jit(solution)/shard_map/ppermute | solution.py:511
  15.1 31.8 %collective-permute-start.11 = (f32[384,384]{1,0:T(8,128)}, f32[384,384]{1,0:T(8,128)}, u32[]{:S(2)}, u32[]{:S(2)}) collective-permute-start(f32[384,384]{1,0:T(8,128)} %get-tuple-element.44), channel_id=1, source_target_pairs={{0,0},{1,2},{2,1},{3,3},{4,4},{5,6},{6,5},{7,7},{8,8},{9,10},{10,9... | collective-permute-start | bytes 1769480 | tf_op jit(solution)/shard_map/ppermute | solution.py:511
  21.1 34.3 %collective-permute-start = (f32[384,384]{1,0:T(8,128)}, f32[384,384]{1,0:T(8,128)S(1)}, u32[]{:S(2)}, u32[]{:S(2)}) collective-permute-start(f32[384,384]{1,0:T(8,128)} %get-tuple-element.29), channel_id=1, source_target_pairs={{0,0},{1,2},{2,1},{3,3},{4,4},{5,6},{6,5},{7,7},{8,8},{9,10},{10,9... | collective-permute-start | bytes 1769480 | tf_op jit(solution)/shard_map/ppermute | solution.py:517
  22.8 32.6 %collective-permute-start.2 = (f32[384,384]{1,0:T(8,128)}, f32[384,384]{1,0:T(8,128)S(1)}, u32[]{:S(2)}, u32[]{:S(2)}) collective-permute-start(f32[384,384]{1,0:T(8,128)} %get-tuple-element.32), channel_id=1, source_target_pairs={{0,2},{1,0},{2,3},{3,1},{4,6},{5,4},{6,7},{7,5},{8,10},{9,8},{10,1... | collective-permute-start | bytes 1769480 | tf_op jit(solution)/shard_map/ppermute | solution.py:519
  31.1 20.6 %collective-permute-start.5 = (f32[128,384]{1,0:T(8,128)}, f32[128,384]{1,0:T(8,128)S(1)}, u32[]{:S(2)}, u32[]{:S(2)}) collective-permute-start(f32[128,384]{1,0:T(8,128)} %get-tuple-element.37), channel_id=1, source_target_pairs={{0,32},{2,33},{4,36},{6,37},{8,40},{10,41},{12,44},{14,45},{16,48}... | collective-permute-start | bytes 589832 | tf_op jit(solution)/shard_map/ppermute | solution.py:511
  38.0 17.4 %collective-permute-start.6 = (f32[128,384]{1,0:T(8,128)}, f32[128,384]{1,0:T(8,128)S(1)}, u32[]{:S(2)}, u32[]{:S(2)}) collective-permute-start(f32[128,384]{1,0:T(8,128)} %get-tuple-element.38), channel_id=1, source_target_pairs={{1,32},{3,33},{5,36},{7,37},{9,40},{11,41},{13,44},{15,45},{17,48}... | collective-permute-start | bytes 589832 | tf_op jit(solution)/shard_map/ppermute | solution.py:511
  51.6 11.4 %collective-permute-start.12 = (f32[512,384]{1,0:T(8,128)S(1)}, f32[512,384]{1,0:T(8,128)S(1)}, u32[]{:S(2)}, u32[]{:S(2)}) collective-permute-start(f32[512,384]{1,0:T(8,128)S(1)} %get-tuple-element.49), channel_id=1, source_target_pairs={{0,1},{1,0},{2,3},{3,2},{4,5},{5,4},{6,7},{7,6},{8,9},{9,8},{10,11... | collective-permute-start | bytes 2359304 | tf_op jit(solution)/shard_map/ppermute | solution.py:528
  51.7 13.3 %collective-permute-start.13 = (f32[512,384]{1,0:T(8,128)S(1)}, f32[512,384]{1,0:T(8,128)S(1)}, u32[]{:S(2)}, u32[]{:S(2)}) collective-permute-start(f32[512,384]{1,0:T(8,128)S(1)} %get-tuple-element.50), channel_id=1, source_target_pairs={{1,4},{4,1},{3,6},{6,3},{5,8},{8,5},{7,10},{10,7},{9,12},{12,9},{1... | collective-permute-start | bytes 2359304 | tf_op jit(solution)/shard_map/ppermute | solution.py:527
  59.5 12.5 %collective-permute-start.7 = (f32[512,384]{1,0:T(8,128)S(1)}, f32[512,384]{1,0:T(8,128)S(1)}, u32[]{:S(2)}, u32[]{:S(2)}) collective-permute-start(f32[512,384]{1,0:T(8,128)S(1)} %get-tuple-element.40), channel_id=1, source_target_pairs={{0,1},{1,0},{2,3},{3,2},{4,5},{5,4},{6,7},{7,6},{8,9},{9,8},{10,11... | collective-permute-start | bytes 2359304 | tf_op jit(solution)/shard_map/ppermute | solution.py:528
  61.1 13.3 %collective-permute-start.8 = (f32[512,384]{1,0:T(8,128)S(1)}, f32[512,384]{1,0:T(8,128)S(1)}, u32[]{:S(2)}, u32[]{:S(2)}) collective-permute-start(f32[512,384]{1,0:T(8,128)S(1)} %get-tuple-element.41), channel_id=1, source_target_pairs={{1,4},{4,1},{3,6},{6,3},{5,8},{8,5},{7,10},{10,7},{9,12},{12,9},{1... | collective-permute-start | bytes 2359304 | tf_op jit(solution)/shard_map/ppermute | solution.py:527
  65.0 22.5 %copy-start = (f32[1536,384]{1,0:T(8,128)S(1)}, f32[1536,384]{1,0:T(8,128)}, u32[]{:S(2)}) copy-start(f32[1536,384]{1,0:T(8,128)} %noise.3) | copy-start | bytes 7077892
  68.0 12.7 %collective-permute-start.14 = (f32[384,384]{1,0:T(8,128)S(1)}, f32[384,384]{1,0:T(8,128)S(1)}, u32[]{:S(2)}, u32[]{:S(2)}) collective-permute-start(f32[384,384]{1,0:T(8,128)S(1)} %get-tuple-element.51), channel_id=1, source_target_pairs={{0,0},{1,2},{2,1},{3,3},{4,4},{5,6},{6,5},{7,7},{8,8},{9,10},{10,9... | collective-permute-start | bytes 1769480 | tf_op jit(solution)/shard_map/ppermute | solution.py:511
  68.7 18.7 %collective-permute-start.15 = (f32[384,384]{1,0:T(8,128)S(1)}, f32[384,384]{1,0:T(8,128)S(1)}, u32[]{:S(2)}, u32[]{:S(2)}) collective-permute-start(f32[384,384]{1,0:T(8,128)S(1)} %get-tuple-element.52), channel_id=1, source_target_pairs={{0,1},{1,3},{2,0},{3,2},{4,5},{5,7},{6,4},{7,6},{8,9},{9,11},{10,8... | collective-permute-start | bytes 1769480 | tf_op jit(solution)/shard_map/ppermute | solution.py:511
  77.4 11.7 %collective-permute-start.9 = (f32[384,384]{1,0:T(8,128)S(1)}, f32[384,384]{1,0:T(8,128)S(1)}, u32[]{:S(2)}, u32[]{:S(2)}) collective-permute-start(f32[384,384]{1,0:T(8,128)S(1)} %get-tuple-element.42), channel_id=1, source_target_pairs={{0,0},{1,2},{2,1},{3,3},{4,4},{5,6},{6,5},{7,7},{8,8},{9,10},{10,9... | collective-permute-start | bytes 1769480 | tf_op jit(solution)/shard_map/ppermute | solution.py:511
  78.1 22.0 %collective-permute-start.10 = (f32[384,384]{1,0:T(8,128)S(1)}, f32[384,384]{1,0:T(8,128)S(1)}, u32[]{:S(2)}, u32[]{:S(2)}) collective-permute-start(f32[384,384]{1,0:T(8,128)S(1)} %get-tuple-element.43), channel_id=1, source_target_pairs={{0,1},{1,3},{2,0},{3,2},{4,5},{5,7},{6,4},{7,6},{8,9},{9,11},{10,8... | collective-permute-start | bytes 1769480 | tf_op jit(solution)/shard_map/ppermute | solution.py:511

commit v5 on v4

--- a/solution.py
+++ b/solution.py
@@ -224,6 +224,10 @@
     return pl.BlockSpec((rows, LANES), lambda i, *_: (0, i))
 
 
+def stacked(rows):
+    return pl.BlockSpec((rows, LANES), lambda i, *_: (i, 0))
+
+
 def rows_step(block, fields):
     table = whole((GX, GX))
     buf = vmem(buffer_rows(12))
@@ -365,7 +369,7 @@
             in_specs=[pl.BlockSpec((LANES, 384), lambda i, *_: (i, 0))] * 4
             + [whole((128, 384))] * len(late)
             + [table] * 3,
-            out_specs=[lane_block(768), lane_block(512), lane_block(512)],
+            out_specs=[stacked(768), stacked(512), stacked(512)],
             scratch_shapes=[
                 pltpu.VMEM((8, 4, GX, LANES), jnp.float32),
                 *[buf] * 4,
@@ -373,7 +377,7 @@
                 vmem(2 * GX, 384),
             ],
         ),
-        out_shape=[shape(768, part), shape(512, part), shape(512, part)],
+        out_shape=[shape(part * 6, LANES), shape(part * 4, LANES), shape(part * 4, LANES)],
         compiler_params=params(24),
         name="columns_step",
     )(scal, s0, s1, r0, r1, *late, *fields)
@@ -425,7 +429,7 @@
         grid_spec=pltpu.PrefetchScalarGridSpec(
             num_scalar_prefetch=1,
             grid=(part // LANES,),
-            in_specs=[lane_block(768), lane_block(512), lane_block(512)] + [table] * 3,
+            in_specs=[stacked(768), stacked(512), stacked(512)] + [table] * 3,
             out_specs=[pl.BlockSpec((LANES, 384), lambda i, *_: (i, 0))] * 2,
             scratch_shapes=[pltpu.VMEM((4, 4, GX, LANES), jnp.float32), buf, buf, vmem(768)],
         ),

time: 102 us -> 102 us (level)
  transfers between devices with their start and end apart: 16 -> 16, of which waited for: 7 -> 7; matrix products, arithmetic and copies ran while one was open for 0% -> 0% of each run, Pallas kernels for 19% -> 18%
where the time goes in v5:
time: 102 us; the launch traced here: 101 us
  starting transfers between devices  39.2 us (38%)
  waiting for transfers between devices  35 us (34%)
  Pallas kernels  26.8 us (26%)
    ppermute x10, starting transfers between devices, send(): return [lax.ppermute(v, both, pairs[k]) for k, v in enumerate(pair)]  31.9 us
    ppermute x10, waiting for transfers between devices, send(): return [lax.ppermute(v, both, pairs[k]) for k, v in enumerate(pair)]  30.2 us
    pallas_call x2, Pallas kernels, columns_step(): pl.pallas_call(columns_kernel, grid_spec=pltpu.PrefetchScalarGridSpec(num...  8.39 us
    pallas_call x1, Pallas kernels, rows_step(): pl.pallas_call(rows_kernel, grid_spec=pltpu.PrefetchScalarGridSpec(num_sc...  6.95 us
    pallas_call x2, Pallas kernels, columns_response(): pl.pallas_call(columns_response_kernel, grid_spec=pltpu.PrefetchScalarGri...  5.71 us
    ppermute x2, waiting for transfers between devices, shards(): outside = lax.ppermute(outside, 'col', outer)  4.8 us
    ppermute x2, starting transfers between devices, shards(): outside = lax.ppermute(outside, 'col', outer)  4.01 us
    pallas_call x2, Pallas kernels, finish_step(): pl.pallas_call(finish_kernel, grid_spec=pltpu.PrefetchScalarGridSpec(num_...  3.32 us
  transfers between devices with their start and end apart: 16, of which 7 were waited for; matrix products, arithmetic and copies ran while one was open for 0% of the time, Pallas kernels for 18%

profile of v5, /device:TPU:120, one launch (start us, length us, event | category | flops | bytes accessed | tf_op | source)
XLA Modules:
  0.0 101.4 jit_solution(16192879047206029656)
XLA Ops:
  0.0 6.9 %rows_step.1 = (f32[384,384]{1,0:T(8,128)}, f32[384,384]{1,0:T(8,128)}, f32[384,384]{1,0:T(8,128)}, f32[384,384]{1,0:T(8,128)}, f32[384,384]{1,0:T(8,128)}, /*in...) custom-call(f32[1536,384]{1,0:T(8,128)} %x_ref.1, f32[64,64]{1,0:T(8,128)} %dep.7, f32[64,64]{1,0:T(8,128)} %cor.7, ...), custom_call_target="tpu_custom_call" | custom-call | tf_op jit(solution)/shard_map/rows_step/pallas_call | solution.py:234
  8.5 4.6 %collective-permute-start.3 = (f32[384,384]{1,0:T(8,128)}, f32[384,384]{1,0:T(8,128)S(1)}, u32[]{:S(2)}, u32[]{:S(2)}) collective-permute-start(f32[384,384]{1,0:T(8,128)} %get-tuple-element.33), channel_id=1, source_target_pairs={{0,32},{2,33},{4,36},{6,37},{8,40},{10,41},{12,44},{14,45},{16,48}... | collective-permute-start | bytes 1769480 | tf_op jit(solution)/shard_map/ppermute | solution.py:515
  13.2 1.9 %collective-permute-start.4 = (f32[384,384]{1,0:T(8,128)}, f32[384,384]{1,0:T(8,128)S(1)}, u32[]{:S(2)}, u32[]{:S(2)}) collective-permute-start(f32[384,384]{1,0:T(8,128)} %get-tuple-element.34), channel_id=1, source_target_pairs={{1,32},{3,33},{5,36},{7,37},{9,40},{11,41},{13,44},{15,45},{17,48}... | collective-permute-start | bytes 1769480 | tf_op jit(solution)/shard_map/ppermute | solution.py:515
  15.1 6.0 %collective-permute-start.11 = (f32[384,384]{1,0:T(8,128)}, f32[384,384]{1,0:T(8,128)}, u32[]{:S(2)}, u32[]{:S(2)}) collective-permute-start(f32[384,384]{1,0:T(8,128)} %get-tuple-element.44), channel_id=1, source_target_pairs={{0,0},{1,2},{2,1},{3,3},{4,4},{5,6},{6,5},{7,7},{8,8},{9,10},{10,9... | collective-permute-start | bytes 1769480 | tf_op jit(solution)/shard_map/ppermute | solution.py:515
  21.1 1.7 %collective-permute-start = (f32[384,384]{1,0:T(8,128)}, f32[384,384]{1,0:T(8,128)S(1)}, u32[]{:S(2)}, u32[]{:S(2)}) collective-permute-start(f32[384,384]{1,0:T(8,128)} %get-tuple-element.29), channel_id=1, source_target_pairs={{0,0},{1,2},{2,1},{3,3},{4,4},{5,6},{6,5},{7,7},{8,8},{9,10},{10,9... | collective-permute-start | bytes 1769480 | tf_op jit(solution)/shard_map/ppermute | solution.py:521
  22.8 8.3 %collective-permute-done.3.m0 = f32[384,384]{1,0:T(8,128)S(1)} collective-permute-done((f32[384,384]{1,0:T(8,128)}, f32[384,384]{1,0:T(8,128)S(1)}, u32[]{:S(2)}, u32[]{:S(2)}) %collective-permute-start.3) | collective-permute-done | bytes 589856 | tf_op jit(solution)/shard_map/ppermute | solution.py:515
  31.1 4.5 %collective-permute-start.5 = (f32[128,384]{1,0:T(8,128)}, f32[128,384]{1,0:T(8,128)S(1)}, u32[]{:S(2)}, u32[]{:S(2)}) collective-permute-start(f32[128,384]{1,0:T(8,128)} %get-tuple-element.37), channel_id=1, source_target_pairs={{0,32},{2,33},{4,36},{6,37},{8,40},{10,41},{12,44},{14,45},{16,48}... | collective-permute-start | bytes 589832 | tf_op jit(solution)/shard_map/ppermute | solution.py:515
  35.6 2.4 %collective-permute-done.4.m1 = f32[384,384]{1,0:T(8,128)S(1)} collective-permute-done((f32[384,384]{1,0:T(8,128)}, f32[384,384]{1,0:T(8,128)S(1)}, u32[]{:S(2)}, u32[]{:S(2)}) %collective-permute-start.4) | collective-permute-done | bytes 589856 | tf_op jit(solution)/shard_map/ppermute | solution.py:515
  38.0 6.4 %collective-permute-start.6 = (f32[128,384]{1,0:T(8,128)}, f32[128,384]{1,0:T(8,128)S(1)}, u32[]{:S(2)}, u32[]{:S(2)}) collective-permute-start(f32[128,384]{1,0:T(8,128)} %get-tuple-element.38), channel_id=1, source_target_pairs={{1,32},{3,33},{5,36},{7,37},{9,40},{11,41},{13,44},{15,45},{17,48}... | collective-permute-start | bytes 589832 | tf_op jit(solution)/shard_map/ppermute | solution.py:515
  44.5 2.4 %rows_response.1 = (f32[384,384]{1,0:T(8,128)S(1)}, f32[384,384]{1,0:T(8,128)S(1)}, f32[384,384]{1,0:T(8,128)S(1)}, f32[384,384]{1,0:T(8,128)S(1)}) custom-call(s32[2]{0:T(128)S(1)} %pad_add_fusion.2.scal, f32[384,384]{1,0:T(8,128)S(1)} %collective-permute-done.3.m0, f32[384,384]{1,0:T(8,128)S(1)} %collective-permute-done.4.m1, f32[64,64]{1,0:T(8,128)S(1)} %copy-done.1, ...), custom_call_target="tpu_custom_call" | custom-call | tf_op jit(solution)/shard_map/rows_response/pallas_call | solution.py:276
  46.9 4.5 %columns_step.3 = (f32[2304,128]{1,0:T(8,128)S(1)}, f32[1536,128]{1,0:T(8,128)S(1)}, f32[1536,128]{1,0:T(8,128)S(1)}) custom-call(s32[4]{0:T(128)S(1)} %pad_add_fusion.1.scal, f32[384,384]{1,0:T(8,128)} %collective-permute-done.11.s0, f32[384,384]{1,0:T(8,128)S(1)} %collective-permute-done.1.s1, f32[384,384]{1,0:T(8,128)S(1)} %get-tuple-element.46.r0, ...), custom_call_target="tpu_custom_call" | custom-call | tf_op jit(solution)/shard_map/columns_step/pallas_call | solution.py:364
  51.5 2.1 %collective-permute-start.13 = (f32[1536,128]{1,0:T(8,128)S(1)}, f32[1536,128]{1,0:T(8,128)S(1)}, u32[]{:S(2)}, u32[]{:S(2)}) collective-permute-start(f32[1536,128]{1,0:T(8,128)S(1)} %get-tuple-element.50), channel_id=1, source_target_pairs={{1,4},{4,1},{3,6},{6,3},{5,8},{8,5},{7,10},{10,7},{9,12},{12,9},{1... | collective-permute-start | bytes 2359304 | tf_op jit(solution)/shard_map/ppermute | solution.py:531
  53.7 1.7 %collective-permute-done.6.refs_1_ = f32[128,384]{1,0:T(8,128)S(1)} collective-permute-done((f32[128,384]{1,0:T(8,128)}, f32[128,384]{1,0:T(8,128)S(1)}, u32[]{:S(2)}, u32[]{:S(2)}) %collective-permute-start.6) | collective-permute-done | bytes 196640 | tf_op jit(solution)/shard_map/ppermute | solution.py:515
  55.4 3.9 %columns_step.2 = (f32[2304,128]{1,0:T(8,128)S(1)}, f32[1536,128]{1,0:T(8,128)S(1)}, f32[1536,128]{1,0:T(8,128)S(1)}) custom-call(s32[4]{0:T(128)S(1)} %pad_add_fusion.1.scal, f32[384,384]{1,0:T(8,128)S(1)} %collective-permute-done.s0, f32[384,384]{1,0:T(8,128)S(1)} %collective-permute-done.2.s1, f32[384,384]{1,0:T(8,128)S(1)} %get-tuple-element.35.r0, ...), custom_call_target="tpu_custom_call" | custom-call | tf_op jit(solution)/shard_map/columns_step/pallas_call | solution.py:364
  60.7 1.9 %collective-permute-start.8 = (f32[1536,128]{1,0:T(8,128)S(1)}, f32[1536,128]{1,0:T(8,128)S(1)}, u32[]{:S(2)}, u32[]{:S(2)}) collective-permute-start(f32[1536,128]{1,0:T(8,128)S(1)} %get-tuple-element.41), channel_id=1, source_target_pairs={{1,4},{4,1},{3,6},{6,3},{5,8},{8,5},{7,10},{10,7},{9,12},{12,9},{1... | collective-permute-start | bytes 2359304 | tf_op jit(solution)/shard_map/ppermute | solution.py:531
  62.7 2.2 %collective-permute-done.13.outer = f32[1536,128]{1,0:T(8,128)S(1)} collective-permute-done((f32[1536,128]{1,0:T(8,128)S(1)}, f32[1536,128]{1,0:T(8,128)S(1)}, u32[]{:S(2)}, u32[]{:S(2)}) %collective-permute-start.13) | collective-permute-done | bytes 786464 | tf_op jit(solution)/shard_map/ppermute | solution.py:531
  64.9 2.9 %columns_response.3 = (f32[384,384]{1,0:T(8,128)S(1)}, f32[384,384]{1,0:T(8,128)S(1)}) custom-call(s32[4]{0:T(128)S(1)} %pad_add_fusion.1.scal, f32[2304,128]{1,0:T(8,128)S(1)} %get-tuple-element.48.own, f32[1536,128]{1,0:T(8,128)S(1)} %collective-permute-done.12.inner, f32[1536,128]{1,0:T(8,128)S(1)} %collective-permute-done.13.outer, ...), custom_call_target="tpu_custom_call" | custom-call | tf_op jit(solution)/shard_map/columns_response/pallas_call | solution.py:427
  68.4 3.0 %collective-permute-start.15 = (f32[384,384]{1,0:T(8,128)S(1)}, f32[384,384]{1,0:T(8,128)S(1)}, u32[]{:S(2)}, u32[]{:S(2)}) collective-permute-start(f32[384,384]{1,0:T(8,128)S(1)} %get-tuple-element.52), channel_id=1, source_target_pairs={{0,1},{1,3},{2,0},{3,2},{4,5},{5,7},{6,4},{7,6},{8,9},{9,11},{10,8... | collective-permute-start | bytes 1769480 | tf_op jit(solution)/shard_map/ppermute | solution.py:515
  71.4 2.6 %collective-permute-done.8.outer = f32[1536,128]{1,0:T(8,128)S(1)} collective-permute-done((f32[1536,128]{1,0:T(8,128)S(1)}, f32[1536,128]{1,0:T(8,128)S(1)}, u32[]{:S(2)}, u32[]{:S(2)}) %collective-permute-start.8) | collective-permute-done | bytes 786464 | tf_op jit(solution)/shard_map/ppermute | solution.py:531
  74.0 2.9 %columns_response.2 = (f32[384,384]{1,0:T(8,128)S(1)}, f32[384,384]{1,0:T(8,128)S(1)}) custom-call(s32[4]{0:T(128)S(1)} %pad_add_fusion.1.scal, f32[2304,128]{1,0:T(8,128)S(1)} %get-tuple-element.39.own, f32[1536,128]{1,0:T(8,128)S(1)} %collective-permute-done.7.inner, f32[1536,128]{1,0:T(8,128)S(1)} %collective-permute-done.8.outer, ...), custom_call_target="tpu_custom_call" | custom-call | tf_op jit(solution)/shard_map/columns_response/pallas_call | solution.py:427
  77.6 2.5 %collective-permute-start.10 = (f32[384,384]{1,0:T(8,128)S(1)}, f32[384,384]{1,0:T(8,128)S(1)}, u32[]{:S(2)}, u32[]{:S(2)}) collective-permute-start(f32[384,384]{1,0:T(8,128)S(1)} %get-tuple-element.43), channel_id=1, source_target_pairs={{0,1},{1,3},{2,0},{3,2},{4,5},{5,7},{6,4},{7,6},{8,9},{9,11},{10,8... | collective-permute-start | bytes 1769480 | tf_op jit(solution)/shard_map/ppermute | solution.py:515
  80.2 6.9 %collective-permute-done.15.z1 = f32[384,384]{1,0:T(8,128)S(1)} collective-permute-done((f32[384,384]{1,0:T(8,128)S(1)}, f32[384,384]{1,0:T(8,128)S(1)}, u32[]{:S(2)}, u32[]{:S(2)}) %collective-permute-start.15) | collective-permute-done | bytes 589856 | tf_op jit(solution)/shard_map/ppermute | solution.py:515
  88.8 11.0 %collective-permute-done.10.z1 = f32[384,384]{1,0:T(8,128)S(1)} collective-permute-done((f32[384,384]{1,0:T(8,128)S(1)}, f32[384,384]{1,0:T(8,128)S(1)}, u32[]{:S(2)}, u32[]{:S(2)}) %collective-permute-start.10) | collective-permute-done | bytes 589856 | tf_op jit(solution)/shard_map/ppermute | solution.py:515
  99.7 1.7 %finish_step.3 = f32[1536,384]{1,0:T(8,128)} custom-call(s32[2]{0:T(128)S(1)} %pad_add_fusion.scal, f32[384,384]{1,0:T(8,128)S(1)} %collective-permute-done.9.z0, f32[384,384]{1,0:T(8,128)S(1)} %collective-permute-done.10.z1, f32[1536,384]{1,0:T(8,128)S(1)} %copy-done, f32[1536,384]{1,0:T(8,128)} %finish_step.2.rest_0_), custom_call_target="tpu_custom_call", output_to_operand_aliasing={{}: (4, {})} | custom-call | tf_op jit(solution)/shard_map/finish_step/pallas_call | solution.py:465
  (27 shorter events, 6.4 us)
Async XLA Ops:
  0.0 44.5 %copy-start.3 = (f32[64,64]{1,0:T(8,128)S(1)}, f32[64,64]{1,0:T(8,128)}, u32[]{:S(2)}) copy-start(f32[64,64]{1,0:T(8,128)} %drag.7) | copy-start | bytes 49156
  0.0 44.5 %copy-start.2 = (f32[64,64]{1,0:T(8,128)S(1)}, f32[64,64]{1,0:T(8,128)}, u32[]{:S(2)}) copy-start(f32[64,64]{1,0:T(8,128)} %cor.7) | copy-start | bytes 49156
  0.0 44.5 %copy-start.1 = (f32[64,64]{1,0:T(8,128)S(1)}, f32[64,64]{1,0:T(8,128)}, u32[]{:S(2)}) copy-start(f32[64,64]{1,0:T(8,128)} %dep.7) | copy-start | bytes 49156
  7.0 15.8 %collective-permute-start.1 = (f32[384,384]{1,0:T(8,128)}, f32[384,384]{1,0:T(8,128)S(1)}, u32[]{:S(2)}, u32[]{:S(2)}) collective-permute-start(f32[384,384]{1,0:T(8,128)} %get-tuple-element.30), channel_id=1, source_target_pairs={{0,2},{1,0},{2,3},{3,1},{4,6},{5,4},{6,7},{7,5},{8,10},{9,8},{10,1... | collective-permute-start | bytes 1769480 | tf_op jit(solution)/shard_map/ppermute | solution.py:515
  8.5 22.5 %collective-permute-start.3 = (f32[384,384]{1,0:T(8,128)}, f32[384,384]{1,0:T(8,128)S(1)}, u32[]{:S(2)}, u32[]{:S(2)}) collective-permute-start(f32[384,384]{1,0:T(8,128)} %get-tuple-element.33), channel_id=1, source_target_pairs={{0,32},{2,33},{4,36},{6,37},{8,40},{10,41},{12,44},{14,45},{16,48}... | collective-permute-start | bytes 1769480 | tf_op jit(solution)/shard_map/ppermute | solution.py:515
  13.2 24.8 %collective-permute-start.4 = (f32[384,384]{1,0:T(8,128)}, f32[384,384]{1,0:T(8,128)S(1)}, u32[]{:S(2)}, u32[]{:S(2)}) collective-permute-start(f32[384,384]{1,0:T(8,128)} %get-tuple-element.34), channel_id=1, source_target_pairs={{1,32},{3,33},{5,36},{7,37},{9,40},{11,41},{13,44},{15,45},{17,48}... | collective-permute-start | bytes 1769480 | tf_op jit(solution)/shard_map/ppermute | solution.py:515
  15.1 31.8 %collective-permute-start.11 = (f32[384,384]{1,0:T(8,128)}, f32[384,384]{1,0:T(8,128)}, u32[]{:S(2)}, u32[]{:S(2)}) collective-permute-start(f32[384,384]{1,0:T(8,128)} %get-tuple-element.44), channel_id=1, source_target_pairs={{0,0},{1,2},{2,1},{3,3},{4,4},{5,6},{6,5},{7,7},{8,8},{9,10},{10,9... | collective-permute-start | bytes 1769480 | tf_op jit(solution)/shard_map/ppermute | solution.py:515
  21.1 34.3 %collective-permute-start = (f32[384,384]{1,0:T(8,128)}, f32[384,384]{1,0:T(8,128)S(1)}, u32[]{:S(2)}, u32[]{:S(2)}) collective-permute-start(f32[384,384]{1,0:T(8,128)} %get-tuple-element.29), channel_id=1, source_target_pairs={{0,0},{1,2},{2,1},{3,3},{4,4},{5,6},{6,5},{7,7},{8,8},{9,10},{10,9... | collective-permute-start | bytes 1769480 | tf_op jit(solution)/shard_map/ppermute | solution.py:521
  22.8 32.6 %collective-permute-start.2 = (f32[384,384]{1,0:T(8,128)}, f32[384,384]{1,0:T(8,128)S(1)}, u32[]{:S(2)}, u32[]{:S(2)}) collective-permute-start(f32[384,384]{1,0:T(8,128)} %get-tuple-element.32), channel_id=1, source_target_pairs={{0,2},{1,0},{2,3},{3,1},{4,6},{5,4},{6,7},{7,5},{8,10},{9,8},{10,1... | collective-permute-start | bytes 1769480 | tf_op jit(solution)/shard_map/ppermute | solution.py:523
  31.1 20.5 %collective-permute-start.5 = (f32[128,384]{1,0:T(8,128)}, f32[128,384]{1,0:T(8,128)S(1)}, u32[]{:S(2)}, u32[]{:S(2)}) collective-permute-start(f32[128,384]{1,0:T(8,128)} %get-tuple-element.37), channel_id=1, source_target_pairs={{0,32},{2,33},{4,36},{6,37},{8,40},{10,41},{12,44},{14,45},{16,48}... | collective-permute-start | bytes 589832 | tf_op jit(solution)/shard_map/ppermute | solution.py:515
  38.0 17.4 %collective-permute-start.6 = (f32[128,384]{1,0:T(8,128)}, f32[128,384]{1,0:T(8,128)S(1)}, u32[]{:S(2)}, u32[]{:S(2)}) collective-permute-start(f32[128,384]{1,0:T(8,128)} %get-tuple-element.38), channel_id=1, source_target_pairs={{1,32},{3,33},{5,36},{7,37},{9,40},{11,41},{13,44},{15,45},{17,48}... | collective-permute-start | bytes 589832 | tf_op jit(solution)/shard_map/ppermute | solution.py:515
  51.4 11.2 %collective-permute-start.12 = (f32[1536,128]{1,0:T(8,128)S(1)}, f32[1536,128]{1,0:T(8,128)S(1)}, u32[]{:S(2)}, u32[]{:S(2)}) collective-permute-start(f32[1536,128]{1,0:T(8,128)S(1)} %get-tuple-element.49), channel_id=1, source_target_pairs={{0,1},{1,0},{2,3},{3,2},{4,5},{5,4},{6,7},{7,6},{8,9},{9,8},{10,11... | collective-permute-start | bytes 2359304 | tf_op jit(solution)/shard_map/ppermute | solution.py:532
  51.5 13.3 %collective-permute-start.13 = (f32[1536,128]{1,0:T(8,128)S(1)}, f32[1536,128]{1,0:T(8,128)S(1)}, u32[]{:S(2)}, u32[]{:S(2)}) collective-permute-start(f32[1536,128]{1,0:T(8,128)S(1)} %get-tuple-element.50), channel_id=1, source_target_pairs={{1,4},{4,1},{3,6},{6,3},{5,8},{8,5},{7,10},{10,7},{9,12},{12,9},{1... | collective-permute-start | bytes 2359304 | tf_op jit(solution)/shard_map/ppermute | solution.py:531
  59.3 12.1 %collective-permute-start.7 = (f32[1536,128]{1,0:T(8,128)S(1)}, f32[1536,128]{1,0:T(8,128)S(1)}, u32[]{:S(2)}, u32[]{:S(2)}) collective-permute-start(f32[1536,128]{1,0:T(8,128)S(1)} %get-tuple-element.40), channel_id=1, source_target_pairs={{0,1},{1,0},{2,3},{3,2},{4,5},{5,4},{6,7},{7,6},{8,9},{9,8},{10,11... | collective-permute-start | bytes 2359304 | tf_op jit(solution)/shard_map/ppermute | solution.py:532
  60.7 13.3 %collective-permute-start.8 = (f32[1536,128]{1,0:T(8,128)S(1)}, f32[1536,128]{1,0:T(8,128)S(1)}, u32[]{:S(2)}, u32[]{:S(2)}) collective-permute-start(f32[1536,128]{1,0:T(8,128)S(1)} %get-tuple-element.41), channel_id=1, source_target_pairs={{1,4},{4,1},{3,6},{6,3},{5,8},{8,5},{7,10},{10,7},{9,12},{12,9},{1... | collective-permute-start | bytes 2359304 | tf_op jit(solution)/shard_map/ppermute | solution.py:531
  64.9 22.3 %copy-start = (f32[1536,384]{1,0:T(8,128)S(1)}, f32[1536,384]{1,0:T(8,128)}, u32[]{:S(2)}) copy-start(f32[1536,384]{1,0:T(8,128)} %noise.3) | copy-start | bytes 7077892
  67.7 12.5 %collective-permute-start.14 = (f32[384,384]{1,0:T(8,128)S(1)}, f32[384,384]{1,0:T(8,128)S(1)}, u32[]{:S(2)}, u32[]{:S(2)}) collective-permute-start(f32[384,384]{1,0:T(8,128)S(1)} %get-tuple-element.51), channel_id=1, source_target_pairs={{0,0},{1,2},{2,1},{3,3},{4,4},{5,6},{6,5},{7,7},{8,8},{9,10},{10,9... | collective-permute-start | bytes 1769480 | tf_op jit(solution)/shard_map/ppermute | solution.py:515
  68.4 18.7 %collective-permute-start.15 = (f32[384,384]{1,0:T(8,128)S(1)}, f32[384,384]{1,0:T(8,128)S(1)}, u32[]{:S(2)}, u32[]{:S(2)}) collective-permute-start(f32[384,384]{1,0:T(8,128)S(1)} %get-tuple-element.52), channel_id=1, source_target_pairs={{0,1},{1,3},{2,0},{3,2},{4,5},{5,7},{6,4},{7,6},{8,9},{9,11},{10,8... | collective-permute-start | bytes 1769480 | tf_op jit(solution)/shard_map/ppermute | solution.py:515
  76.9 11.9 %collective-permute-start.9 = (f32[384,384]{1,0:T(8,128)S(1)}, f32[384,384]{1,0:T(8,128)S(1)}, u32[]{:S(2)}, u32[]{:S(2)}) collective-permute-start(f32[384,384]{1,0:T(8,128)S(1)} %get-tuple-element.42), channel_id=1, source_target_pairs={{0,0},{1,2},{2,1},{3,3},{4,4},{5,6},{6,5},{7,7},{8,8},{9,10},{10,9... | collective-permute-start | bytes 1769480 | tf_op jit(solution)/shard_map/ppermute | solution.py:515
  77.6 22.2 %collective-permute-start.10 = (f32[384,384]{1,0:T(8,128)S(1)}, f32[384,384]{1,0:T(8,128)S(1)}, u32[]{:S(2)}, u32[]{:S(2)}) collective-permute-start(f32[384,384]{1,0:T(8,128)S(1)} %get-tuple-element.43), channel_id=1, source_target_pairs={{0,1},{1,3},{2,0},{3,2},{4,5},{5,7},{6,4},{7,6},{8,9},{9,11},{10,8... | collective-permute-start | bytes 1769480 | tf_op jit(solution)/shard_map/ppermute | solution.py:515
